TPU v7x, 32 devices: a whole 2x2x4 slice. The times are simulated.
32 devices in a mesh: users: 16 (over z, y, x), cand: 2 (over core).
Axes of the slice: x: 2, y: 2, z: 4, core: 2. Of those that a mesh axis runs over, the one named last changes fastest.
Arguments:
- candidate_rows: bfloat16 [2048, 1024], P(('users', 'cand')), may hold values from -6 to 6
- weight_in: bfloat16 [2, 1024, 8, 512], P(None, None, 'cand'), may hold values from -0.1875 to 0.1875
- weight_out: bfloat16 [2, 8, 128, 1024], P(None, 'cand'), may hold values from -0.1875 to 0.1875
- history_cache: bfloat16 [2, 2, 2048, 8, 128], P(None, None, 'users', 'cand'), may hold values from -6 to 6
- block_user: int32 [16], replicated, may hold values from 0 to 3, as said below
- block_offset: int32 [16], replicated, may hold values from 0 to 7, as said below
- history_length: int32 [4], replicated, may hold values from 1 to 1024, as said below
- candidate_count: int32 [4], replicated, may hold values from 1 to 1024, as said below
Outputs:
- scored_rows: bfloat16 [2048, 1024], P(('users', 'cand'))
Inputs may be any that keep to these rules, and one draw needn't show every extreme that they name: `block_user`: every one of the 4 users owns at least one block; the blocks of one user may stand anywhere; exactly one user owns 16 / 2 blocks, every other user fewer. `block_offset`: the blocks of a user that owns b blocks carry the offsets 0 to b - 1, each once. `history_length`: a user that owns b blocks has more than (b - 1) * 128 and at most b * 128 history rows. `candidate_count`: the counts sum to 2048; the rows of one user are consecutive, users in increasing order.
All inputs are finite; a program needn't handle non-finite values.
Results may differ from a plain program's by a relative error of at most 0.027.
Values may be sent and summed in bfloat16 or wider, within the bound.
No kernel may reach another device: no remote copies, remote signals or barrier semaphores. Data moves between devices by JAX's collectives and lax.ppermute only.
A program may use at most 64 MiB of HBM per device.

v0:
```python
import math

import jax
import jax.numpy as jnp
from jax import lax
from jax.sharding import PartitionSpec as P

BLOCK = 128


def body(
    candidate_rows,
    weight_in,
    weight_out,
    history_cache,
    block_user,
    block_offset,
    history_length,
    candidate_count,
):
    own_rows, model_width = candidate_rows.shape
    layers, model_again, heads_here, packed = weight_in.shape
    head_dim = packed // 4
    cand_devices = lax.axis_size("cand")
    row_count = own_rows * cand_devices
    score_scale = 1.0 / math.sqrt(head_dim)
    user_count = history_length.shape[0]
    users_all = jnp.arange(user_count, dtype=jnp.int32)
    user_ends = jnp.cumsum(candidate_count)
    group_rows = lax.axis_index("users") * row_count + jnp.arange(row_count, dtype=jnp.int32)
    cand_user = jnp.sum((group_rows[:, None] >= user_ends[None, :]).astype(jnp.int32), axis=1)
    step_rows = 4 * BLOCK

    def block_term(accumulated, key_value, piece_start, queries):
        span_rows = key_value.shape[1]
        span_blocks = span_rows // BLOCK
        first_block = piece_start // BLOCK
        owners = lax.dynamic_slice_in_dim(block_user, first_block, span_blocks)
        places = lax.dynamic_slice_in_dim(block_offset, first_block, span_blocks)
        row_user = jnp.broadcast_to(owners[:, None], (span_blocks, BLOCK)).reshape(span_rows)
        row_place = (places[:, None] * BLOCK + jnp.arange(BLOCK, dtype=jnp.int32)[None, :]).reshape(
            span_rows
        )
        row_length = jnp.sum(
            jnp.where(row_user[:, None] == users_all[None, :], history_length[None, :], 0), axis=1
        )
        visible = (cand_user[:, None] == row_user[None, :]) & (row_place < row_length)[None, :]
        scores = (
            jnp.einsum("rhd,nhd->hrn", queries, key_value[0], preferred_element_type=jnp.float32)
            * score_scale
        )
        weights = jnp.where(visible[None], jax.nn.silu(scores), 0.0).astype(jnp.bfloat16)
        return accumulated + jnp.einsum(
            "hrn,nhd->rhd", weights, key_value[1], preferred_element_type=jnp.float32
        )

    current_own = candidate_rows
    for layer_index in range(layers):
        project_segment = lax.all_gather(current_own, "cand", axis=0, tiled=True)
        flat = weight_in[layer_index].reshape(model_width, heads_here * packed)
        mixed = jnp.dot(project_segment, flat, preferred_element_type=jnp.float32)
        projected = (
            jax.nn.silu(mixed)
            .astype(jnp.bfloat16)
            .reshape(project_segment.shape[0], heads_here, 4, head_dim)
        )
        gate_part = projected[:, :, 0]
        values_part = projected[:, :, 1]
        queries = projected[:, :, 2]
        keys_part = projected[:, :, 3]
        own_score = (
            jnp.sum(queries.astype(jnp.float32) * keys_part.astype(jnp.float32), axis=-1)
            * score_scale
        )
        own_weight = jax.nn.silu(own_score).astype(jnp.bfloat16)
        own_term = own_weight.astype(jnp.float32)[..., None] * values_part.astype(jnp.float32)
        empty_sum = jnp.zeros((row_count, heads_here, head_dim), jnp.float32)
        segment = lax.all_gather(history_cache[layer_index], "users", axis=1, tiled=True)
        fold_span_rows = segment.shape[1]
        turns = fold_span_rows // step_rows

        def advance(position, running):
            sliced = lax.dynamic_slice_in_dim(segment, position * step_rows, step_rows, 1)
            return block_term(running, sliced, position * step_rows, queries)

        attended = lax.fori_loop(0, turns, advance, empty_sum)
        attended = attended + own_term
        centred = attended - jnp.mean(attended, axis=-1, keepdims=True)
        variance = jnp.mean(centred * centred, axis=-1, keepdims=True)
        gated = (centred * lax.rsqrt(variance + 1e-05) * gate_part.astype(jnp.float32)).astype(
            jnp.bfloat16
        )
        partial_out = jnp.dot(
            gated.reshape(row_count, heads_here * head_dim),
            weight_out[layer_index].reshape(heads_here * head_dim, model_width),
            preferred_element_type=jnp.float32,
        )
        shared = lax.psum_scatter(
            partial_out.astype(jnp.bfloat16), "cand", scatter_dimension=0, tiled=True
        ).astype(jnp.float32)
        current_own = (current_own.astype(jnp.float32) + shared).astype(jnp.bfloat16)
    return current_own


def solution(mesh):
    placed = (
        P(("users", "cand"), None),
        P(None, None, "cand", None),
        P(None, "cand", None, None),
        P(None, None, "users", "cand", None),
        P(),
        P(),
        P(),
        P(),
    )
    return jax.shard_map(
        body, mesh=mesh, in_specs=placed, out_specs=P(("users", "cand"), None), check_vma=False
    )
```

profile of v0, /device:TPU:0, one launch (start us, length us, event | category | flops | bytes accessed | tf_op | source)
XLA Modules:
  0.0 214.8 jit_solution(1076151484264249114)
XLA Ops:
  6.5 1.2 fusion.41
  8.6 7.0 %fusion.38 = (bf16[1,1024,4,512]{3,2,1,0:T(4,128)(2,1)}, bf16[1,1024,4,512]{3,2,1,0:T(4,128)(2,1)S(1)}) fusion(bf16[2,1024,4,512]{3,2,1,0:T(4,128)(2,1)} %param.13), kind=kLoop, calls=%fused_computation.82 | loop fusion | bytes 16777216 | tf_op jit(solution)/shard_map/slice | solution.py:60
  15.6 1.4 copy.51
  17.0 2.1 all_gather.13
  21.8 1.8 fusion.39
  23.7 65.7 %all-gather.5.cloned.1.call-done = bf16[1,2,2048,4,128]{4,2,3,1,0:T(8,128)(2,1)} async-done(((bf16[1,2,128,4,128]{4,2,3,1,0:T(8,128)(2,1)}), bf16[1,2,2048,4,128]{4,2,3,1,0:T(8,128)(2,1)}) %all-gather.5.cloned.1.call-update) | async-done | bytes 4194320 | tf_op jit(solution)/shard_map/all_gather | solution.py:78
  89.3 10.5 %while.32 = (s32[]{:T(128)}, f32[128,4,128]{0,2,1:T(8,128)S(1)}, bf16[2,2048,4,128]{3,1,2,0:T(8,128)(2,1)}, s32[128]{0:T(128)S(1)}, s32[16]{0:T(128)S(1)}, /*ind...) while((s32[]{:T(128)}, f32[128,4,128]{0,2,1:T(8,128)S(1)}, ...), condition=%wide.region_4.5_spmd.clone, body=%wide.region_2.4_spmd.clone.sunk | while | flops 136321568 | bytes 1849351 | solution.py:86
  89.9 2.0 fusion.58
  92.6 2.0 fusion.58
  95.2 2.0 fusion.58
  97.9 2.0 fusion.58
  100.1 1.0 convolution_convert_fusion.1
  102.0 5.6 %copy.52 = bf16[128,8,4,512]{3,1,2,0:T(8,128)(2,1)} copy(bf16[128,8,4,512]{3,2,1,0:T(4,128)(2,1)} %bitcast.134) | data formatting | bytes 8388608
  108.5 2.2 %all_gather.15 = bf16[128,1024]{1,0:T(8,128)(2,1)S(1)} all-gather(bf16[64,1024]{1,0:T(8,128)(2,1)S(1)} %add_convert_fusion.1), channel_id=1, replica_groups=mesh['users'=16,'cand'=2] {'cand'}, dimensions={0}, use_global_device_ids=true | all-gather | bytes 393216 | tf_op jit(solution)/shard_map/all_gather | solution.py:59
  110.7 3.0 %multiply_convert_fusion = bf16[128,2048]{1,0:T(8,128)(2,1)S(1)} fusion(bf16[128,1024]{1,0:T(8,128)(2,1)S(1)} %all_gather.15, bf16[1024,2048]{1,0:T(8,128)(2,1)} %bitcast.136), kind=kOutput, calls=%fused_computation.46 | convolution fusion | flops 538181632 | bytes 4980736 | tf_op jit(solution)/shard_map/dot_general | solution.py:61
  114.9 73.3 %all-gather.7.cloned.1.call-done = bf16[1,2,2048,4,128]{4,2,3,1,0:T(8,128)(2,1)} async-done(((bf16[1,2,128,4,128]{4,2,3,1,0:T(8,128)(2,1)}), bf16[1,2,2048,4,128]{4,2,3,1,0:T(8,128)(2,1)}) %all-gather.7.cloned.1.call-update) | async-done | bytes 4194320 | tf_op jit(solution)/shard_map/all_gather | solution.py:78
  188.3 10.5 %while.33 = (s32[]{:T(128)}, f32[128,4,128]{0,2,1:T(8,128)S(1)}, bf16[2,2048,4,128]{3,1,2,0:T(8,128)(2,1)}, s32[128]{0:T(128)S(1)}, s32[16]{0:T(128)S(1)}, /*ind...) while((s32[]{:T(128)}, f32[128,4,128]{0,2,1:T(8,128)S(1)}, ...), condition=%wide.region_11.12_spmd.clone, body=%wide.region_9.11_spmd.clone.sunk | while | flops 136321568 | bytes 1849351 | solution.py:86
  188.9 2.0 fusion.60
  191.5 2.0 fusion.60
  194.1 2.0 fusion.60
  196.8 2.0 fusion.60
  199.3 1.0 convolution_convert_fusion
  200.4 6.3 %reduce-scatter.5.cloned.1.call-done = bf16[64,1024]{1,0:T(8,128)(2,1)} async-done(((bf16[128,1024]{1,0:T(8,128)(2,1)}), bf16[64,1024]{1,0:T(8,128)(2,1)}) %reduce-scatter.5.cloned.1.call-update) | async-done | bytes 131088 | tf_op jit(solution)/shard_map/reduce_scatter | solution.py:98
  206.7 1.6 add_convert_fusion
  (98 shorter events, 12.0 us)
Async XLA Ops:
  6.5 82.8 %all-gather.5.cloned.1.call-start = ((), (), s32[]{:S(2)}) async-start(), calls=%async_computation.4 | async-start | bytes 4456448 | tf_op jit(solution)/shard_map/all_gather | solution.py:78
  8.5 99.1 %reduce-scatter.3.cloned.1.call-start = ((), (), s32[]{:S(2)}) async-start(), calls=%async_computation.2 | async-start | bytes 393216 | tf_op jit(solution)/shard_map/reduce_scatter | solution.py:98
  15.6 1.4 copy-start
  19.1 1.2 copy-start.2
  19.9 69.4 %copy-start.1 = (s32[4]{0:T(128)S(1)}, s32[4]{0:T(128)}, u32[]{:S(2)}) copy-start(s32[4]{0:T(128)} %param.18) | copy-start | bytes 52
  19.9 69.4 %copy-start.3 = (s32[16]{0:T(128)S(1)}, s32[16]{0:T(128)}, u32[]{:S(2)}) copy-start(s32[16]{0:T(128)} %param.16) | copy-start | bytes 196
  19.9 69.4 %copy-start.4 = (s32[16]{0:T(128)S(1)}, s32[16]{0:T(128)}, u32[]{:S(2)}) copy-start(s32[16]{0:T(128)} %param.17) | copy-start | bytes 196
  101.1 87.1 %all-gather.7.cloned.1.call-start = ((), (), s32[]{:S(2)}) async-start(), calls=%async_computation.5 | async-start | bytes 4456448 | tf_op jit(solution)/shard_map/all_gather | solution.py:78
  102.0 104.7 %reduce-scatter.5.cloned.1.call-start = ((), (), s32[]{:S(2)}) async-start(), calls=%async_computation.3 | async-start | bytes 393216 | tf_op jit(solution)/shard_map/reduce_scatter | solution.py:98
Sparse Core Ops, SparseCore 0:
  10.1 79.1 all-gather.4
  101.3 6.1 reduce-scatter.2
  110.6 77.5 all-gather.6
  200.5 6.1 reduce-scatter.4
where the time goes:
time: 215 us
  waiting for transfers between devices  145 us (67%)
  local copies, waits for them, and re-layouts  22.6 us (11%)
  matrix products  21.7 us (10%)
  between operations  13.3 us (6%)
  other arithmetic  7.07 us (3%)
  blocking collectives  4.26 us (2%)
    all_gather x2, waiting for transfers between devices, body(): lax.all_gather(history_cache[layer_index], 'users', axis=1, tiled=True)  139 us
    dot_general x8, matrix products, block_term(): jnp.einsum('hrn,nhd->rhd', weights, key_value[1], preferred_element_type=...  15.8 us
    unnamed x18, local copies, waits for them, and re-layouts  9.09 us
    slice x1, local copies, waits for them, and re-layouts, body(): flat = weight_in[layer_index].reshape(model_width, heads_here * packed)  7.01 us
    reduce_scatter x2, waiting for transfers between devices, body(): lax.psum_scatter(partial_out.astype(jnp.bfloat16), 'cand', scatter_dimens...  6.31 us
  transfers between devices with their start and end apart: 4, of which 3 were waited for; matrix products, arithmetic and copies ran while one was open for 11% of the time, Pallas kernels for 0%

commit v1 on v0

v1 whole, which is shorter than its diff:
```python
import functools
import math

import jax
import jax.numpy as jnp
from jax import lax
from jax.experimental import pallas as pl
from jax.experimental.pallas import tpu as pltpu
from jax.sharding import PartitionSpec as P

BLOCK = 128
LANES = 128
FAR = -1e30
MIB = 1024 * 1024

VMEM_SPEC = pl.BlockSpec(memory_space=pltpu.VMEM)
SMEM_SPEC = pl.BlockSpec(memory_space=pltpu.SMEM)


def half_silu(half):
    return half + half * jnp.tanh(half)


def position(spot_bits):
    chip = lax.axis_index("users")
    spot = sum((((chip >> b) & 1) << i for i, b in enumerate(spot_bits)), chip * 0)
    return chip, spot, lax.axis_index("cand")


def order_history_kernel(spot_bits, h_ref, *refs):
    o_refs, pieces = refs[:-1], refs[-1]
    _, spot, _ = position(spot_bits)
    for layer_index in range(h_ref.shape[0]):
        for kind in range(h_ref.shape[1]):
            for head in range(h_ref.shape[3]):
                pieces[spot ^ head, layer_index, kind] = h_ref[layer_index, kind, :, head, :]
    for step, o_ref in enumerate(o_refs):
        o_ref[...] = pieces[step]


def join_layers_kernel(count, *refs):
    every_ref, *layer_refs = refs[count:]
    for layer_index, o_ref in enumerate(layer_refs):
        for at, ref in enumerate(refs[:count]):
            every_ref[layer_index, at] = ref[layer_index]
            o_ref[at] = ref[layer_index]


def halves_kernel(i_ref, low_ref, high_ref):
    size = low_ref.shape[0]
    low_ref[...] = i_ref[:size]
    high_ref[...] = i_ref[size:]


def join_kernel(*refs):
    o_ref = refs[-1]
    for at, ref in enumerate(refs[:-1]):
        o_ref[at] = ref[...]


def pick_head_kernel(layer_index, spot_bits, w_ref, o_ref, held, sems):
    _, spot, _ = position(spot_bits)
    chunks, rows = held.shape[:2]
    copies = [
        pltpu.make_async_copy(
            w_ref.at[layer_index, pl.ds(at * rows, rows)], held.at[at], sems.at[at]
        )
        for at in range(chunks)
    ]
    for copy in copies:
        copy.start()
    for at, copy in enumerate(copies):
        copy.wait()
        for head in range(held.shape[2]):

            @pl.when(spot == head)
            def _(at=at, head=head):
                o_ref[at * rows : (at + 1) * rows] = held[at, :, head, :]


def project(x_ref, w_ref, q_ref, gate_ref, own_ref, score_scale):
    dim = q_ref.shape[1]

    def part(first):
        w = w_ref[:, first * dim : (first + 2) * dim]
        mixed = jnp.dot(x_ref[...], w, preferred_element_type=jnp.float32)
        return half_silu(mixed * 0.5).astype(jnp.bfloat16)

    tail = part(2)
    query = tail[:, :dim]
    q_ref[...] = query
    score = jnp.sum(
        query.astype(jnp.float32) * tail[:, dim:].astype(jnp.float32), axis=-1, keepdims=True
    )
    weight = half_silu(score * (0.5 * score_scale)).astype(jnp.bfloat16).astype(jnp.float32)
    front = part(0)
    gate_ref[...] = front[:, :dim]
    own_ref[...] = weight * front[:, dim:].astype(jnp.float32)


def begin_kernel(spots, cores, spot_bits, score_scale, *refs):
    _, spot, core_here = position(spot_bits)
    x_refs, (w_ref, x_out, q_ref, gate_ref, own_ref) = refs[:-5], refs[-5:]
    own_rows = x_out.shape[0] // (spots * cores)
    for shift in range(cores):
        core = lax.rem(core_here + (cores - shift), cores)
        for step in range(spots):
            if shift == 0:
                piece = x_refs[step][...]
            else:
                piece = x_refs[spots + shift - 1][step]
            at = ((spot ^ step) * cores + core) * own_rows
            x_out[pl.ds(pl.multiple_of(at, own_rows), own_rows)] = piece
    project(x_out, w_ref, q_ref, gate_ref, own_ref, score_scale)


def gather_heads(gated_refs, spot, wide):
    dim = gated_refs[0].shape[1]
    for step, ref in enumerate(gated_refs):
        at = pl.multiple_of((spot ^ step) * dim, dim)
        wide[:, pl.ds(at, dim)] = ref[...]


def term_kernel(spots, spot_bits, layer_index, *refs):
    _, spot, _ = position(spot_bits)
    gated_refs, (weight_ref, o_ref, wide) = refs[:spots], refs[spots:]
    gather_heads(gated_refs, spot, wide)
    depth, width = wide.shape[1], o_ref.shape[1]
    tile = min(width, 256)
    for first in range(0, width, tile):
        columns = slice(first, first + tile)
        weight = weight_ref[layer_index, :, :, columns].reshape(depth, tile)
        o_ref[:, columns] = jnp.dot(
            wide[...], weight, preferred_element_type=jnp.float32
        ).astype(jnp.bfloat16)


def step_kernel(spots, cores, spot_bits, score_scale, *refs):
    _, spot, core = position(spot_bits)
    term_refs, (x_ref, w_ref, x_own, q_ref, gate_ref, own_ref, x_next) = refs[:cores], refs[cores:]
    total = x_ref[...].astype(jnp.float32)
    for ref in term_refs:
        total = total + ref[...].astype(jnp.float32)
    x_next[...] = total.astype(jnp.bfloat16)
    own_rows = x_own.shape[0]
    at = (spot * cores + core) * own_rows
    x_own[...] = x_next[pl.ds(pl.multiple_of(at, own_rows), own_rows)]
    project(x_next, w_ref, q_ref, gate_ref, own_ref, score_scale)


def last_term_kernel(spots, cores, spot_bits, layer_index, *refs):
    _, spot, core = position(spot_bits)
    gated_refs, (weight_ref, *o_refs, wide, total) = refs[:spots], refs[spots:]
    gather_heads(gated_refs, spot, wide)
    own_rows, width = o_refs[0].shape
    weight = weight_ref[layer_index].reshape(wide.shape[1], width)
    total[...] = jnp.dot(wide[...], weight, preferred_element_type=jnp.float32)
    for shift, o_ref in enumerate(o_refs):
        at = lax.rem(core + shift, cores) * own_rows
        o_ref[...] = total[pl.ds(pl.multiple_of(at, own_rows), own_rows)].astype(jnp.bfloat16)


def add_kernel(*refs):
    total = refs[0][...].astype(jnp.float32)
    for ref in refs[1:-1]:
        total = total + ref[...].astype(jnp.float32)
    refs[-1][...] = total.astype(jnp.bfloat16)


def visit_history(spot_bits, masks, held, layer_index, scalar_refs, history_refs, q_wide, total):
    user_ref, offset_ref, length_ref = scalar_refs
    spot_masks, member_masks, spot_of_chip, row_count = masks
    spots = len(spot_masks)
    dim = total.shape[1]
    scale = 0.5 / math.sqrt(dim)
    chip, _, _ = position(spot_bits)
    spot_part = chip & spot_of_chip
    member_part = chip - spot_part
    history_refs = [ref if len(ref.shape) == 4 else ref.at[layer_index] for ref in history_refs]

    def visit(ref, first, count, member, at):
        keys, values = [], []
        for piece in range(count):
            for block in range(ref.shape[2] // BLOCK):
                source = (member | (spot_part ^ spot_masks[at + piece])) * (ref.shape[2] // BLOCK) + block
                owner = user_ref[source]
                limit = length_ref[owner] - offset_ref[source] * BLOCK
                lanes = lax.broadcasted_iota(jnp.int32, (BLOCK, LANES), 1)
                sublanes = lax.broadcasted_iota(jnp.int32, (BLOCK, LANES), 0)
                seen = (lanes == owner) & (sublanes < limit)
                side = jnp.where(seen, 0.0, FAR).astype(jnp.bfloat16)
                at_rows = pl.ds(block * BLOCK, BLOCK)
                keys.append(jnp.concatenate([ref[first + piece, 0, at_rows], side], axis=1))
                values.append(ref[first + piece, 1, at_rows])
        half = lax.dot_general(
            q_wide[...],
            jnp.concatenate(keys, axis=0),
            (((1,), (1,)), ((), ())),
            preferred_element_type=jnp.float32,
        )
        weights = half_silu(half * scale).astype(jnp.bfloat16)
        total[...] += jnp.dot(
            weights, jnp.concatenate(values, axis=0), preferred_element_type=jnp.float32
        )

    if len(history_refs) == len(held):
        for ref, (mask, at) in zip(history_refs, held):
            visit(ref, 0, ref.shape[0], member_part ^ mask, at)
    else:

        @pl.loop(0, len(member_masks))
        def _(turn):
            member = turn * 0
            for i in range((len(member_masks) - 1).bit_length()):
                member = member | (((turn >> i) & 1) * member_masks[1 << i])
            visit(history_refs[0], turn * spots, spots, member, 0)


def attend_kernel(spot_bits, masks, held, layer_index, *refs):
    user_ref, offset_ref, length_ref, count_ref, q_ref, own_ref = refs[:6]
    history_refs, (q_wide, total) = refs[6:-2], refs[-2:]
    spot_masks, member_masks, spot_of_chip, row_count = masks
    spots = len(spot_masks)
    rows = q_ref.shape[0] // spots
    dim = q_ref.shape[1]
    user_count = length_ref.shape[0]
    chip, _, _ = position(spot_bits)
    member_part = chip - (chip & spot_of_chip)
    lane = lax.broadcasted_iota(jnp.int32, (1, LANES), 1)
    starts = jnp.zeros((1, LANES), jnp.int32)
    ends = jnp.zeros((1, LANES), jnp.int32)
    running = jnp.int32(0)
    for user in range(user_count):
        starts = jnp.where(lane == user, running, starts)
        running = running + count_ref[user]
        ends = jnp.where(lane == user, running, ends)
    q_wide[:, :dim] = q_ref[...]
    for at in range(spots):
        first = (member_part | spot_masks[at]) * row_count
        index = first + lax.broadcasted_iota(jnp.int32, (rows, LANES), 0)
        mine = (index >= starts) & (index < ends)
        q_wide[at * rows : (at + 1) * rows, dim:] = jnp.where(mine, 1.0, 0.0).astype(
            jnp.bfloat16
        )
    total[...] = own_ref[...]
    visit_history(
        spot_bits,
        masks,
        held,
        layer_index,
        (user_ref, offset_ref, length_ref),
        history_refs,
        q_wide,
        total,
    )


def finish_kernel(spot_bits, masks, held, layer_index, last, *refs):
    scalar_refs, (q_wide, before_ref, gate_ref), refs = refs[:3], refs[3:6], refs[6:]
    spots = len(masks[0])
    outs = spots if last else 1
    history_refs, o_refs, total = refs[: -outs - 1], refs[-outs - 1 : -1], refs[-1]
    rows = before_ref.shape[0] // spots
    _, spot, _ = position(spot_bits)
    total[...] = before_ref[...]
    if history_refs:
        visit_history(
            spot_bits, masks, held, layer_index, scalar_refs, history_refs, q_wide, total
        )
    full = total[...]
    centred = full - jnp.mean(full, axis=-1, keepdims=True)
    variance = jnp.mean(centred * centred, axis=-1, keepdims=True)
    gated = centred * lax.rsqrt(variance + 1e-05) * gate_ref[...].astype(jnp.float32)
    if not last:
        o_refs[0][...] = gated.astype(jnp.bfloat16)
        return
    total[...] = gated
    for step in range(spots):
        at_rows = pl.ds(pl.multiple_of((spot ^ step) * rows, rows), rows)
        o_refs[step][...] = total[at_rows].astype(jnp.bfloat16)


def body(
    candidate_rows,
    weight_in,
    weight_out,
    history_cache,
    block_user,
    block_offset,
    history_length,
    candidate_count,
):
    own_rows, model_width = candidate_rows.shape
    layers, model_again, heads_here, packed = weight_in.shape
    head_dim = packed // 4
    local_rows = history_cache.shape[2]
    cores = lax.axis_size("cand")
    chips = lax.axis_size("users")
    spots = heads_here
    groups = chips // spots
    row_count = own_rows * cores
    all_rows = row_count * spots
    score_scale = 1.0 / math.sqrt(head_dim)

    bits = list(range(chips.bit_length() - 1))
    spot_bits = sorted((bits[::2] + bits[1::2])[: spots.bit_length() - 1])
    member_bits = [b for b in bits if b not in spot_bits]

    def mask_of(number, places):
        return sum(((number >> i) & 1) << b for i, b in enumerate(places))

    def swap(value, mask):
        return lax.ppermute(value, "users", [(u, u ^ mask) for u in range(chips)])

    def trade_spots(values):
        return [values[0]] + [swap(values[m], mask_of(m, spot_bits)) for m in range(1, spots)]

    def gather_spots(value):
        found = [value]
        for bit in reversed(range(len(spot_bits))):
            mask = 1 << spot_bits[bit]
            found = [(v, swap(v, mask)) for v in found]
            found = [v for v, _ in found] + [w for _, w in found]
        order = [0]
        for bit in reversed(range(len(spot_bits))):
            order = order + [o | (1 << bit) for o in order]
        return [found[order.index(m)] for m in range(spots)]

    def shift_core(value, step):
        pairs = [(c, (c + step) % cores) for c in range(cores)]
        return lax.ppermute(value, "cand", pairs)

    spot_masks = [mask_of(m, spot_bits) for m in range(spots)]
    member_masks = [mask_of(m, member_bits) for m in range(groups)]

    masks = (spot_masks, member_masks, spot_masks[-1], row_count)

    def gather_members(pieces):
        if groups <= 2:
            return [pieces] + [swap(pieces, mask) for mask in member_masks[1:]]
        chips_of = [[mask_of(s, spot_bits) | m for m in member_masks] for s in range(spots)]
        return [
            lax.all_gather(pieces, "users", axis=0, axis_index_groups=chips_of, tiled=True)
        ]

    def after(value, *others):
        return lax.optimization_barrier((value,) + others)[0]

    def kernel_call(kernel, outs, name, operands, scratch=(), limit=8, specs=None):
        results = pl.pallas_call(
            kernel,
            out_shape=[jax.ShapeDtypeStruct(*out) for out in outs],
            in_specs=specs or [VMEM_SPEC] * len(operands),
            out_specs=[VMEM_SPEC] * len(outs),
            scratch_shapes=scratch,
            compiler_params=pltpu.CompilerParams(vmem_limit_bytes=limit * MIB),
            name=name,
        )(*operands)
        return list(results)

    def pick_head(layer_index):
        rows = min(model_width, 128)
        chunks = model_width // rows
        return kernel_call(
            functools.partial(pick_head_kernel, layer_index, spot_bits),
            [((model_width, packed), weight_in.dtype)],
            "pick_head",
            [weight_in],
            [
                pltpu.VMEM((chunks, rows, heads_here, packed), weight_in.dtype),
                pltpu.SemaphoreType.DMA((chunks,)),
            ],
            51,
            [pl.BlockSpec(memory_space=pl.ANY)],
        )[0]

    def order_history():
        shape = (layers, 2, local_rows, head_dim)
        return kernel_call(
            functools.partial(order_history_kernel, spot_bits),
            [(shape, jnp.bfloat16)] * spots,
            "order_history",
            [history_cache],
            [pltpu.VMEM((spots,) + shape, jnp.bfloat16)],
            4,
        )

    def join_layers(pieces):
        shape = (spots, 2, local_rows, head_dim)
        every, first, *later = kernel_call(
            functools.partial(join_layers_kernel, spots),
            [((layers,) + shape, jnp.bfloat16)] + [(shape, jnp.bfloat16)] * layers,
            "join_layers",
            list(pieces),
        )
        return every, first, later

    def halves(pieces):
        shape = (pieces.shape[0] // 2,) + pieces.shape[1:]
        return kernel_call(halves_kernel, [(shape, pieces.dtype)] * 2, "halves", [pieces])

    def join(pieces):
        if len(pieces) == 1:
            return pieces[0][None]
        shape = (len(pieces),) + pieces[0].shape
        return kernel_call(join_kernel, [(shape, pieces[0].dtype)], "join", list(pieces))[0]

    def together(*values):
        return lax.optimization_barrier(values)

    pieces, first_weight = together(trade_spots(order_history()), pick_head(0))
    every, first, later = join_layers(pieces)
    x_pieces = trade_spots([after(candidate_rows, first)] * spots)
    crossed = groups == 4
    if crossed:
        near_mask, far_mask = member_masks[1:3]
        far, near, x_pieces = together(
            swap(first, far_mask), swap(every, near_mask), x_pieces
        )
        history = [[every, near, far, swap(far, near_mask)]]
    else:
        history = [gather_members(first)]
    x_group = x_pieces + [shift_core(join(x_pieces), s) for s in range(1, cores)]

    scalars = [block_user, block_offset, history_length, candidate_count]
    one_head = (all_rows, head_dim)
    head_outs = [(one_head, jnp.bfloat16), (one_head, jnp.bfloat16), (one_head, jnp.float32)]
    x, *projected = kernel_call(
        functools.partial(begin_kernel, spots, cores, spot_bits, score_scale),
        [((all_rows, model_width), jnp.bfloat16)] + head_outs,
        "begin",
        x_group + [first_weight],
    )

    for layer_index in range(layers):
        last = layer_index + 1 == layers
        outs = [((row_count, head_dim), jnp.bfloat16)] * spots if last else head_outs[:1]
        query, gate, own = projected
        held, split = (), 1
        if crossed:
            parts = 2 if layer_index else 1
            cuts = [spots // parts * part for part in range(parts)]
            held = ((0, 0), (near_mask, 0))
            held += tuple((m, at) for m in (far_mask, near_mask | far_mask) for at in cuts)
            split = 2 + parts + parts // 2
        ready, coming = history[layer_index][:split], history[layer_index][split:]
        operands = scalars + [query, own] + ready
        wide_query, total = kernel_call(
            functools.partial(attend_kernel, spot_bits, masks, held[:split], layer_index),
            [((all_rows, head_dim + LANES), jnp.bfloat16), (one_head, jnp.float32)],
            "attend",
            operands,
            (),
            16,
            [SMEM_SPEC] * 4 + [VMEM_SPEC] * (len(operands) - 4),
        )
        operands = scalars[:3] + [wide_query, total, gate] + coming
        gated = kernel_call(
            functools.partial(finish_kernel, spot_bits, masks, held[split:], layer_index, last),
            outs,
            "finish",
            operands,
            [pltpu.VMEM(one_head, jnp.float32)],
            16,
            [SMEM_SPEC] * 3 + [VMEM_SPEC] * (len(operands) - 3),
        )
        if not last:
            gated = trade_spots(list(gated) * spots)
            next_weight = pick_head(layer_index + 1)
            if crossed:
                far = swap(after(later[layer_index], far), far_mask)
                far = halves(after(far, gated[1]))
                ahead = swap(far[0], near_mask)
                gated, far, ahead, next_weight = together(gated, far, ahead, next_weight)
                arrays = [every, near] + far + [ahead, swap(far[1], near_mask)]
            else:
                arrays = gather_members(later[layer_index])
            terms = kernel_call(
                functools.partial(term_kernel, spots, spot_bits, layer_index),
                [((all_rows, model_width), jnp.bfloat16)],
                "term",
                gated + [weight_out],
                [pltpu.VMEM((all_rows, spots * head_dim), jnp.bfloat16)],
            )
            terms = terms + [shift_core(terms[0], s) for s in range(1, cores)]
            history.append(arrays)
            x, *projected = kernel_call(
                functools.partial(step_kernel, spots, cores, spot_bits, score_scale),
                [((own_rows, model_width), jnp.bfloat16)] + head_outs,
                "step",
                terms + [x, next_weight],
                [pltpu.VMEM((all_rows, model_width), jnp.bfloat16)],
                12,
            )
        else:
            terms = kernel_call(
                functools.partial(last_term_kernel, spots, cores, spot_bits, layer_index),
                [((own_rows, model_width), jnp.bfloat16)] * cores,
                "last_term",
                trade_spots(gated) + [weight_out],
                [
                    pltpu.VMEM((row_count, spots * head_dim), jnp.bfloat16),
                    pltpu.VMEM((row_count, model_width), jnp.float32),
                ],
            )
            terms = terms[:1] + [shift_core(terms[s], s) for s in range(1, cores)]
            (out,) = kernel_call(
                add_kernel, [((own_rows, model_width), jnp.bfloat16)], "add", [x] + terms
            )
    return out


def solution(mesh):
    placed = (
        P(("users", "cand"), None),
        P(None, None, "cand", None),
        P(None, "cand", None, None),
        P(None, None, "users", "cand", None),
        P(),
        P(),
        P(),
        P(),
    )
    return jax.shard_map(
        body, mesh=mesh, in_specs=placed, out_specs=P(("users", "cand"), None), check_vma=False
    )
```

time: 215 us -> 67.9 us (0.32)
  waiting for transfers between devices: 145 us -> 24.7 us
  starting transfers between devices: 0.13 us -> 23.7 us
  matrix products: 21.7 us -> 0 us
  local copies, waits for them, and re-layouts: 22.6 us -> 1.07 us
  Pallas kernels: 0 us -> 18.1 us
  between operations: 13.3 us -> 0.19 us
  other arithmetic: 7.07 us -> 0 us
  blocking collectives: 4.26 us -> 0 us
    all_gather x2 -> x0, waiting for transfers between devices: 139 us -> none  [body(): lax.all_gather(history_cache[layer_index], 'users', axis=1, tiled=True)]
    ppermute x0 -> x21, waiting for transfers between devices: none -> 24.7 us  [the longest x18 21.2 us: swap(): return lax.ppermute(value, 'users', [(u, u ^ mask) for u in range(chips)])]
    ppermute x0 -> x21, starting transfers between devices: none -> 23.7 us  [the longest x18 23.5 us: swap(): return lax.ppermute(value, 'users', [(u, u ^ mask) for u in range(chips)])]
    dot_general x12 -> x0, matrix products: 21.7 us -> none  [the longest x8 15.8 us: block_term(): jnp.einsum('hrn,nhd->rhd', weights, key_value[1], preferred_element_type=...]
    pallas_call x0 -> x15, Pallas kernels: none -> 18.1 us  [kernel_call(): pl.pallas_call(kernel, out_shape=[jax.ShapeDtypeStruct(*out) for out in o...]
    slice x5 -> x0, local copies, waits for them, and re-layouts: 11.5 us -> none  [the longest x1 7.01 us: body(): flat = weight_in[layer_index].reshape(model_width, heads_here * packed)]
    unnamed x18 -> x14, local copies, waits for them, and re-layouts: 9.09 us -> 1.07 us
    reduce_scatter x2 -> x0, waiting for transfers between devices: 6.31 us -> none  [body(): lax.psum_scatter(partial_out.astype(jnp.bfloat16), 'cand', scatter_dimens...]
  transfers between devices with their start and end apart: 4 -> 21, of which waited for: 3 -> 15; matrix products, arithmetic and copies ran while one was open for 11% -> 0% of each run, Pallas kernels for 0% -> 20%
where the time goes in v1:
time: 67.9 us; the launch traced here: 67.8 us
  waiting for transfers between devices  24.7 us (36%)
  starting transfers between devices  23.7 us (35%)
  Pallas kernels  18.1 us (27%)
  local copies, waits for them, and re-layouts  1.07 us (2%)
    ppermute x18, starting transfers between devices, swap(): return lax.ppermute(value, 'users', [(u, u ^ mask) for u in range(chips)])  23.5 us
    ppermute x18, waiting for transfers between devices, swap(): return lax.ppermute(value, 'users', [(u, u ^ mask) for u in range(chips)])  21.2 us
    pallas_call x15, Pallas kernels, kernel_call(): pl.pallas_call(kernel, out_shape=[jax.ShapeDtypeStruct(*out) for out in o...  18.1 us
    ppermute x3, waiting for transfers between devices, shift_core(): return lax.ppermute(value, 'cand', pairs)  3.47 us
  transfers between devices with their start and end apart: 21, of which 15 were waited for; matrix products, arithmetic and copies ran while one was open for 0% of the time, Pallas kernels for 20%

profile of v1, /device:TPU:0, one launch (start us, length us, event | category | flops | bytes accessed | tf_op | source)
XLA Modules:
  0.0 67.8 jit_solution(14789272487726373252)
XLA Ops:
  1.1 1.3 %order_history.1 = (bf16[2,2,128,128]{3,2,1,0:T(8,128)(2,1)S(1)}, bf16[2,2,128,128]{3,2,1,0:T(8,128)(2,1)S(1)}, bf16[2,2,128,128]{3,2,1,0:T(8,128)(2,1)S(1)}, bf16[2,2,128,128]{3,2,1,0:T(8,128)(2,1)S(1)}) custom-call(bf16[2,2,128,4,128]{4,3,2,1,0:T(4,128)(2,1)S(1)} %copy-done.1), custom_call_target="tpu_custom_call" | custom-call | tf_op jit(solution)/shard_map/order_history/pallas_call | solution.py:350
  2.3 3.0 %collective-permute-start = (bf16[2,2,128,128]{3,2,1,0:T(8,128)(2,1)S(1)}, bf16[2,2,128,128]{3,2,1,0:T(8,128)(2,1)S(1)}, u32[]{:S(2)}, u32[]{:S(2)}) collective-permute-start(bf16[2,2,128,128]{3,2,1,0:T(8,128)(2,1)S(1)} %get-tuple-element.55), channel_id=1, source_target_pairs={{0,2},{2,0},{4,6},{6,4},{8,10},{10,8},{12,14},{14,12},{16,18},{18,... | collective-permute-start | bytes 393224 | tf_op jit(solution)/shard_map/ppermute | solution.py:313
  5.3 1.6 %collective-permute-start.1 = (bf16[2,2,128,128]{3,2,1,0:T(8,128)(2,1)S(1)}, bf16[2,2,128,128]{3,2,1,0:T(8,128)(2,1)S(1)}, u32[]{:S(2)}, u32[]{:S(2)}) collective-permute-start(bf16[2,2,128,128]{3,2,1,0:T(8,128)(2,1)S(1)} %get-tuple-element.56), channel_id=1, source_target_pairs={{0,8},{2,10},{4,12},{6,14},{8,0},{10,2},{12,4},{14,6},{16,24},{18,... | collective-permute-start | bytes 393224 | tf_op jit(solution)/shard_map/ppermute | solution.py:313
  6.9 3.4 %pick_head.2.refs_5_ = bf16[1024,512]{1,0:T(8,128)(2,1)S(1)} custom-call(bf16[2,1024,4,512]{3,2,1,0:T(4,128)(2,1)} %w_ref.3), custom_call_target="tpu_custom_call" | custom-call | tf_op jit(solution)/shard_map/pick_head/pallas_call | solution.py:350
  10.3 1.4 %collective-permute-done.1.refs_2_ = bf16[2,2,128,128]{3,2,1,0:T(8,128)(2,1)S(1)} collective-permute-done((bf16[2,2,128,128]{3,2,1,0:T(8,128)(2,1)S(1)}, bf16[2,2,128,128]{3,2,1,0:T(8,128)(2,1)S(1)}, u32[]{:S(2)}, u32[]{:S(2)}) %collective-permute-start.1) | collective-permute-done | bytes 131104 | tf_op jit(solution)/shard_map/ppermute | solution.py:313
  13.0 1.8 %collective-permute-start.4 = (bf16[2,4,2,128,128]{4,3,2,1,0:T(8,128)(2,1)S(1)}, bf16[2,4,2,128,128]{4,3,2,1,0:T(8,128)(2,1)S(1)}, u32[]{:S(2)}, u32[]{:S(2)}) collective-permute-start(bf16[2,4,2,128,128]{4,3,2,1,0:T(8,128)(2,1)S(1)} %get-tuple-element.63.refs_6_), channel_id=1, source_target_pairs={{0,4},{2,6},{4,0},{6,2},{8,12},{10,14},{12,8},{14,10},{16,20},{18,... | collective-permute-start | bytes 1572872 | tf_op jit(solution)/shard_map/ppermute | solution.py:313
  14.8 2.6 %collective-permute-start.3 = (bf16[4,2,128,128]{3,2,1,0:T(8,128)(2,1)S(1)}, bf16[4,2,128,128]{3,2,1,0:T(8,128)(2,1)S(1)}, u32[]{:S(2)}, u32[]{:S(2)}) collective-permute-start(bf16[4,2,128,128]{3,2,1,0:T(8,128)(2,1)S(1)} %get-tuple-element.62), channel_id=1, source_target_pairs={{0,16},{2,18},{4,20},{6,22},{8,24},{10,26},{12,28},{14,30},{16,0},... | collective-permute-start | bytes 786440 | tf_op jit(solution)/shard_map/ppermute | solution.py:313
  17.4 1.5 %collective-permute-start.5 = (bf16[64,1024]{1,0:T(8,128)(2,1)S(1)}, bf16[64,1024]{1,0:T(8,128)(2,1)S(1)}, u32[]{:S(2)}, u32[]{:S(2)}) collective-permute-start(bf16[64,1024]{1,0:T(8,128)(2,1)S(1)} %copy-done.2), channel_id=1, source_target_pairs={{0,2},{2,0},{4,6},{6,4},{8,10},{10,8},{12,14},{14,12},{16,18},{18,... | collective-permute-start | bytes 393224 | tf_op jit(solution)/shard_map/ppermute | solution.py:313
  18.9 1.6 %collective-permute-start.6 = (bf16[64,1024]{1,0:T(8,128)(2,1)S(1)}, bf16[64,1024]{1,0:T(8,128)(2,1)S(1)}, u32[]{:S(2)}, u32[]{:S(2)}) collective-permute-start(bf16[64,1024]{1,0:T(8,128)(2,1)S(1)} %copy-done.2), channel_id=1, source_target_pairs={{0,8},{2,10},{4,12},{6,14},{8,0},{10,2},{12,4},{14,6},{16,24},{18,... | collective-permute-start | bytes 393224 | tf_op jit(solution)/shard_map/ppermute | solution.py:313
  20.9 2.3 %collective-permute-done.5.refs_1_ = bf16[64,1024]{1,0:T(8,128)(2,1)S(1)} collective-permute-done((bf16[64,1024]{1,0:T(8,128)(2,1)S(1)}, bf16[64,1024]{1,0:T(8,128)(2,1)S(1)}, u32[]{:S(2)}, u32[]{:S(2)}) %collective-permute-start.5) | collective-permute-done | bytes 131104 | tf_op jit(solution)/shard_map/ppermute | solution.py:313
  23.2 5.1 %collective-permute-done.6.refs_2_ = bf16[64,1024]{1,0:T(8,128)(2,1)S(1)} collective-permute-done((bf16[64,1024]{1,0:T(8,128)(2,1)S(1)}, bf16[64,1024]{1,0:T(8,128)(2,1)S(1)}, u32[]{:S(2)}, u32[]{:S(2)}) %collective-permute-start.6) | collective-permute-done | bytes 131104 | tf_op jit(solution)/shard_map/ppermute | solution.py:313
  28.3 1.6 %collective-permute-done.7.refs_3_ = bf16[64,1024]{1,0:T(8,128)(2,1)S(1)} collective-permute-done((bf16[64,1024]{1,0:T(8,128)(2,1)S(1)}, bf16[64,1024]{1,0:T(8,128)(2,1)S(1)}, u32[]{:S(2)}, u32[]{:S(2)}) %collective-permute-start.7) | collective-permute-done | bytes 131104 | tf_op jit(solution)/shard_map/ppermute | solution.py:313
  32.9 1.7 %attend.2 = (bf16[512,256]{1,0:T(8,128)(2,1)S(1)}, f32[512,128]{1,0:T(8,128)S(1)}) custom-call(s32[16]{0:T(128)S(1)} %copy-done.3, s32[16]{0:T(128)S(1)} %copy-done.4, s32[4]{0:T(128)S(1)} %copy-done.5, s32[4]{0:T(128)S(1)} %copy-done.6, bf16[512,128]{1,0:T(8,128)(2,1)S(1)} %get-tuple-element.70.refs_4_, f32[512,128]{1,0:T(8,128)S(1)} %get-tuple-element.71.refs_5_, ...), custom_call_target="tpu_custom_call" | custom-call | tf_op jit(solution)/shard_map/attend/pallas_call | solution.py:350
  34.6 4.1 %collective-permute-done.9.refs_6_ = bf16[4,2,128,128]{3,2,1,0:T(8,128)(2,1)S(1)} collective-permute-done((bf16[4,2,128,128]{3,2,1,0:T(8,128)(2,1)S(1)}, bf16[4,2,128,128]{3,2,1,0:T(8,128)(2,1)S(1)}, u32[]{:S(2)}, u32[]{:S(2)}) %collective-permute-start.9) | collective-permute-done | bytes 262176 | tf_op jit(solution)/shard_map/ppermute | solution.py:313
  38.7 1.3 %finish.2.refs_0_ = bf16[512,128]{1,0:T(8,128)(2,1)S(1)} custom-call(s32[16]{0:T(128)S(1)} %copy-done.3, s32[16]{0:T(128)S(1)} %copy-done.4, s32[4]{0:T(128)S(1)} %copy-done.5, bf16[512,256]{1,0:T(8,128)(2,1)S(1)} %get-tuple-element.74.refs_3_, f32[512,128]{1,0:T(8,128)S(1)} %get-tuple-element.75.refs_4_, bf16[512,128]{1,0:T(8,128)(2,1)S(1)} %get-tuple-element.76.refs_5_, ...), custom_call_target="tpu_custom_call" | custom-call | tf_op jit(solution)/shard_map/finish/pallas_call | solution.py:350
  40.0 1.4 %collective-permute-start.10 = (bf16[512,128]{1,0:T(8,128)(2,1)S(1)}, bf16[512,128]{1,0:T(8,128)(2,1)S(1)}, u32[]{:S(2)}, u32[]{:S(2)}) collective-permute-start(bf16[512,128]{1,0:T(8,128)(2,1)S(1)} %finish.2.refs_0_), channel_id=1, source_target_pairs={{0,2},{2,0},{4,6},{6,4},{8,10},{10,8},{12,14},{14,12},{16,18},{18,... | collective-permute-start | bytes 393224 | tf_op jit(solution)/shard_map/ppermute | solution.py:313
  41.6 2.0 %collective-permute-start.12 = (bf16[512,128]{1,0:T(8,128)(2,1)S(1)}, bf16[512,128]{1,0:T(8,128)(2,1)S(1)}, u32[]{:S(2)}, u32[]{:S(2)}) collective-permute-start(bf16[512,128]{1,0:T(8,128)(2,1)S(1)} %finish.2.refs_0_), channel_id=1, source_target_pairs={{0,10},{2,8},{4,14},{6,12},{8,2},{10,0},{12,6},{14,4},{16,26},{18,... | collective-permute-start | bytes 393224 | tf_op jit(solution)/shard_map/ppermute | solution.py:313
  43.6 1.8 %collective-permute-done.13.i_ref = bf16[4,2,128,128]{3,2,1,0:T(8,128)(2,1)S(1)} collective-permute-done((bf16[4,2,128,128]{3,2,1,0:T(8,128)(2,1)S(1)}, bf16[4,2,128,128]{3,2,1,0:T(8,128)(2,1)S(1)}, u32[]{:S(2)}, u32[]{:S(2)}) %collective-permute-start.13) | collective-permute-done | bytes 262176 | tf_op jit(solution)/shard_map/ppermute | solution.py:313
  45.4 1.6 %collective-permute-start.14 = (bf16[2,2,128,128]{3,2,1,0:T(8,128)(2,1)S(1)}, bf16[2,2,128,128]{3,2,1,0:T(8,128)(2,1)S(1)}, u32[]{:S(2)}, u32[]{:S(2)}) collective-permute-start(bf16[2,2,128,128]{3,2,1,0:T(8,128)(2,1)S(1)} %get-tuple-element.91.refs_8_), channel_id=1, source_target_pairs={{0,4},{2,6},{4,0},{6,2},{8,12},{10,14},{12,8},{14,10},{16,20},{18,... | collective-permute-start | bytes 393224 | tf_op jit(solution)/shard_map/ppermute | solution.py:313
  47.0 3.4 %pick_head.3.refs_3_ = bf16[1024,512]{1,0:T(8,128)(2,1)S(1)} custom-call(bf16[2,1024,4,512]{3,2,1,0:T(4,128)(2,1)} %w_ref.3), custom_call_target="tpu_custom_call" | custom-call | tf_op jit(solution)/shard_map/pick_head/pallas_call | solution.py:350
  52.4 1.6 %collective-permute-start.16 = (bf16[2,2,128,128]{3,2,1,0:T(8,128)(2,1)S(1)}, bf16[2,2,128,128]{3,2,1,0:T(8,128)(2,1)S(1)}, u32[]{:S(2)}, u32[]{:S(2)}) collective-permute-start(bf16[2,2,128,128]{3,2,1,0:T(8,128)(2,1)S(1)} %get-tuple-element.92.refs_9_), channel_id=1, source_target_pairs={{0,4},{2,6},{4,0},{6,2},{8,12},{10,14},{12,8},{14,10},{16,20},{18,... | collective-permute-start | bytes 393224 | tf_op jit(solution)/shard_map/ppermute | solution.py:313
  56.0 1.8 %attend.3 = (bf16[512,256]{1,0:T(8,128)(2,1)S(1)}, f32[512,128]{1,0:T(8,128)S(1)}) custom-call(s32[16]{0:T(128)S(1)} %copy-done.3, s32[16]{0:T(128)S(1)} %copy-done.4, s32[4]{0:T(128)S(1)} %copy-done.5, s32[4]{0:T(128)S(1)} %copy-done.6, bf16[512,128]{1,0:T(8,128)(2,1)S(1)} %get-tuple-element.89.refs_4_, f32[512,128]{1,0:T(8,128)S(1)} %get-tuple-element.90.refs_5_, ...), custom_call_target="tpu_custom_call" | custom-call | tf_op jit(solution)/shard_map/attend/pallas_call | solution.py:350
  60.4 2.6 %collective-permute-start.19 = (bf16[128,128]{1,0:T(8,128)(2,1)S(1)}, bf16[128,128]{1,0:T(8,128)(2,1)S(1)}, u32[]{:S(2)}, u32[]{:S(2)}) collective-permute-start(bf16[128,128]{1,0:T(8,128)(2,1)S(1)} %get-tuple-element.100), channel_id=1, source_target_pairs={{0,10},{2,8},{4,14},{6,12},{8,2},{10,0},{12,6},{14,4},{16,26},{18,... | collective-permute-start | bytes 98312 | tf_op jit(solution)/shard_map/ppermute | solution.py:313
  65.7 1.3 %collective-permute-done.20.refs_2_ = bf16[64,1024]{1,0:T(8,128)(2,1)S(1)} collective-permute-done((bf16[64,1024]{1,0:T(8,128)(2,1)S(1)}, bf16[64,1024]{1,0:T(8,128)(2,1)S(1)}, u32[]{:S(2)}, u32[]{:S(2)}) %collective-permute-start.20) | collective-permute-done | bytes 131104 | tf_op jit(solution)/shard_map/ppermute | solution.py:331
  (47 shorter events, 16.0 us)
Async XLA Ops:
  1.0 31.9 %copy-start.5 = (s32[4]{0:T(128)S(1)}, s32[4]{0:T(128)}, u32[]{:S(2)}) copy-start(s32[4]{0:T(128)} %refs_2_.7) | copy-start | bytes 52
  1.1 31.9 %copy-start.6 = (s32[4]{0:T(128)S(1)}, s32[4]{0:T(128)}, u32[]{:S(2)}) copy-start(s32[4]{0:T(128)} %refs_3_.3) | copy-start | bytes 52
  2.3 8.0 %collective-permute-start = (bf16[2,2,128,128]{3,2,1,0:T(8,128)(2,1)S(1)}, bf16[2,2,128,128]{3,2,1,0:T(8,128)(2,1)S(1)}, u32[]{:S(2)}, u32[]{:S(2)}) collective-permute-start(bf16[2,2,128,128]{3,2,1,0:T(8,128)(2,1)S(1)} %get-tuple-element.55), channel_id=1, source_target_pairs={{0,2},{2,0},{4,6},{6,4},{8,10},{10,8},{12,14},{14,12},{16,18},{18,... | collective-permute-start | bytes 393224 | tf_op jit(solution)/shard_map/ppermute | solution.py:313
  5.3 6.4 %collective-permute-start.1 = (bf16[2,2,128,128]{3,2,1,0:T(8,128)(2,1)S(1)}, bf16[2,2,128,128]{3,2,1,0:T(8,128)(2,1)S(1)}, u32[]{:S(2)}, u32[]{:S(2)}) collective-permute-start(bf16[2,2,128,128]{3,2,1,0:T(8,128)(2,1)S(1)} %get-tuple-element.56), channel_id=1, source_target_pairs={{0,8},{2,10},{4,12},{6,14},{8,0},{10,2},{12,4},{14,6},{16,24},{18,... | collective-permute-start | bytes 393224 | tf_op jit(solution)/shard_map/ppermute | solution.py:313
  6.9 6.0 %collective-permute-start.2 = (bf16[2,2,128,128]{3,2,1,0:T(8,128)(2,1)S(1)}, bf16[2,2,128,128]{3,2,1,0:T(8,128)(2,1)S(1)}, u32[]{:S(2)}, u32[]{:S(2)}) collective-permute-start(bf16[2,2,128,128]{3,2,1,0:T(8,128)(2,1)S(1)} %get-tuple-element.57), channel_id=1, source_target_pairs={{0,10},{2,8},{4,14},{6,12},{8,2},{10,0},{12,6},{14,4},{16,26},{18,... | collective-permute-start | bytes 393224 | tf_op jit(solution)/shard_map/ppermute | solution.py:313
  10.3 41.2 %copy-start = (bf16[2,4,128,1024]{3,2,1,0:T(8,128)(2,1)S(1)}, bf16[2,4,128,1024]{3,2,1,0:T(8,128)(2,1)}, u32[]{:S(2)}) copy-start(bf16[2,4,128,1024]{3,2,1,0:T(8,128)(2,1)} %refs_4_.3) | copy-start | bytes 6291460
  13.0 16.9 %collective-permute-start.4 = (bf16[2,4,2,128,128]{4,3,2,1,0:T(8,128)(2,1)S(1)}, bf16[2,4,2,128,128]{4,3,2,1,0:T(8,128)(2,1)S(1)}, u32[]{:S(2)}, u32[]{:S(2)}) collective-permute-start(bf16[2,4,2,128,128]{4,3,2,1,0:T(8,128)(2,1)S(1)} %get-tuple-element.63.refs_6_), channel_id=1, source_target_pairs={{0,4},{2,6},{4,0},{6,2},{8,12},{10,14},{12,8},{14,10},{16,20},{18,... | collective-permute-start | bytes 1572872 | tf_op jit(solution)/shard_map/ppermute | solution.py:313
  14.8 15.1 %collective-permute-start.3 = (bf16[4,2,128,128]{3,2,1,0:T(8,128)(2,1)S(1)}, bf16[4,2,128,128]{3,2,1,0:T(8,128)(2,1)S(1)}, u32[]{:S(2)}, u32[]{:S(2)}) collective-permute-start(bf16[4,2,128,128]{3,2,1,0:T(8,128)(2,1)S(1)} %get-tuple-element.62), channel_id=1, source_target_pairs={{0,16},{2,18},{4,20},{6,22},{8,24},{10,26},{12,28},{14,30},{16,0},... | collective-permute-start | bytes 786440 | tf_op jit(solution)/shard_map/ppermute | solution.py:313
  17.4 5.8 %collective-permute-start.5 = (bf16[64,1024]{1,0:T(8,128)(2,1)S(1)}, bf16[64,1024]{1,0:T(8,128)(2,1)S(1)}, u32[]{:S(2)}, u32[]{:S(2)}) collective-permute-start(bf16[64,1024]{1,0:T(8,128)(2,1)S(1)} %copy-done.2), channel_id=1, source_target_pairs={{0,2},{2,0},{4,6},{6,4},{8,10},{10,8},{12,14},{14,12},{16,18},{18,... | collective-permute-start | bytes 393224 | tf_op jit(solution)/shard_map/ppermute | solution.py:313
  18.9 9.4 %collective-permute-start.6 = (bf16[64,1024]{1,0:T(8,128)(2,1)S(1)}, bf16[64,1024]{1,0:T(8,128)(2,1)S(1)}, u32[]{:S(2)}, u32[]{:S(2)}) collective-permute-start(bf16[64,1024]{1,0:T(8,128)(2,1)S(1)} %copy-done.2), channel_id=1, source_target_pairs={{0,8},{2,10},{4,12},{6,14},{8,0},{10,2},{12,4},{14,6},{16,24},{18,... | collective-permute-start | bytes 393224 | tf_op jit(solution)/shard_map/ppermute | solution.py:313
  20.5 9.4 %collective-permute-start.7 = (bf16[64,1024]{1,0:T(8,128)(2,1)S(1)}, bf16[64,1024]{1,0:T(8,128)(2,1)S(1)}, u32[]{:S(2)}, u32[]{:S(2)}) collective-permute-start(bf16[64,1024]{1,0:T(8,128)(2,1)S(1)} %copy-done.2), channel_id=1, source_target_pairs={{0,10},{2,8},{4,14},{6,12},{8,2},{10,0},{12,6},{14,4},{16,26},{18,... | collective-permute-start | bytes 393224 | tf_op jit(solution)/shard_map/ppermute | solution.py:313
  29.9 2.0 %collective-permute-start.8 = (bf16[4,64,1024]{2,1,0:T(8,128)(2,1)S(1)}, bf16[4,64,1024]{2,1,0:T(8,128)(2,1)S(1)}, u32[]{:S(2)}, u32[]{:S(2)}) collective-permute-start(bf16[4,64,1024]{2,1,0:T(8,128)(2,1)S(1)} %join.1), channel_id=1, source_target_pairs={{0,1},{1,0},{2,3},{3,2},{4,5},{5,4},{6,7},{7,6},{8,9},{9,8},{10,11... | collective-permute-start | bytes 1572872 | tf_op jit(solution)/shard_map/ppermute | solution.py:331
  30.0 8.7 %collective-permute-start.9 = (bf16[4,2,128,128]{3,2,1,0:T(8,128)(2,1)S(1)}, bf16[4,2,128,128]{3,2,1,0:T(8,128)(2,1)S(1)}, u32[]{:S(2)}, u32[]{:S(2)}) collective-permute-start(bf16[4,2,128,128]{3,2,1,0:T(8,128)(2,1)S(1)} %collective-permute-done.3.refs_8_), channel_id=1, source_target_pairs={{0,4},{2,6},{4,0},{6,2},{8,12},{10,14},{12,8},{14,10},{16,20},{18,... | collective-permute-start | bytes 786440 | tf_op jit(solution)/shard_map/ppermute | solution.py:313
  30.6 14.8 %collective-permute-start.13 = (bf16[4,2,128,128]{3,2,1,0:T(8,128)(2,1)S(1)}, bf16[4,2,128,128]{3,2,1,0:T(8,128)(2,1)S(1)}, u32[]{:S(2)}, u32[]{:S(2)}) collective-permute-start(bf16[4,2,128,128]{3,2,1,0:T(8,128)(2,1)S(1)} %get-tuple-element.78), channel_id=1, source_target_pairs={{0,16},{2,18},{4,20},{6,22},{8,24},{10,26},{12,28},{14,30},{16,0},... | collective-permute-start | bytes 786440 | tf_op jit(solution)/shard_map/ppermute | solution.py:313
  40.0 5.4 %collective-permute-start.10 = (bf16[512,128]{1,0:T(8,128)(2,1)S(1)}, bf16[512,128]{1,0:T(8,128)(2,1)S(1)}, u32[]{:S(2)}, u32[]{:S(2)}) collective-permute-start(bf16[512,128]{1,0:T(8,128)(2,1)S(1)} %finish.2.refs_0_), channel_id=1, source_target_pairs={{0,2},{2,0},{4,6},{6,4},{8,10},{10,8},{12,14},{14,12},{16,18},{18,... | collective-permute-start | bytes 393224 | tf_op jit(solution)/shard_map/ppermute | solution.py:313
  41.4 9.1 %collective-permute-start.11 = (bf16[512,128]{1,0:T(8,128)(2,1)S(1)}, bf16[512,128]{1,0:T(8,128)(2,1)S(1)}, u32[]{:S(2)}, u32[]{:S(2)}) collective-permute-start(bf16[512,128]{1,0:T(8,128)(2,1)S(1)} %finish.2.refs_0_), channel_id=1, source_target_pairs={{0,8},{2,10},{4,12},{6,14},{8,0},{10,2},{12,4},{14,6},{16,24},{18,... | collective-permute-start | bytes 393224 | tf_op jit(solution)/shard_map/ppermute | solution.py:313
  41.6 9.9 %collective-permute-start.12 = (bf16[512,128]{1,0:T(8,128)(2,1)S(1)}, bf16[512,128]{1,0:T(8,128)(2,1)S(1)}, u32[]{:S(2)}, u32[]{:S(2)}) collective-permute-start(bf16[512,128]{1,0:T(8,128)(2,1)S(1)} %finish.2.refs_0_), channel_id=1, source_target_pairs={{0,10},{2,8},{4,14},{6,12},{8,2},{10,0},{12,6},{14,4},{16,26},{18,... | collective-permute-start | bytes 393224 | tf_op jit(solution)/shard_map/ppermute | solution.py:313
  45.4 6.1 %collective-permute-start.14 = (bf16[2,2,128,128]{3,2,1,0:T(8,128)(2,1)S(1)}, bf16[2,2,128,128]{3,2,1,0:T(8,128)(2,1)S(1)}, u32[]{:S(2)}, u32[]{:S(2)}) collective-permute-start(bf16[2,2,128,128]{3,2,1,0:T(8,128)(2,1)S(1)} %get-tuple-element.91.refs_8_), channel_id=1, source_target_pairs={{0,4},{2,6},{4,0},{6,2},{8,12},{10,14},{12,8},{14,10},{16,20},{18,... | collective-permute-start | bytes 393224 | tf_op jit(solution)/shard_map/ppermute | solution.py:313
  52.3 2.7 %collective-permute-start.15 = (bf16[512,1024]{1,0:T(8,128)(2,1)S(1)}, bf16[512,1024]{1,0:T(8,128)(2,1)S(1)}, u32[]{:S(2)}, u32[]{:S(2)}) collective-permute-start(bf16[512,1024]{1,0:T(8,128)(2,1)S(1)} %term.1.refs_0_), channel_id=1, source_target_pairs={{0,1},{1,0},{2,3},{3,2},{4,5},{5,4},{6,7},{7,6},{8,9},{9,8},{10,11... | collective-permute-start | bytes 3145736 | tf_op jit(solution)/shard_map/ppermute | solution.py:331
  52.4 5.9 %collective-permute-start.16 = (bf16[2,2,128,128]{3,2,1,0:T(8,128)(2,1)S(1)}, bf16[2,2,128,128]{3,2,1,0:T(8,128)(2,1)S(1)}, u32[]{:S(2)}, u32[]{:S(2)}) collective-permute-start(bf16[2,2,128,128]{3,2,1,0:T(8,128)(2,1)S(1)} %get-tuple-element.92.refs_9_), channel_id=1, source_target_pairs={{0,4},{2,6},{4,0},{6,2},{8,12},{10,14},{12,8},{14,10},{16,20},{18,... | collective-permute-start | bytes 393224 | tf_op jit(solution)/shard_map/ppermute | solution.py:313
  59.5 4.3 %collective-permute-start.17 = (bf16[128,128]{1,0:T(8,128)(2,1)S(1)}, bf16[128,128]{1,0:T(8,128)(2,1)S(1)}, u32[]{:S(2)}, u32[]{:S(2)}) collective-permute-start(bf16[128,128]{1,0:T(8,128)(2,1)S(1)} %get-tuple-element.98), channel_id=1, source_target_pairs={{0,2},{2,0},{4,6},{6,4},{8,10},{10,8},{12,14},{14,12},{16,18},{18,... | collective-permute-start | bytes 98312 | tf_op jit(solution)/shard_map/ppermute | solution.py:313
  60.4 3.9 %collective-permute-start.18 = (bf16[128,128]{1,0:T(8,128)(2,1)S(1)}, bf16[128,128]{1,0:T(8,128)(2,1)S(1)}, u32[]{:S(2)}, u32[]{:S(2)}) collective-permute-start(bf16[128,128]{1,0:T(8,128)(2,1)S(1)} %get-tuple-element.99), channel_id=1, source_target_pairs={{0,8},{2,10},{4,12},{6,14},{8,0},{10,2},{12,4},{14,6},{16,24},{18,... | collective-permute-start | bytes 98312 | tf_op jit(solution)/shard_map/ppermute | solution.py:313
  60.4 4.8 %collective-permute-start.19 = (bf16[128,128]{1,0:T(8,128)(2,1)S(1)}, bf16[128,128]{1,0:T(8,128)(2,1)S(1)}, u32[]{:S(2)}, u32[]{:S(2)}) collective-permute-start(bf16[128,128]{1,0:T(8,128)(2,1)S(1)} %get-tuple-element.100), channel_id=1, source_target_pairs={{0,10},{2,8},{4,14},{6,12},{8,2},{10,0},{12,6},{14,4},{16,26},{18,... | collective-permute-start | bytes 98312 | tf_op jit(solution)/shard_map/ppermute | solution.py:313
  65.6 1.4 %collective-permute-start.20 = (bf16[64,1024]{1,0:T(8,128)(2,1)S(1)}, bf16[64,1024]{1,0:T(8,128)(2,1)S(1)}, u32[]{:S(2)}, u32[]{:S(2)}) collective-permute-start(bf16[64,1024]{1,0:T(8,128)(2,1)S(1)} %get-tuple-element.102), channel_id=1, source_target_pairs={{0,1},{1,0},{2,3},{3,2},{4,5},{5,4},{6,7},{7,6},{8,9},{9,8},{10,11... | collective-permute-start | bytes 393224 | tf_op jit(solution)/shard_map/ppermute | solution.py:331
  (4 other events, 81.1 us)

commit v2 on v1

--- a/solution.py
+++ b/solution.py
@@ -39,10 +39,8 @@
 
 
 def join_layers_kernel(count, *refs):
-    every_ref, *layer_refs = refs[count:]
-    for layer_index, o_ref in enumerate(layer_refs):
+    for layer_index, o_ref in enumerate(refs[count:]):
         for at, ref in enumerate(refs[:count]):
-            every_ref[layer_index, at] = ref[layer_index]
             o_ref[at] = ref[layer_index]
 
 
@@ -176,7 +174,6 @@
     chip, _, _ = position(spot_bits)
     spot_part = chip & spot_of_chip
     member_part = chip - spot_part
-    history_refs = [ref if len(ref.shape) == 4 else ref.at[layer_index] for ref in history_refs]
 
     def visit(ref, first, count, member, at):
         keys, values = [], []
@@ -387,13 +384,13 @@
 
     def join_layers(pieces):
         shape = (spots, 2, local_rows, head_dim)
-        every, first, *later = kernel_call(
+        first, *later = kernel_call(
             functools.partial(join_layers_kernel, spots),
-            [((layers,) + shape, jnp.bfloat16)] + [(shape, jnp.bfloat16)] * layers,
+            [(shape, jnp.bfloat16)] * layers,
             "join_layers",
             list(pieces),
         )
-        return every, first, later
+        return first, later
 
     def halves(pieces):
         shape = (pieces.shape[0] // 2,) + pieces.shape[1:]
@@ -409,15 +406,15 @@
         return lax.optimization_barrier(values)
 
     pieces, first_weight = together(trade_spots(order_history()), pick_head(0))
-    every, first, later = join_layers(pieces)
+    first, later = join_layers(pieces)
     x_pieces = trade_spots([after(candidate_rows, first)] * spots)
     crossed = groups == 4
     if crossed:
         near_mask, far_mask = member_masks[1:3]
-        far, near, x_pieces = together(
-            swap(first, far_mask), swap(every, near_mask), x_pieces
-        )
-        history = [[every, near, far, swap(far, near_mask)]]
+        far = swap(first, far_mask)
+        near = swap(first, near_mask)
+        far, near, x_pieces = together(far, near, x_pieces)
+        history = [[first, near, far, swap(far, near_mask)]]
     else:
         history = [gather_members(first)]
     x_group = x_pieces + [shift_core(join(x_pieces), s) for s in range(1, cores)]
@@ -468,11 +465,12 @@
             gated = trade_spots(list(gated) * spots)
             next_weight = pick_head(layer_index + 1)
             if crossed:
-                far = swap(after(later[layer_index], far), far_mask)
-                far = halves(after(far, gated[1]))
+                whole = after(later[layer_index], far, near)
+                far, near = swap(whole, far_mask), swap(whole, near_mask)
+                far = halves(after(far, near, gated[1]))
                 ahead = swap(far[0], near_mask)
                 gated, far, ahead, next_weight = together(gated, far, ahead, next_weight)
-                arrays = [every, near] + far + [ahead, swap(far[1], near_mask)]
+                arrays = [whole, near] + far + [ahead, swap(far[1], near_mask)]
             else:
                 arrays = gather_members(later[layer_index])
             terms = kernel_call(

time: 67.9 us -> 67.6 us (level)
    ppermute x18 -> x19, waiting for transfers between devices: 21.2 us -> 21.5 us  [swap(): return lax.ppermute(value, 'users', [(u, u ^ mask) for u in range(chips)])]
    ppermute x18 -> x19, starting transfers between devices: 23.5 us -> 23.5 us  [swap(): return lax.ppermute(value, 'users', [(u, u ^ mask) for u in range(chips)])]
  transfers between devices with their start and end apart: 21 -> 22, of which waited for: 15 -> 15; matrix products, arithmetic and copies ran while one was open for 0% -> 0% of each run, Pallas kernels for 20% -> 20%
where the time goes in v2:
time: 67.6 us; the launch traced here: 67.4 us
  waiting for transfers between devices  24.5 us (36%)
  starting transfers between devices  23.7 us (35%)
  Pallas kernels  17.9 us (26%)
  local copies, waits for them, and re-layouts  1.07 us (2%)
    ppermute x19, starting transfers between devices, swap(): return lax.ppermute(value, 'users', [(u, u ^ mask) for u in range(chips)])  23.5 us
    ppermute x19, waiting for transfers between devices, swap(): return lax.ppermute(value, 'users', [(u, u ^ mask) for u in range(chips)])  21.5 us
    pallas_call x15, Pallas kernels, kernel_call(): pl.pallas_call(kernel, out_shape=[jax.ShapeDtypeStruct(*out) for out in o...  17.9 us
    ppermute x3, waiting for transfers between devices, shift_core(): return lax.ppermute(value, 'cand', pairs)  2.98 us
  transfers between devices with their start and end apart: 22, of which 15 were waited for; matrix products, arithmetic and copies ran while one was open for 0% of the time, Pallas kernels for 20%

profile of v2, /device:TPU:0, one launch (start us, length us, event | category | flops | bytes accessed | tf_op | source)
XLA Modules:
  0.0 67.4 jit_solution(385889049944705642)
XLA Ops:
  2.3 3.0 %collective-permute-start = (bf16[2,2,128,128]{3,2,1,0:T(8,128)(2,1)S(1)}, bf16[2,2,128,128]{3,2,1,0:T(8,128)(2,1)S(1)}, u32[]{:S(2)}, u32[]{:S(2)}) collective-permute-start(bf16[2,2,128,128]{3,2,1,0:T(8,128)(2,1)S(1)} %get-tuple-element.54), channel_id=1, source_target_pairs={{0,2},{2,0},{4,6},{6,4},{8,10},{10,8},{12,14},{14,12},{16,18},{18,... | collective-permute-start | bytes 393224 | tf_op jit(solution)/shard_map/ppermute | solution.py:310
  5.3 1.6 %collective-permute-start.1 = (bf16[2,2,128,128]{3,2,1,0:T(8,128)(2,1)S(1)}, bf16[2,2,128,128]{3,2,1,0:T(8,128)(2,1)S(1)}, u32[]{:S(2)}, u32[]{:S(2)}) collective-permute-start(bf16[2,2,128,128]{3,2,1,0:T(8,128)(2,1)S(1)} %get-tuple-element.55), channel_id=1, source_target_pairs={{0,8},{2,10},{4,12},{6,14},{8,0},{10,2},{12,4},{14,6},{16,24},{18,... | collective-permute-start | bytes 393224 | tf_op jit(solution)/shard_map/ppermute | solution.py:310
  6.9 3.4 %pick_head.2.refs_5_ = bf16[1024,512]{1,0:T(8,128)(2,1)S(1)} custom-call(bf16[2,1024,4,512]{3,2,1,0:T(4,128)(2,1)} %w_ref.3), custom_call_target="tpu_custom_call" | custom-call | tf_op jit(solution)/shard_map/pick_head/pallas_call | solution.py:347
  10.3 1.4 %collective-permute-done.1.refs_2_ = bf16[2,2,128,128]{3,2,1,0:T(8,128)(2,1)S(1)} collective-permute-done((bf16[2,2,128,128]{3,2,1,0:T(8,128)(2,1)S(1)}, bf16[2,2,128,128]{3,2,1,0:T(8,128)(2,1)S(1)}, u32[]{:S(2)}, u32[]{:S(2)}) %collective-permute-start.1) | collective-permute-done | bytes 131104 | tf_op jit(solution)/shard_map/ppermute | solution.py:310
  12.9 2.8 %collective-permute-start.3 = (bf16[4,2,128,128]{3,2,1,0:T(8,128)(2,1)S(1)}, bf16[4,2,128,128]{3,2,1,0:T(8,128)(2,1)S(1)}, u32[]{:S(2)}, u32[]{:S(2)}) collective-permute-start(bf16[4,2,128,128]{3,2,1,0:T(8,128)(2,1)S(1)} %get-tuple-element.61.refs_6_), channel_id=1, source_target_pairs={{0,16},{2,18},{4,20},{6,22},{8,24},{10,26},{12,28},{14,30},{16,0},... | collective-permute-start | bytes 786440 | tf_op jit(solution)/shard_map/ppermute | solution.py:310
  15.8 1.5 %collective-permute-start.4 = (bf16[4,2,128,128]{3,2,1,0:T(8,128)(2,1)S(1)}, bf16[4,2,128,128]{3,2,1,0:T(8,128)(2,1)S(1)}, u32[]{:S(2)}, u32[]{:S(2)}) collective-permute-start(bf16[4,2,128,128]{3,2,1,0:T(8,128)(2,1)S(1)} %get-tuple-element.61.refs_6_), channel_id=1, source_target_pairs={{0,4},{2,6},{4,0},{6,2},{8,12},{10,14},{12,8},{14,10},{16,20},{18,... | collective-permute-start | bytes 786440 | tf_op jit(solution)/shard_map/ppermute | solution.py:310
  17.3 1.5 %collective-permute-start.5 = (bf16[64,1024]{1,0:T(8,128)(2,1)S(1)}, bf16[64,1024]{1,0:T(8,128)(2,1)S(1)}, u32[]{:S(2)}, u32[]{:S(2)}) collective-permute-start(bf16[64,1024]{1,0:T(8,128)(2,1)S(1)} %copy-done.2), channel_id=1, source_target_pairs={{0,2},{2,0},{4,6},{6,4},{8,10},{10,8},{12,14},{14,12},{16,18},{18,... | collective-permute-start | bytes 393224 | tf_op jit(solution)/shard_map/ppermute | solution.py:310
  18.8 1.6 %collective-permute-start.6 = (bf16[64,1024]{1,0:T(8,128)(2,1)S(1)}, bf16[64,1024]{1,0:T(8,128)(2,1)S(1)}, u32[]{:S(2)}, u32[]{:S(2)}) collective-permute-start(bf16[64,1024]{1,0:T(8,128)(2,1)S(1)} %copy-done.2), channel_id=1, source_target_pairs={{0,8},{2,10},{4,12},{6,14},{8,0},{10,2},{12,4},{14,6},{16,24},{18,... | collective-permute-start | bytes 393224 | tf_op jit(solution)/shard_map/ppermute | solution.py:310
  20.8 2.0 %collective-permute-done.5.refs_1_ = bf16[64,1024]{1,0:T(8,128)(2,1)S(1)} collective-permute-done((bf16[64,1024]{1,0:T(8,128)(2,1)S(1)}, bf16[64,1024]{1,0:T(8,128)(2,1)S(1)}, u32[]{:S(2)}, u32[]{:S(2)}) %collective-permute-start.5) | collective-permute-done | bytes 131104 | tf_op jit(solution)/shard_map/ppermute | solution.py:310
  22.7 5.4 %collective-permute-done.6.refs_2_ = bf16[64,1024]{1,0:T(8,128)(2,1)S(1)} collective-permute-done((bf16[64,1024]{1,0:T(8,128)(2,1)S(1)}, bf16[64,1024]{1,0:T(8,128)(2,1)S(1)}, u32[]{:S(2)}, u32[]{:S(2)}) %collective-permute-start.6) | collective-permute-done | bytes 131104 | tf_op jit(solution)/shard_map/ppermute | solution.py:310
  28.2 1.4 %collective-permute-done.7.refs_3_ = bf16[64,1024]{1,0:T(8,128)(2,1)S(1)} collective-permute-done((bf16[64,1024]{1,0:T(8,128)(2,1)S(1)}, bf16[64,1024]{1,0:T(8,128)(2,1)S(1)}, u32[]{:S(2)}, u32[]{:S(2)}) %collective-permute-start.7) | collective-permute-done | bytes 131104 | tf_op jit(solution)/shard_map/ppermute | solution.py:310
  30.5 1.3 %collective-permute-start.14 = (bf16[4,2,128,128]{3,2,1,0:T(8,128)(2,1)S(1)}, bf16[4,2,128,128]{3,2,1,0:T(8,128)(2,1)S(1)}, u32[]{:S(2)}, u32[]{:S(2)}) collective-permute-start(bf16[4,2,128,128]{3,2,1,0:T(8,128)(2,1)S(1)} %get-tuple-element.76.refs_6_), channel_id=1, source_target_pairs={{0,4},{2,6},{4,0},{6,2},{8,12},{10,14},{12,8},{14,10},{16,20},{18,... | collective-permute-start | bytes 786440 | tf_op jit(solution)/shard_map/ppermute | solution.py:310
  32.8 1.7 %attend.2 = (bf16[512,256]{1,0:T(8,128)(2,1)S(1)}, f32[512,128]{1,0:T(8,128)S(1)}) custom-call(s32[16]{0:T(128)S(1)} %copy-done.3, s32[16]{0:T(128)S(1)} %copy-done.4, s32[4]{0:T(128)S(1)} %copy-done.5, s32[4]{0:T(128)S(1)} %copy-done.6, bf16[512,128]{1,0:T(8,128)(2,1)S(1)} %get-tuple-element.68.refs_4_, f32[512,128]{1,0:T(8,128)S(1)} %get-tuple-element.69.refs_5_, ...), custom_call_target="tpu_custom_call" | custom-call | tf_op jit(solution)/shard_map/attend/pallas_call | solution.py:347
  34.5 4.3 %collective-permute-done.9.refs_6_ = bf16[4,2,128,128]{3,2,1,0:T(8,128)(2,1)S(1)} collective-permute-done((bf16[4,2,128,128]{3,2,1,0:T(8,128)(2,1)S(1)}, bf16[4,2,128,128]{3,2,1,0:T(8,128)(2,1)S(1)}, u32[]{:S(2)}, u32[]{:S(2)}) %collective-permute-start.9) | collective-permute-done | bytes 262176 | tf_op jit(solution)/shard_map/ppermute | solution.py:310
  38.9 1.3 %finish.2.refs_0_ = bf16[512,128]{1,0:T(8,128)(2,1)S(1)} custom-call(s32[16]{0:T(128)S(1)} %copy-done.3, s32[16]{0:T(128)S(1)} %copy-done.4, s32[4]{0:T(128)S(1)} %copy-done.5, bf16[512,256]{1,0:T(8,128)(2,1)S(1)} %get-tuple-element.72.refs_3_, f32[512,128]{1,0:T(8,128)S(1)} %get-tuple-element.73.refs_4_, bf16[512,128]{1,0:T(8,128)(2,1)S(1)} %get-tuple-element.74.refs_5_, ...), custom_call_target="tpu_custom_call" | custom-call | tf_op jit(solution)/shard_map/finish/pallas_call | solution.py:347
  40.2 1.5 %collective-permute-start.10 = (bf16[512,128]{1,0:T(8,128)(2,1)S(1)}, bf16[512,128]{1,0:T(8,128)(2,1)S(1)}, u32[]{:S(2)}, u32[]{:S(2)}) collective-permute-start(bf16[512,128]{1,0:T(8,128)(2,1)S(1)} %finish.2.refs_0_), channel_id=1, source_target_pairs={{0,2},{2,0},{4,6},{6,4},{8,10},{10,8},{12,14},{14,12},{16,18},{18,... | collective-permute-start | bytes 393224 | tf_op jit(solution)/shard_map/ppermute | solution.py:310
  41.7 2.0 %collective-permute-start.12 = (bf16[512,128]{1,0:T(8,128)(2,1)S(1)}, bf16[512,128]{1,0:T(8,128)(2,1)S(1)}, u32[]{:S(2)}, u32[]{:S(2)}) collective-permute-start(bf16[512,128]{1,0:T(8,128)(2,1)S(1)} %finish.2.refs_0_), channel_id=1, source_target_pairs={{0,10},{2,8},{4,14},{6,12},{8,2},{10,0},{12,6},{14,4},{16,26},{18,... | collective-permute-start | bytes 393224 | tf_op jit(solution)/shard_map/ppermute | solution.py:310
  43.7 1.3 %collective-permute-done.13.i_ref = bf16[4,2,128,128]{3,2,1,0:T(8,128)(2,1)S(1)} collective-permute-done((bf16[4,2,128,128]{3,2,1,0:T(8,128)(2,1)S(1)}, bf16[4,2,128,128]{3,2,1,0:T(8,128)(2,1)S(1)}, u32[]{:S(2)}, u32[]{:S(2)}) %collective-permute-start.13) | collective-permute-done | bytes 262176 | tf_op jit(solution)/shard_map/ppermute | solution.py:310
  46.1 3.4 %pick_head.3.refs_3_ = bf16[1024,512]{1,0:T(8,128)(2,1)S(1)} custom-call(bf16[2,1024,4,512]{3,2,1,0:T(4,128)(2,1)} %w_ref.3), custom_call_target="tpu_custom_call" | custom-call | tf_op jit(solution)/shard_map/pick_head/pallas_call | solution.py:347
  49.5 1.6 %collective-permute-done.12.refs_3_ = bf16[512,128]{1,0:T(8,128)(2,1)S(1)} collective-permute-done((bf16[512,128]{1,0:T(8,128)(2,1)S(1)}, bf16[512,128]{1,0:T(8,128)(2,1)S(1)}, u32[]{:S(2)}, u32[]{:S(2)}) %collective-permute-start.12) | collective-permute-done | bytes 131104 | tf_op jit(solution)/shard_map/ppermute | solution.py:310
  53.0 1.6 %collective-permute-done.16.refs_1_ = bf16[512,1024]{1,0:T(8,128)(2,1)S(1)} collective-permute-done((bf16[512,1024]{1,0:T(8,128)(2,1)S(1)}, bf16[512,1024]{1,0:T(8,128)(2,1)S(1)}, u32[]{:S(2)}, u32[]{:S(2)}) %collective-permute-start.16) | collective-permute-done | bytes 1048608 | tf_op jit(solution)/shard_map/ppermute | solution.py:328
  55.6 1.8 %attend.3 = (bf16[512,256]{1,0:T(8,128)(2,1)S(1)}, f32[512,128]{1,0:T(8,128)S(1)}) custom-call(s32[16]{0:T(128)S(1)} %copy-done.3, s32[16]{0:T(128)S(1)} %copy-done.4, s32[4]{0:T(128)S(1)} %copy-done.5, s32[4]{0:T(128)S(1)} %copy-done.6, bf16[512,128]{1,0:T(8,128)(2,1)S(1)} %get-tuple-element.87.refs_4_, f32[512,128]{1,0:T(8,128)S(1)} %get-tuple-element.88.refs_5_, ...), custom_call_target="tpu_custom_call" | custom-call | tf_op jit(solution)/shard_map/attend/pallas_call | solution.py:347
  60.1 2.6 %collective-permute-start.20 = (bf16[128,128]{1,0:T(8,128)(2,1)S(1)}, bf16[128,128]{1,0:T(8,128)(2,1)S(1)}, u32[]{:S(2)}, u32[]{:S(2)}) collective-permute-start(bf16[128,128]{1,0:T(8,128)(2,1)S(1)} %get-tuple-element.98), channel_id=1, source_target_pairs={{0,10},{2,8},{4,14},{6,12},{8,2},{10,0},{12,6},{14,4},{16,26},{18,... | collective-permute-start | bytes 98312 | tf_op jit(solution)/shard_map/ppermute | solution.py:310
  65.4 1.3 %collective-permute-done.21.refs_2_ = bf16[64,1024]{1,0:T(8,128)(2,1)S(1)} collective-permute-done((bf16[64,1024]{1,0:T(8,128)(2,1)S(1)}, bf16[64,1024]{1,0:T(8,128)(2,1)S(1)}, u32[]{:S(2)}, u32[]{:S(2)}) %collective-permute-start.21) | collective-permute-done | bytes 131104 | tf_op jit(solution)/shard_map/ppermute | solution.py:328
  (49 shorter events, 15.7 us)
Async XLA Ops:
  1.1 31.8 %copy-start.6 = (s32[4]{0:T(128)S(1)}, s32[4]{0:T(128)}, u32[]{:S(2)}) copy-start(s32[4]{0:T(128)} %refs_3_.3) | copy-start | bytes 52
  2.3 8.0 %collective-permute-start = (bf16[2,2,128,128]{3,2,1,0:T(8,128)(2,1)S(1)}, bf16[2,2,128,128]{3,2,1,0:T(8,128)(2,1)S(1)}, u32[]{:S(2)}, u32[]{:S(2)}) collective-permute-start(bf16[2,2,128,128]{3,2,1,0:T(8,128)(2,1)S(1)} %get-tuple-element.54), channel_id=1, source_target_pairs={{0,2},{2,0},{4,6},{6,4},{8,10},{10,8},{12,14},{14,12},{16,18},{18,... | collective-permute-start | bytes 393224 | tf_op jit(solution)/shard_map/ppermute | solution.py:310
  5.3 6.4 %collective-permute-start.1 = (bf16[2,2,128,128]{3,2,1,0:T(8,128)(2,1)S(1)}, bf16[2,2,128,128]{3,2,1,0:T(8,128)(2,1)S(1)}, u32[]{:S(2)}, u32[]{:S(2)}) collective-permute-start(bf16[2,2,128,128]{3,2,1,0:T(8,128)(2,1)S(1)} %get-tuple-element.55), channel_id=1, source_target_pairs={{0,8},{2,10},{4,12},{6,14},{8,0},{10,2},{12,4},{14,6},{16,24},{18,... | collective-permute-start | bytes 393224 | tf_op jit(solution)/shard_map/ppermute | solution.py:310
  6.9 6.0 %collective-permute-start.2 = (bf16[2,2,128,128]{3,2,1,0:T(8,128)(2,1)S(1)}, bf16[2,2,128,128]{3,2,1,0:T(8,128)(2,1)S(1)}, u32[]{:S(2)}, u32[]{:S(2)}) collective-permute-start(bf16[2,2,128,128]{3,2,1,0:T(8,128)(2,1)S(1)} %get-tuple-element.56), channel_id=1, source_target_pairs={{0,10},{2,8},{4,14},{6,12},{8,2},{10,0},{12,6},{14,4},{16,26},{18,... | collective-permute-start | bytes 393224 | tf_op jit(solution)/shard_map/ppermute | solution.py:310
  10.3 40.9 %copy-start = (bf16[2,4,128,1024]{3,2,1,0:T(8,128)(2,1)S(1)}, bf16[2,4,128,1024]{3,2,1,0:T(8,128)(2,1)}, u32[]{:S(2)}) copy-start(bf16[2,4,128,1024]{3,2,1,0:T(8,128)(2,1)} %refs_4_.3) | copy-start | bytes 6291460
  12.9 16.6 %collective-permute-start.3 = (bf16[4,2,128,128]{3,2,1,0:T(8,128)(2,1)S(1)}, bf16[4,2,128,128]{3,2,1,0:T(8,128)(2,1)S(1)}, u32[]{:S(2)}, u32[]{:S(2)}) collective-permute-start(bf16[4,2,128,128]{3,2,1,0:T(8,128)(2,1)S(1)} %get-tuple-element.61.refs_6_), channel_id=1, source_target_pairs={{0,16},{2,18},{4,20},{6,22},{8,24},{10,26},{12,28},{14,30},{16,0},... | collective-permute-start | bytes 786440 | tf_op jit(solution)/shard_map/ppermute | solution.py:310
  15.8 13.8 %collective-permute-start.4 = (bf16[4,2,128,128]{3,2,1,0:T(8,128)(2,1)S(1)}, bf16[4,2,128,128]{3,2,1,0:T(8,128)(2,1)S(1)}, u32[]{:S(2)}, u32[]{:S(2)}) collective-permute-start(bf16[4,2,128,128]{3,2,1,0:T(8,128)(2,1)S(1)} %get-tuple-element.61.refs_6_), channel_id=1, source_target_pairs={{0,4},{2,6},{4,0},{6,2},{8,12},{10,14},{12,8},{14,10},{16,20},{18,... | collective-permute-start | bytes 786440 | tf_op jit(solution)/shard_map/ppermute | solution.py:310
  17.3 5.5 %collective-permute-start.5 = (bf16[64,1024]{1,0:T(8,128)(2,1)S(1)}, bf16[64,1024]{1,0:T(8,128)(2,1)S(1)}, u32[]{:S(2)}, u32[]{:S(2)}) collective-permute-start(bf16[64,1024]{1,0:T(8,128)(2,1)S(1)} %copy-done.2), channel_id=1, source_target_pairs={{0,2},{2,0},{4,6},{6,4},{8,10},{10,8},{12,14},{14,12},{16,18},{18,... | collective-permute-start | bytes 393224 | tf_op jit(solution)/shard_map/ppermute | solution.py:310
  18.8 9.4 %collective-permute-start.6 = (bf16[64,1024]{1,0:T(8,128)(2,1)S(1)}, bf16[64,1024]{1,0:T(8,128)(2,1)S(1)}, u32[]{:S(2)}, u32[]{:S(2)}) collective-permute-start(bf16[64,1024]{1,0:T(8,128)(2,1)S(1)} %copy-done.2), channel_id=1, source_target_pairs={{0,8},{2,10},{4,12},{6,14},{8,0},{10,2},{12,4},{14,6},{16,24},{18,... | collective-permute-start | bytes 393224 | tf_op jit(solution)/shard_map/ppermute | solution.py:310
  20.4 9.2 %collective-permute-start.7 = (bf16[64,1024]{1,0:T(8,128)(2,1)S(1)}, bf16[64,1024]{1,0:T(8,128)(2,1)S(1)}, u32[]{:S(2)}, u32[]{:S(2)}) collective-permute-start(bf16[64,1024]{1,0:T(8,128)(2,1)S(1)} %copy-done.2), channel_id=1, source_target_pairs={{0,10},{2,8},{4,14},{6,12},{8,2},{10,0},{12,6},{14,4},{16,26},{18,... | collective-permute-start | bytes 393224 | tf_op jit(solution)/shard_map/ppermute | solution.py:310
  29.6 2.2 %collective-permute-start.8 = (bf16[4,64,1024]{2,1,0:T(8,128)(2,1)S(1)}, bf16[4,64,1024]{2,1,0:T(8,128)(2,1)S(1)}, u32[]{:S(2)}, u32[]{:S(2)}) collective-permute-start(bf16[4,64,1024]{2,1,0:T(8,128)(2,1)S(1)} %join.1), channel_id=1, source_target_pairs={{0,1},{1,0},{2,3},{3,2},{4,5},{5,4},{6,7},{7,6},{8,9},{9,8},{10,11... | collective-permute-start | bytes 1572872 | tf_op jit(solution)/shard_map/ppermute | solution.py:328
  29.7 9.2 %collective-permute-start.9 = (bf16[4,2,128,128]{3,2,1,0:T(8,128)(2,1)S(1)}, bf16[4,2,128,128]{3,2,1,0:T(8,128)(2,1)S(1)}, u32[]{:S(2)}, u32[]{:S(2)}) collective-permute-start(bf16[4,2,128,128]{3,2,1,0:T(8,128)(2,1)S(1)} %collective-permute-done.3.refs_8_), channel_id=1, source_target_pairs={{0,4},{2,6},{4,0},{6,2},{8,12},{10,14},{12,8},{14,10},{16,20},{18,... | collective-permute-start | bytes 786440 | tf_op jit(solution)/shard_map/ppermute | solution.py:310
  30.5 14.6 %collective-permute-start.13 = (bf16[4,2,128,128]{3,2,1,0:T(8,128)(2,1)S(1)}, bf16[4,2,128,128]{3,2,1,0:T(8,128)(2,1)S(1)}, u32[]{:S(2)}, u32[]{:S(2)}) collective-permute-start(bf16[4,2,128,128]{3,2,1,0:T(8,128)(2,1)S(1)} %get-tuple-element.76.refs_6_), channel_id=1, source_target_pairs={{0,16},{2,18},{4,20},{6,22},{8,24},{10,26},{12,28},{14,30},{16,0},... | collective-permute-start | bytes 786440 | tf_op jit(solution)/shard_map/ppermute | solution.py:310
  30.5 14.5 %collective-permute-start.14 = (bf16[4,2,128,128]{3,2,1,0:T(8,128)(2,1)S(1)}, bf16[4,2,128,128]{3,2,1,0:T(8,128)(2,1)S(1)}, u32[]{:S(2)}, u32[]{:S(2)}) collective-permute-start(bf16[4,2,128,128]{3,2,1,0:T(8,128)(2,1)S(1)} %get-tuple-element.76.refs_6_), channel_id=1, source_target_pairs={{0,4},{2,6},{4,0},{6,2},{8,12},{10,14},{12,8},{14,10},{16,20},{18,... | collective-permute-start | bytes 786440 | tf_op jit(solution)/shard_map/ppermute | solution.py:310
  40.2 5.0 %collective-permute-start.10 = (bf16[512,128]{1,0:T(8,128)(2,1)S(1)}, bf16[512,128]{1,0:T(8,128)(2,1)S(1)}, u32[]{:S(2)}, u32[]{:S(2)}) collective-permute-start(bf16[512,128]{1,0:T(8,128)(2,1)S(1)} %finish.2.refs_0_), channel_id=1, source_target_pairs={{0,2},{2,0},{4,6},{6,4},{8,10},{10,8},{12,14},{14,12},{16,18},{18,... | collective-permute-start | bytes 393224 | tf_op jit(solution)/shard_map/ppermute | solution.py:310
  41.7 7.9 %collective-permute-start.11 = (bf16[512,128]{1,0:T(8,128)(2,1)S(1)}, bf16[512,128]{1,0:T(8,128)(2,1)S(1)}, u32[]{:S(2)}, u32[]{:S(2)}) collective-permute-start(bf16[512,128]{1,0:T(8,128)(2,1)S(1)} %finish.2.refs_0_), channel_id=1, source_target_pairs={{0,8},{2,10},{4,12},{6,14},{8,0},{10,2},{12,4},{14,6},{16,24},{18,... | collective-permute-start | bytes 393224 | tf_op jit(solution)/shard_map/ppermute | solution.py:310
  41.7 9.5 %collective-permute-start.12 = (bf16[512,128]{1,0:T(8,128)(2,1)S(1)}, bf16[512,128]{1,0:T(8,128)(2,1)S(1)}, u32[]{:S(2)}, u32[]{:S(2)}) collective-permute-start(bf16[512,128]{1,0:T(8,128)(2,1)S(1)} %finish.2.refs_0_), channel_id=1, source_target_pairs={{0,10},{2,8},{4,14},{6,12},{8,2},{10,0},{12,6},{14,4},{16,26},{18,... | collective-permute-start | bytes 393224 | tf_op jit(solution)/shard_map/ppermute | solution.py:310
  45.2 5.9 %collective-permute-start.15 = (bf16[2,2,128,128]{3,2,1,0:T(8,128)(2,1)S(1)}, bf16[2,2,128,128]{3,2,1,0:T(8,128)(2,1)S(1)}, u32[]{:S(2)}, u32[]{:S(2)}) collective-permute-start(bf16[2,2,128,128]{3,2,1,0:T(8,128)(2,1)S(1)} %get-tuple-element.89.refs_8_), channel_id=1, source_target_pairs={{0,4},{2,6},{4,0},{6,2},{8,12},{10,14},{12,8},{14,10},{16,20},{18,... | collective-permute-start | bytes 393224 | tf_op jit(solution)/shard_map/ppermute | solution.py:310
  52.0 2.7 %collective-permute-start.16 = (bf16[512,1024]{1,0:T(8,128)(2,1)S(1)}, bf16[512,1024]{1,0:T(8,128)(2,1)S(1)}, u32[]{:S(2)}, u32[]{:S(2)}) collective-permute-start(bf16[512,1024]{1,0:T(8,128)(2,1)S(1)} %term.1.refs_0_), channel_id=1, source_target_pairs={{0,1},{1,0},{2,3},{3,2},{4,5},{5,4},{6,7},{7,6},{8,9},{9,8},{10,11... | collective-permute-start | bytes 3145736 | tf_op jit(solution)/shard_map/ppermute | solution.py:328
  52.0 5.9 %collective-permute-start.17 = (bf16[2,2,128,128]{3,2,1,0:T(8,128)(2,1)S(1)}, bf16[2,2,128,128]{3,2,1,0:T(8,128)(2,1)S(1)}, u32[]{:S(2)}, u32[]{:S(2)}) collective-permute-start(bf16[2,2,128,128]{3,2,1,0:T(8,128)(2,1)S(1)} %get-tuple-element.90.refs_9_), channel_id=1, source_target_pairs={{0,4},{2,6},{4,0},{6,2},{8,12},{10,14},{12,8},{14,10},{16,20},{18,... | collective-permute-start | bytes 393224 | tf_op jit(solution)/shard_map/ppermute | solution.py:310
  59.1 4.3 %collective-permute-start.18 = (bf16[128,128]{1,0:T(8,128)(2,1)S(1)}, bf16[128,128]{1,0:T(8,128)(2,1)S(1)}, u32[]{:S(2)}, u32[]{:S(2)}) collective-permute-start(bf16[128,128]{1,0:T(8,128)(2,1)S(1)} %get-tuple-element.96), channel_id=1, source_target_pairs={{0,2},{2,0},{4,6},{6,4},{8,10},{10,8},{12,14},{14,12},{16,18},{18,... | collective-permute-start | bytes 98312 | tf_op jit(solution)/shard_map/ppermute | solution.py:310
  60.1 3.9 %collective-permute-start.19 = (bf16[128,128]{1,0:T(8,128)(2,1)S(1)}, bf16[128,128]{1,0:T(8,128)(2,1)S(1)}, u32[]{:S(2)}, u32[]{:S(2)}) collective-permute-start(bf16[128,128]{1,0:T(8,128)(2,1)S(1)} %get-tuple-element.97), channel_id=1, source_target_pairs={{0,8},{2,10},{4,12},{6,14},{8,0},{10,2},{12,4},{14,6},{16,24},{18,... | collective-permute-start | bytes 98312 | tf_op jit(solution)/shard_map/ppermute | solution.py:310
  60.1 4.8 %collective-permute-start.20 = (bf16[128,128]{1,0:T(8,128)(2,1)S(1)}, bf16[128,128]{1,0:T(8,128)(2,1)S(1)}, u32[]{:S(2)}, u32[]{:S(2)}) collective-permute-start(bf16[128,128]{1,0:T(8,128)(2,1)S(1)} %get-tuple-element.98), channel_id=1, source_target_pairs={{0,10},{2,8},{4,14},{6,12},{8,2},{10,0},{12,6},{14,4},{16,26},{18,... | collective-permute-start | bytes 98312 | tf_op jit(solution)/shard_map/ppermute | solution.py:310
  65.3 1.4 %collective-permute-start.21 = (bf16[64,1024]{1,0:T(8,128)(2,1)S(1)}, bf16[64,1024]{1,0:T(8,128)(2,1)S(1)}, u32[]{:S(2)}, u32[]{:S(2)}) collective-permute-start(bf16[64,1024]{1,0:T(8,128)(2,1)S(1)} %get-tuple-element.100), channel_id=1, source_target_pairs={{0,1},{1,0},{2,3},{3,2},{4,5},{5,4},{6,7},{7,6},{8,9},{9,8},{10,11... | collective-permute-start | bytes 393224 | tf_op jit(solution)/shard_map/ppermute | solution.py:328
  (5 other events, 112.5 us)

commit v3 on v2

--- a/solution.py
+++ b/solution.py
@@ -32,8 +32,9 @@
     _, spot, _ = position(spot_bits)
     for layer_index in range(h_ref.shape[0]):
         for kind in range(h_ref.shape[1]):
+            by_head = jnp.swapaxes(h_ref[layer_index, kind], 0, 1)
             for head in range(h_ref.shape[3]):
-                pieces[spot ^ head, layer_index, kind] = h_ref[layer_index, kind, :, head, :]
+                pieces[spot ^ head, layer_index, kind] = by_head[head]
     for step, o_ref in enumerate(o_refs):
         o_ref[...] = pieces[step]
 
@@ -119,18 +120,23 @@
         wide[:, pl.ds(at, dim)] = ref[...]
 
 
-def term_kernel(spots, spot_bits, layer_index, *refs):
+def term_kernel(spot_bits, layer_index, first_step, *refs):
     _, spot, _ = position(spot_bits)
-    gated_refs, (weight_ref, o_ref, wide) = refs[:spots], refs[spots:]
-    gather_heads(gated_refs, spot, wide)
-    depth, width = wide.shape[1], o_ref.shape[1]
+    count = len(refs) - 2 - (1 if first_step else 0)
+    gated_refs, (weight_ref, *before_refs, o_ref) = refs[:count], refs[count:]
+    gated = jnp.concatenate([ref[...] for ref in gated_refs], axis=1)
+    width = o_ref.shape[1]
     tile = min(width, 256)
     for first in range(0, width, tile):
         columns = slice(first, first + tile)
-        weight = weight_ref[layer_index, :, :, columns].reshape(depth, tile)
-        o_ref[:, columns] = jnp.dot(
-            wide[...], weight, preferred_element_type=jnp.float32
-        ).astype(jnp.bfloat16)
+        weight = jnp.concatenate(
+            [weight_ref[layer_index, spot ^ (first_step + at), :, columns] for at in range(count)],
+            axis=0,
+        )
+        term = jnp.dot(gated, weight, preferred_element_type=jnp.float32)
+        if before_refs:
+            term = term + before_refs[0][:, columns]
+        o_ref[:, columns] = term.astype(o_ref.dtype)
 
 
 def step_kernel(spots, cores, spot_bits, score_scale, *refs):
@@ -469,17 +475,26 @@
                 far, near = swap(whole, far_mask), swap(whole, near_mask)
                 far = halves(after(far, near, gated[1]))
                 ahead = swap(far[0], near_mask)
-                gated, far, ahead, next_weight = together(gated, far, ahead, next_weight)
+                early, far, next_weight = together(gated[:-1], far, next_weight)
+                late, ahead = together(gated[-1:], ahead)
+                parts = [(0, early), (spots - 1, late)]
                 arrays = [whole, near] + far + [ahead, swap(far[1], near_mask)]
             else:
                 arrays = gather_members(later[layer_index])
-            terms = kernel_call(
-                functools.partial(term_kernel, spots, spot_bits, layer_index),
-                [((all_rows, model_width), jnp.bfloat16)],
-                "term",
-                gated + [weight_out],
-                [pltpu.VMEM((all_rows, spots * head_dim), jnp.bfloat16)],
-            )
+                parts = [(0, gated)]
+            terms = []
+            for first_step, heads in parts:
+                terms = kernel_call(
+                    functools.partial(term_kernel, spot_bits, layer_index, first_step),
+                    [
+                        (
+                            (all_rows, model_width),
+                            jnp.bfloat16 if first_step + len(heads) == spots else jnp.float32,
+                        )
+                    ],
+                    "term",
+                    heads + [weight_out] + terms,
+                )
             terms = terms + [shift_core(terms[0], s) for s in range(1, cores)]
             history.append(arrays)
             x, *projected = kernel_call(

time: 67.6 us -> 66.4 us (0.982)
  waiting for transfers between devices: 24.5 us -> 23.7 us
    ppermute x19, waiting for transfers between devices: 21.5 us -> 20.7 us  [swap(): return lax.ppermute(value, 'users', [(u, u ^ mask) for u in range(chips)])]
    pallas_call x15 -> x16, Pallas kernels: 17.9 us -> 17.5 us  [kernel_call(): pl.pallas_call(kernel, out_shape=[jax.ShapeDtypeStruct(*out) for out in o...]
  transfers between devices with their start and end apart: 22 -> 22, of which waited for: 15 -> 15; matrix products, arithmetic and copies ran while one was open for 0% -> 0% of each run, Pallas kernels for 20% -> 22%
where the time goes in v3:
time: 66.4 us; the launch traced here: 66.2 us
  starting transfers between devices  23.7 us (36%)
  waiting for transfers between devices  23.7 us (36%)
  Pallas kernels  17.5 us (26%)
  local copies, waits for them, and re-layouts  1.08 us (2%)
    ppermute x19, starting transfers between devices, swap(): return lax.ppermute(value, 'users', [(u, u ^ mask) for u in range(chips)])  23.5 us
    ppermute x19, waiting for transfers between devices, swap(): return lax.ppermute(value, 'users', [(u, u ^ mask) for u in range(chips)])  20.7 us
    pallas_call x16, Pallas kernels, kernel_call(): pl.pallas_call(kernel, out_shape=[jax.ShapeDtypeStruct(*out) for out in o...  17.5 us
    ppermute x3, waiting for transfers between devices, shift_core(): return lax.ppermute(value, 'cand', pairs)  2.98 us
  transfers between devices with their start and end apart: 22, of which 15 were waited for; matrix products, arithmetic and copies ran while one was open for 0% of the time, Pallas kernels for 22%

profile of v3, /device:TPU:0, one launch (start us, length us, event | category | flops | bytes accessed | tf_op | source)
XLA Modules:
  0.0 66.2 jit_solution(2934260373890692154)
XLA Ops:
  1.5 3.0 %collective-permute-start = (bf16[2,2,128,128]{3,2,1,0:T(8,128)(2,1)S(1)}, bf16[2,2,128,128]{3,2,1,0:T(8,128)(2,1)S(1)}, u32[]{:S(2)}, u32[]{:S(2)}) collective-permute-start(bf16[2,2,128,128]{3,2,1,0:T(8,128)(2,1)S(1)} %get-tuple-element.54), channel_id=1, source_target_pairs={{0,2},{2,0},{4,6},{6,4},{8,10},{10,8},{12,14},{14,12},{16,18},{18,... | collective-permute-start | bytes 393224 | tf_op jit(solution)/shard_map/ppermute | solution.py:316
  4.5 1.6 %collective-permute-start.1 = (bf16[2,2,128,128]{3,2,1,0:T(8,128)(2,1)S(1)}, bf16[2,2,128,128]{3,2,1,0:T(8,128)(2,1)S(1)}, u32[]{:S(2)}, u32[]{:S(2)}) collective-permute-start(bf16[2,2,128,128]{3,2,1,0:T(8,128)(2,1)S(1)} %get-tuple-element.55), channel_id=1, source_target_pairs={{0,8},{2,10},{4,12},{6,14},{8,0},{10,2},{12,4},{14,6},{16,24},{18,... | collective-permute-start | bytes 393224 | tf_op jit(solution)/shard_map/ppermute | solution.py:316
  6.1 3.4 %pick_head.2.refs_5_ = bf16[1024,512]{1,0:T(8,128)(2,1)S(1)} custom-call(bf16[2,1024,4,512]{3,2,1,0:T(4,128)(2,1)} %w_ref.3), custom_call_target="tpu_custom_call" | custom-call | tf_op jit(solution)/shard_map/pick_head/pallas_call | solution.py:353
  9.6 1.3 %collective-permute-done.1.refs_2_ = bf16[2,2,128,128]{3,2,1,0:T(8,128)(2,1)S(1)} collective-permute-done((bf16[2,2,128,128]{3,2,1,0:T(8,128)(2,1)S(1)}, bf16[2,2,128,128]{3,2,1,0:T(8,128)(2,1)S(1)}, u32[]{:S(2)}, u32[]{:S(2)}) %collective-permute-start.1) | collective-permute-done | bytes 131104 | tf_op jit(solution)/shard_map/ppermute | solution.py:316
  10.9 1.2 %collective-permute-done.2.refs_3_ = bf16[2,2,128,128]{3,2,1,0:T(8,128)(2,1)S(1)} collective-permute-done((bf16[2,2,128,128]{3,2,1,0:T(8,128)(2,1)S(1)}, bf16[2,2,128,128]{3,2,1,0:T(8,128)(2,1)S(1)}, u32[]{:S(2)}, u32[]{:S(2)}) %collective-permute-start.2) | collective-permute-done | bytes 131104 | tf_op jit(solution)/shard_map/ppermute | solution.py:316
  12.1 2.8 %collective-permute-start.3 = (bf16[4,2,128,128]{3,2,1,0:T(8,128)(2,1)S(1)}, bf16[4,2,128,128]{3,2,1,0:T(8,128)(2,1)S(1)}, u32[]{:S(2)}, u32[]{:S(2)}) collective-permute-start(bf16[4,2,128,128]{3,2,1,0:T(8,128)(2,1)S(1)} %get-tuple-element.61.refs_6_), channel_id=1, source_target_pairs={{0,16},{2,18},{4,20},{6,22},{8,24},{10,26},{12,28},{14,30},{16,0},... | collective-permute-start | bytes 786440 | tf_op jit(solution)/shard_map/ppermute | solution.py:316
  14.9 1.5 %collective-permute-start.4 = (bf16[4,2,128,128]{3,2,1,0:T(8,128)(2,1)S(1)}, bf16[4,2,128,128]{3,2,1,0:T(8,128)(2,1)S(1)}, u32[]{:S(2)}, u32[]{:S(2)}) collective-permute-start(bf16[4,2,128,128]{3,2,1,0:T(8,128)(2,1)S(1)} %get-tuple-element.61.refs_6_), channel_id=1, source_target_pairs={{0,4},{2,6},{4,0},{6,2},{8,12},{10,14},{12,8},{14,10},{16,20},{18,... | collective-permute-start | bytes 786440 | tf_op jit(solution)/shard_map/ppermute | solution.py:316
  16.5 1.5 %collective-permute-start.5 = (bf16[64,1024]{1,0:T(8,128)(2,1)S(1)}, bf16[64,1024]{1,0:T(8,128)(2,1)S(1)}, u32[]{:S(2)}, u32[]{:S(2)}) collective-permute-start(bf16[64,1024]{1,0:T(8,128)(2,1)S(1)} %copy-done.2), channel_id=1, source_target_pairs={{0,2},{2,0},{4,6},{6,4},{8,10},{10,8},{12,14},{14,12},{16,18},{18,... | collective-permute-start | bytes 393224 | tf_op jit(solution)/shard_map/ppermute | solution.py:316
  17.9 1.6 %collective-permute-start.6 = (bf16[64,1024]{1,0:T(8,128)(2,1)S(1)}, bf16[64,1024]{1,0:T(8,128)(2,1)S(1)}, u32[]{:S(2)}, u32[]{:S(2)}) collective-permute-start(bf16[64,1024]{1,0:T(8,128)(2,1)S(1)} %copy-done.2), channel_id=1, source_target_pairs={{0,8},{2,10},{4,12},{6,14},{8,0},{10,2},{12,4},{14,6},{16,24},{18,... | collective-permute-start | bytes 393224 | tf_op jit(solution)/shard_map/ppermute | solution.py:316
  20.0 2.0 %collective-permute-done.5.refs_1_ = bf16[64,1024]{1,0:T(8,128)(2,1)S(1)} collective-permute-done((bf16[64,1024]{1,0:T(8,128)(2,1)S(1)}, bf16[64,1024]{1,0:T(8,128)(2,1)S(1)}, u32[]{:S(2)}, u32[]{:S(2)}) %collective-permute-start.5) | collective-permute-done | bytes 131104 | tf_op jit(solution)/shard_map/ppermute | solution.py:316
  21.9 5.4 %collective-permute-done.6.refs_2_ = bf16[64,1024]{1,0:T(8,128)(2,1)S(1)} collective-permute-done((bf16[64,1024]{1,0:T(8,128)(2,1)S(1)}, bf16[64,1024]{1,0:T(8,128)(2,1)S(1)}, u32[]{:S(2)}, u32[]{:S(2)}) %collective-permute-start.6) | collective-permute-done | bytes 131104 | tf_op jit(solution)/shard_map/ppermute | solution.py:316
  27.3 1.4 %collective-permute-done.7.refs_3_ = bf16[64,1024]{1,0:T(8,128)(2,1)S(1)} collective-permute-done((bf16[64,1024]{1,0:T(8,128)(2,1)S(1)}, bf16[64,1024]{1,0:T(8,128)(2,1)S(1)}, u32[]{:S(2)}, u32[]{:S(2)}) %collective-permute-start.7) | collective-permute-done | bytes 131104 | tf_op jit(solution)/shard_map/ppermute | solution.py:316
  29.7 1.3 %collective-permute-start.12 = (bf16[4,2,128,128]{3,2,1,0:T(8,128)(2,1)S(1)}, bf16[4,2,128,128]{3,2,1,0:T(8,128)(2,1)S(1)}, u32[]{:S(2)}, u32[]{:S(2)}) collective-permute-start(bf16[4,2,128,128]{3,2,1,0:T(8,128)(2,1)S(1)} %get-tuple-element.76.refs_6_), channel_id=1, source_target_pairs={{0,4},{2,6},{4,0},{6,2},{8,12},{10,14},{12,8},{14,10},{16,20},{18,... | collective-permute-start | bytes 786440 | tf_op jit(solution)/shard_map/ppermute | solution.py:316
  32.0 1.7 %attend.2 = (bf16[512,256]{1,0:T(8,128)(2,1)S(1)}, f32[512,128]{1,0:T(8,128)S(1)}) custom-call(s32[16]{0:T(128)S(1)} %copy-done.3, s32[16]{0:T(128)S(1)} %copy-done.4, s32[4]{0:T(128)S(1)} %copy-done.5, s32[4]{0:T(128)S(1)} %copy-done.6, bf16[512,128]{1,0:T(8,128)(2,1)S(1)} %get-tuple-element.68.refs_4_, f32[512,128]{1,0:T(8,128)S(1)} %get-tuple-element.69.refs_5_, ...), custom_call_target="tpu_custom_call" | custom-call | tf_op jit(solution)/shard_map/attend/pallas_call | solution.py:353
  33.7 4.3 %collective-permute-done.9.refs_6_ = bf16[4,2,128,128]{3,2,1,0:T(8,128)(2,1)S(1)} collective-permute-done((bf16[4,2,128,128]{3,2,1,0:T(8,128)(2,1)S(1)}, bf16[4,2,128,128]{3,2,1,0:T(8,128)(2,1)S(1)}, u32[]{:S(2)}, u32[]{:S(2)}) %collective-permute-start.9) | collective-permute-done | bytes 262176 | tf_op jit(solution)/shard_map/ppermute | solution.py:316
  38.0 1.3 %finish.2.refs_0_ = bf16[512,128]{1,0:T(8,128)(2,1)S(1)} custom-call(s32[16]{0:T(128)S(1)} %copy-done.3, s32[16]{0:T(128)S(1)} %copy-done.4, s32[4]{0:T(128)S(1)} %copy-done.5, bf16[512,256]{1,0:T(8,128)(2,1)S(1)} %get-tuple-element.72.refs_3_, f32[512,128]{1,0:T(8,128)S(1)} %get-tuple-element.73.refs_4_, bf16[512,128]{1,0:T(8,128)(2,1)S(1)} %get-tuple-element.74.refs_5_, ...), custom_call_target="tpu_custom_call" | custom-call | tf_op jit(solution)/shard_map/finish/pallas_call | solution.py:353
  39.3 1.5 %collective-permute-start.13 = (bf16[512,128]{1,0:T(8,128)(2,1)S(1)}, bf16[512,128]{1,0:T(8,128)(2,1)S(1)}, u32[]{:S(2)}, u32[]{:S(2)}) collective-permute-start(bf16[512,128]{1,0:T(8,128)(2,1)S(1)} %finish.2.refs_0_), channel_id=1, source_target_pairs={{0,2},{2,0},{4,6},{6,4},{8,10},{10,8},{12,14},{14,12},{16,18},{18,... | collective-permute-start | bytes 393224 | tf_op jit(solution)/shard_map/ppermute | solution.py:316
  40.8 2.0 %collective-permute-start.10 = (bf16[512,128]{1,0:T(8,128)(2,1)S(1)}, bf16[512,128]{1,0:T(8,128)(2,1)S(1)}, u32[]{:S(2)}, u32[]{:S(2)}) collective-permute-start(bf16[512,128]{1,0:T(8,128)(2,1)S(1)} %finish.2.refs_0_), channel_id=1, source_target_pairs={{0,10},{2,8},{4,14},{6,12},{8,2},{10,0},{12,6},{14,4},{16,26},{18,... | collective-permute-start | bytes 393224 | tf_op jit(solution)/shard_map/ppermute | solution.py:316
  42.9 1.3 %collective-permute-done.11.i_ref = bf16[4,2,128,128]{3,2,1,0:T(8,128)(2,1)S(1)} collective-permute-done((bf16[4,2,128,128]{3,2,1,0:T(8,128)(2,1)S(1)}, bf16[4,2,128,128]{3,2,1,0:T(8,128)(2,1)S(1)}, u32[]{:S(2)}, u32[]{:S(2)}) %collective-permute-start.11) | collective-permute-done | bytes 262176 | tf_op jit(solution)/shard_map/ppermute | solution.py:316
  45.3 3.4 %pick_head.3.refs_3_ = bf16[1024,512]{1,0:T(8,128)(2,1)S(1)} custom-call(bf16[2,1024,4,512]{3,2,1,0:T(4,128)(2,1)} %w_ref.3), custom_call_target="tpu_custom_call" | custom-call | tf_op jit(solution)/shard_map/pick_head/pallas_call | solution.py:353
  51.8 1.6 %collective-permute-done.16.refs_1_ = bf16[512,1024]{1,0:T(8,128)(2,1)S(1)} collective-permute-done((bf16[512,1024]{1,0:T(8,128)(2,1)S(1)}, bf16[512,1024]{1,0:T(8,128)(2,1)S(1)}, u32[]{:S(2)}, u32[]{:S(2)}) %collective-permute-start.16) | collective-permute-done | bytes 1048608 | tf_op jit(solution)/shard_map/ppermute | solution.py:334
  54.4 1.8 %attend.3 = (bf16[512,256]{1,0:T(8,128)(2,1)S(1)}, f32[512,128]{1,0:T(8,128)S(1)}) custom-call(s32[16]{0:T(128)S(1)} %copy-done.3, s32[16]{0:T(128)S(1)} %copy-done.4, s32[4]{0:T(128)S(1)} %copy-done.5, s32[4]{0:T(128)S(1)} %copy-done.6, bf16[512,128]{1,0:T(8,128)(2,1)S(1)} %get-tuple-element.87.refs_4_, f32[512,128]{1,0:T(8,128)S(1)} %get-tuple-element.88.refs_5_, ...), custom_call_target="tpu_custom_call" | custom-call | tf_op jit(solution)/shard_map/attend/pallas_call | solution.py:353
  58.9 2.6 %collective-permute-start.20 = (bf16[128,128]{1,0:T(8,128)(2,1)S(1)}, bf16[128,128]{1,0:T(8,128)(2,1)S(1)}, u32[]{:S(2)}, u32[]{:S(2)}) collective-permute-start(bf16[128,128]{1,0:T(8,128)(2,1)S(1)} %get-tuple-element.98), channel_id=1, source_target_pairs={{0,10},{2,8},{4,14},{6,12},{8,2},{10,0},{12,6},{14,4},{16,26},{18,... | collective-permute-start | bytes 98312 | tf_op jit(solution)/shard_map/ppermute | solution.py:316
  64.2 1.3 %collective-permute-done.21.refs_2_ = bf16[64,1024]{1,0:T(8,128)(2,1)S(1)} collective-permute-done((bf16[64,1024]{1,0:T(8,128)(2,1)S(1)}, bf16[64,1024]{1,0:T(8,128)(2,1)S(1)}, u32[]{:S(2)}, u32[]{:S(2)}) %collective-permute-start.21) | collective-permute-done | bytes 131104 | tf_op jit(solution)/shard_map/ppermute | solution.py:334
  (50 shorter events, 14.9 us)
Async XLA Ops:
  1.5 8.1 %collective-permute-start = (bf16[2,2,128,128]{3,2,1,0:T(8,128)(2,1)S(1)}, bf16[2,2,128,128]{3,2,1,0:T(8,128)(2,1)S(1)}, u32[]{:S(2)}, u32[]{:S(2)}) collective-permute-start(bf16[2,2,128,128]{3,2,1,0:T(8,128)(2,1)S(1)} %get-tuple-element.54), channel_id=1, source_target_pairs={{0,2},{2,0},{4,6},{6,4},{8,10},{10,8},{12,14},{14,12},{16,18},{18,... | collective-permute-start | bytes 393224 | tf_op jit(solution)/shard_map/ppermute | solution.py:316
  4.5 6.4 %collective-permute-start.1 = (bf16[2,2,128,128]{3,2,1,0:T(8,128)(2,1)S(1)}, bf16[2,2,128,128]{3,2,1,0:T(8,128)(2,1)S(1)}, u32[]{:S(2)}, u32[]{:S(2)}) collective-permute-start(bf16[2,2,128,128]{3,2,1,0:T(8,128)(2,1)S(1)} %get-tuple-element.55), channel_id=1, source_target_pairs={{0,8},{2,10},{4,12},{6,14},{8,0},{10,2},{12,4},{14,6},{16,24},{18,... | collective-permute-start | bytes 393224 | tf_op jit(solution)/shard_map/ppermute | solution.py:316
  6.1 6.0 %collective-permute-start.2 = (bf16[2,2,128,128]{3,2,1,0:T(8,128)(2,1)S(1)}, bf16[2,2,128,128]{3,2,1,0:T(8,128)(2,1)S(1)}, u32[]{:S(2)}, u32[]{:S(2)}) collective-permute-start(bf16[2,2,128,128]{3,2,1,0:T(8,128)(2,1)S(1)} %get-tuple-element.56), channel_id=1, source_target_pairs={{0,10},{2,8},{4,14},{6,12},{8,2},{10,0},{12,6},{14,4},{16,26},{18,... | collective-permute-start | bytes 393224 | tf_op jit(solution)/shard_map/ppermute | solution.py:316
  9.5 22.4 %copy-start.3 = (s32[16]{0:T(128)S(1)}, s32[16]{0:T(128)}, u32[]{:S(2)}) copy-start(s32[16]{0:T(128)} %refs_0_.9) | copy-start | bytes 196
  9.5 22.4 %copy-start.4 = (s32[16]{0:T(128)S(1)}, s32[16]{0:T(128)}, u32[]{:S(2)}) copy-start(s32[16]{0:T(128)} %refs_1_.9) | copy-start | bytes 196
  12.1 16.6 %collective-permute-start.3 = (bf16[4,2,128,128]{3,2,1,0:T(8,128)(2,1)S(1)}, bf16[4,2,128,128]{3,2,1,0:T(8,128)(2,1)S(1)}, u32[]{:S(2)}, u32[]{:S(2)}) collective-permute-start(bf16[4,2,128,128]{3,2,1,0:T(8,128)(2,1)S(1)} %get-tuple-element.61.refs_6_), channel_id=1, source_target_pairs={{0,16},{2,18},{4,20},{6,22},{8,24},{10,26},{12,28},{14,30},{16,0},... | collective-permute-start | bytes 786440 | tf_op jit(solution)/shard_map/ppermute | solution.py:316
  14.9 13.8 %collective-permute-start.4 = (bf16[4,2,128,128]{3,2,1,0:T(8,128)(2,1)S(1)}, bf16[4,2,128,128]{3,2,1,0:T(8,128)(2,1)S(1)}, u32[]{:S(2)}, u32[]{:S(2)}) collective-permute-start(bf16[4,2,128,128]{3,2,1,0:T(8,128)(2,1)S(1)} %get-tuple-element.61.refs_6_), channel_id=1, source_target_pairs={{0,4},{2,6},{4,0},{6,2},{8,12},{10,14},{12,8},{14,10},{16,20},{18,... | collective-permute-start | bytes 786440 | tf_op jit(solution)/shard_map/ppermute | solution.py:316
  16.5 5.5 %collective-permute-start.5 = (bf16[64,1024]{1,0:T(8,128)(2,1)S(1)}, bf16[64,1024]{1,0:T(8,128)(2,1)S(1)}, u32[]{:S(2)}, u32[]{:S(2)}) collective-permute-start(bf16[64,1024]{1,0:T(8,128)(2,1)S(1)} %copy-done.2), channel_id=1, source_target_pairs={{0,2},{2,0},{4,6},{6,4},{8,10},{10,8},{12,14},{14,12},{16,18},{18,... | collective-permute-start | bytes 393224 | tf_op jit(solution)/shard_map/ppermute | solution.py:316
  17.9 9.4 %collective-permute-start.6 = (bf16[64,1024]{1,0:T(8,128)(2,1)S(1)}, bf16[64,1024]{1,0:T(8,128)(2,1)S(1)}, u32[]{:S(2)}, u32[]{:S(2)}) collective-permute-start(bf16[64,1024]{1,0:T(8,128)(2,1)S(1)} %copy-done.2), channel_id=1, source_target_pairs={{0,8},{2,10},{4,12},{6,14},{8,0},{10,2},{12,4},{14,6},{16,24},{18,... | collective-permute-start | bytes 393224 | tf_op jit(solution)/shard_map/ppermute | solution.py:316
  19.5 9.2 %collective-permute-start.7 = (bf16[64,1024]{1,0:T(8,128)(2,1)S(1)}, bf16[64,1024]{1,0:T(8,128)(2,1)S(1)}, u32[]{:S(2)}, u32[]{:S(2)}) collective-permute-start(bf16[64,1024]{1,0:T(8,128)(2,1)S(1)} %copy-done.2), channel_id=1, source_target_pairs={{0,10},{2,8},{4,14},{6,12},{8,2},{10,0},{12,6},{14,4},{16,26},{18,... | collective-permute-start | bytes 393224 | tf_op jit(solution)/shard_map/ppermute | solution.py:316
  28.8 2.2 %collective-permute-start.8 = (bf16[4,64,1024]{2,1,0:T(8,128)(2,1)S(1)}, bf16[4,64,1024]{2,1,0:T(8,128)(2,1)S(1)}, u32[]{:S(2)}, u32[]{:S(2)}) collective-permute-start(bf16[4,64,1024]{2,1,0:T(8,128)(2,1)S(1)} %join.1), channel_id=1, source_target_pairs={{0,1},{1,0},{2,3},{3,2},{4,5},{5,4},{6,7},{7,6},{8,9},{9,8},{10,11... | collective-permute-start | bytes 1572872 | tf_op jit(solution)/shard_map/ppermute | solution.py:334
  28.9 9.2 %collective-permute-start.9 = (bf16[4,2,128,128]{3,2,1,0:T(8,128)(2,1)S(1)}, bf16[4,2,128,128]{3,2,1,0:T(8,128)(2,1)S(1)}, u32[]{:S(2)}, u32[]{:S(2)}) collective-permute-start(bf16[4,2,128,128]{3,2,1,0:T(8,128)(2,1)S(1)} %collective-permute-done.3.refs_8_), channel_id=1, source_target_pairs={{0,4},{2,6},{4,0},{6,2},{8,12},{10,14},{12,8},{14,10},{16,20},{18,... | collective-permute-start | bytes 786440 | tf_op jit(solution)/shard_map/ppermute | solution.py:316
  29.7 14.6 %collective-permute-start.11 = (bf16[4,2,128,128]{3,2,1,0:T(8,128)(2,1)S(1)}, bf16[4,2,128,128]{3,2,1,0:T(8,128)(2,1)S(1)}, u32[]{:S(2)}, u32[]{:S(2)}) collective-permute-start(bf16[4,2,128,128]{3,2,1,0:T(8,128)(2,1)S(1)} %get-tuple-element.76.refs_6_), channel_id=1, source_target_pairs={{0,16},{2,18},{4,20},{6,22},{8,24},{10,26},{12,28},{14,30},{16,0},... | collective-permute-start | bytes 786440 | tf_op jit(solution)/shard_map/ppermute | solution.py:316
  29.7 14.5 %collective-permute-start.12 = (bf16[4,2,128,128]{3,2,1,0:T(8,128)(2,1)S(1)}, bf16[4,2,128,128]{3,2,1,0:T(8,128)(2,1)S(1)}, u32[]{:S(2)}, u32[]{:S(2)}) collective-permute-start(bf16[4,2,128,128]{3,2,1,0:T(8,128)(2,1)S(1)} %get-tuple-element.76.refs_6_), channel_id=1, source_target_pairs={{0,4},{2,6},{4,0},{6,2},{8,12},{10,14},{12,8},{14,10},{16,20},{18,... | collective-permute-start | bytes 786440 | tf_op jit(solution)/shard_map/ppermute | solution.py:316
  39.3 5.0 %collective-permute-start.13 = (bf16[512,128]{1,0:T(8,128)(2,1)S(1)}, bf16[512,128]{1,0:T(8,128)(2,1)S(1)}, u32[]{:S(2)}, u32[]{:S(2)}) collective-permute-start(bf16[512,128]{1,0:T(8,128)(2,1)S(1)} %finish.2.refs_0_), channel_id=1, source_target_pairs={{0,2},{2,0},{4,6},{6,4},{8,10},{10,8},{12,14},{14,12},{16,18},{18,... | collective-permute-start | bytes 393224 | tf_op jit(solution)/shard_map/ppermute | solution.py:316
  40.8 7.9 %collective-permute-start.15 = (bf16[512,128]{1,0:T(8,128)(2,1)S(1)}, bf16[512,128]{1,0:T(8,128)(2,1)S(1)}, u32[]{:S(2)}, u32[]{:S(2)}) collective-permute-start(bf16[512,128]{1,0:T(8,128)(2,1)S(1)} %finish.2.refs_0_), channel_id=1, source_target_pairs={{0,8},{2,10},{4,12},{6,14},{8,0},{10,2},{12,4},{14,6},{16,24},{18,... | collective-permute-start | bytes 393224 | tf_op jit(solution)/shard_map/ppermute | solution.py:316
  40.8 9.5 %collective-permute-start.10 = (bf16[512,128]{1,0:T(8,128)(2,1)S(1)}, bf16[512,128]{1,0:T(8,128)(2,1)S(1)}, u32[]{:S(2)}, u32[]{:S(2)}) collective-permute-start(bf16[512,128]{1,0:T(8,128)(2,1)S(1)} %finish.2.refs_0_), channel_id=1, source_target_pairs={{0,10},{2,8},{4,14},{6,12},{8,2},{10,0},{12,6},{14,4},{16,26},{18,... | collective-permute-start | bytes 393224 | tf_op jit(solution)/shard_map/ppermute | solution.py:316
  44.4 5.9 %collective-permute-start.14 = (bf16[2,2,128,128]{3,2,1,0:T(8,128)(2,1)S(1)}, bf16[2,2,128,128]{3,2,1,0:T(8,128)(2,1)S(1)}, u32[]{:S(2)}, u32[]{:S(2)}) collective-permute-start(bf16[2,2,128,128]{3,2,1,0:T(8,128)(2,1)S(1)} %get-tuple-element.89.refs_8_), channel_id=1, source_target_pairs={{0,4},{2,6},{4,0},{6,2},{8,12},{10,14},{12,8},{14,10},{16,20},{18,... | collective-permute-start | bytes 393224 | tf_op jit(solution)/shard_map/ppermute | solution.py:316
  50.7 2.7 %collective-permute-start.16 = (bf16[512,1024]{1,0:T(8,128)(2,1)S(1)}, bf16[512,1024]{1,0:T(8,128)(2,1)S(1)}, u32[]{:S(2)}, u32[]{:S(2)}) collective-permute-start(bf16[512,1024]{1,0:T(8,128)(2,1)S(1)} %term.3.refs_0_), channel_id=1, source_target_pairs={{0,1},{1,0},{2,3},{3,2},{4,5},{5,4},{6,7},{7,6},{8,9},{9,8},{10,11... | collective-permute-start | bytes 3145736 | tf_op jit(solution)/shard_map/ppermute | solution.py:334
  50.8 5.9 %collective-permute-start.17 = (bf16[2,2,128,128]{3,2,1,0:T(8,128)(2,1)S(1)}, bf16[2,2,128,128]{3,2,1,0:T(8,128)(2,1)S(1)}, u32[]{:S(2)}, u32[]{:S(2)}) collective-permute-start(bf16[2,2,128,128]{3,2,1,0:T(8,128)(2,1)S(1)} %get-tuple-element.90.refs_9_), channel_id=1, source_target_pairs={{0,4},{2,6},{4,0},{6,2},{8,12},{10,14},{12,8},{14,10},{16,20},{18,... | collective-permute-start | bytes 393224 | tf_op jit(solution)/shard_map/ppermute | solution.py:316
  57.9 4.3 %collective-permute-start.18 = (bf16[128,128]{1,0:T(8,128)(2,1)S(1)}, bf16[128,128]{1,0:T(8,128)(2,1)S(1)}, u32[]{:S(2)}, u32[]{:S(2)}) collective-permute-start(bf16[128,128]{1,0:T(8,128)(2,1)S(1)} %get-tuple-element.96), channel_id=1, source_target_pairs={{0,2},{2,0},{4,6},{6,4},{8,10},{10,8},{12,14},{14,12},{16,18},{18,... | collective-permute-start | bytes 98312 | tf_op jit(solution)/shard_map/ppermute | solution.py:316
  58.9 3.9 %collective-permute-start.19 = (bf16[128,128]{1,0:T(8,128)(2,1)S(1)}, bf16[128,128]{1,0:T(8,128)(2,1)S(1)}, u32[]{:S(2)}, u32[]{:S(2)}) collective-permute-start(bf16[128,128]{1,0:T(8,128)(2,1)S(1)} %get-tuple-element.97), channel_id=1, source_target_pairs={{0,8},{2,10},{4,12},{6,14},{8,0},{10,2},{12,4},{14,6},{16,24},{18,... | collective-permute-start | bytes 98312 | tf_op jit(solution)/shard_map/ppermute | solution.py:316
  58.9 4.8 %collective-permute-start.20 = (bf16[128,128]{1,0:T(8,128)(2,1)S(1)}, bf16[128,128]{1,0:T(8,128)(2,1)S(1)}, u32[]{:S(2)}, u32[]{:S(2)}) collective-permute-start(bf16[128,128]{1,0:T(8,128)(2,1)S(1)} %get-tuple-element.98), channel_id=1, source_target_pairs={{0,10},{2,8},{4,14},{6,12},{8,2},{10,0},{12,6},{14,4},{16,26},{18,... | collective-permute-start | bytes 98312 | tf_op jit(solution)/shard_map/ppermute | solution.py:316
  64.1 1.4 %collective-permute-start.21 = (bf16[64,1024]{1,0:T(8,128)(2,1)S(1)}, bf16[64,1024]{1,0:T(8,128)(2,1)S(1)}, u32[]{:S(2)}, u32[]{:S(2)}) collective-permute-start(bf16[64,1024]{1,0:T(8,128)(2,1)S(1)} %get-tuple-element.100), channel_id=1, source_target_pairs={{0,1},{1,0},{2,3},{3,2},{4,5},{5,4},{6,7},{7,6},{8,9},{9,8},{10,11... | collective-permute-start | bytes 393224 | tf_op jit(solution)/shard_map/ppermute | solution.py:334
  (5 other events, 60.6 us)

commit v4 on v3

--- a/solution.py
+++ b/solution.py
@@ -70,11 +70,12 @@
         copy.start()
     for at, copy in enumerate(copies):
         copy.wait()
+        by_head = jnp.swapaxes(held[at], 0, 1)
         for head in range(held.shape[2]):
 
             @pl.when(spot == head)
-            def _(at=at, head=head):
-                o_ref[at * rows : (at + 1) * rows] = held[at, :, head, :]
+            def _(at=at, head=head, by_head=by_head):
+                o_ref[at * rows : (at + 1) * rows] = by_head[head]
 
 
 def project(x_ref, w_ref, q_ref, gate_ref, own_ref, score_scale):
@@ -315,8 +316,12 @@
     def swap(value, mask):
         return lax.ppermute(value, "users", [(u, u ^ mask) for u in range(chips)])
 
-    def trade_spots(values):
-        return [values[0]] + [swap(values[m], mask_of(m, spot_bits)) for m in range(1, spots)]
+    def trade_spots(values, diagonal_first=True):
+        steps = range(1, spots)
+        moved = {0: values[0]}
+        for m in reversed(steps) if diagonal_first else steps:
+            moved[m] = swap(values[m], mask_of(m, spot_bits))
+        return [moved[m] for m in range(spots)]
 
     def gather_spots(value):
         found = [value]
@@ -468,7 +473,7 @@
             [SMEM_SPEC] * 3 + [VMEM_SPEC] * (len(operands) - 3),
         )
         if not last:
-            gated = trade_spots(list(gated) * spots)
+            gated = trade_spots(list(gated) * spots, False)
             next_weight = pick_head(layer_index + 1)
             if crossed:
                 whole = after(later[layer_index], far, near)

time: 66.4 us -> 66.4 us (level)
  Pallas kernels: 17.5 us -> 15.3 us
  waiting for transfers between devices: 23.7 us -> 25.9 us
    ppermute x19, waiting for transfers between devices: 20.7 us -> 22.9 us  [swap(): return lax.ppermute(value, 'users', [(u, u ^ mask) for u in range(chips)])]
    pallas_call x16, Pallas kernels: 17.5 us -> 15.3 us  [kernel_call(): pl.pallas_call(kernel, out_shape=[jax.ShapeDtypeStruct(*out) for out in o...]
  transfers between devices with their start and end apart: 22 -> 22, of which waited for: 15 -> 15; matrix products, arithmetic and copies ran while one was open for 0% -> 0% of each run, Pallas kernels for 22% -> 18%
where the time goes in v4:
time: 66.4 us; the launch traced here: 66.2 us
  waiting for transfers between devices  25.9 us (39%)
  starting transfers between devices  23.7 us (36%)
  Pallas kernels  15.3 us (23%)
  local copies, waits for them, and re-layouts  1.08 us (2%)
    ppermute x19, starting transfers between devices, swap(): return lax.ppermute(value, 'users', [(u, u ^ mask) for u in range(chips)])  23.5 us
    ppermute x19, waiting for transfers between devices, swap(): return lax.ppermute(value, 'users', [(u, u ^ mask) for u in range(chips)])  22.9 us
    pallas_call x16, Pallas kernels, kernel_call(): pl.pallas_call(kernel, out_shape=[jax.ShapeDtypeStruct(*out) for out in o...  15.3 us
    ppermute x3, waiting for transfers between devices, shift_core(): return lax.ppermute(value, 'cand', pairs)  2.98 us
  transfers between devices with their start and end apart: 22, of which 15 were waited for; matrix products, arithmetic and copies ran while one was open for 0% of the time, Pallas kernels for 18%

profile of v4, /device:TPU:0, one launch (start us, length us, event | category | flops | bytes accessed | tf_op | source)
XLA Modules:
  0.0 66.2 jit_solution(7653423659553769432)
XLA Ops:
  1.5 3.0 %collective-permute-start = (bf16[2,2,128,128]{3,2,1,0:T(8,128)(2,1)S(1)}, bf16[2,2,128,128]{3,2,1,0:T(8,128)(2,1)S(1)}, u32[]{:S(2)}, u32[]{:S(2)}) collective-permute-start(bf16[2,2,128,128]{3,2,1,0:T(8,128)(2,1)S(1)} %get-tuple-element.54), channel_id=1, source_target_pairs={{0,2},{2,0},{4,6},{6,4},{8,10},{10,8},{12,14},{14,12},{16,18},{18,... | collective-permute-start | bytes 393224 | tf_op jit(solution)/shard_map/ppermute | solution.py:317
  4.5 1.6 %collective-permute-start.1 = (bf16[2,2,128,128]{3,2,1,0:T(8,128)(2,1)S(1)}, bf16[2,2,128,128]{3,2,1,0:T(8,128)(2,1)S(1)}, u32[]{:S(2)}, u32[]{:S(2)}) collective-permute-start(bf16[2,2,128,128]{3,2,1,0:T(8,128)(2,1)S(1)} %get-tuple-element.55), channel_id=1, source_target_pairs={{0,8},{2,10},{4,12},{6,14},{8,0},{10,2},{12,4},{14,6},{16,24},{18,... | collective-permute-start | bytes 393224 | tf_op jit(solution)/shard_map/ppermute | solution.py:317
  6.1 2.3 %pick_head.2.refs_5_ = bf16[1024,512]{1,0:T(8,128)(2,1)S(1)} custom-call(bf16[2,1024,4,512]{3,2,1,0:T(4,128)(2,1)} %w_ref.3), custom_call_target="tpu_custom_call" | custom-call | tf_op jit(solution)/shard_map/pick_head/pallas_call | solution.py:358
  8.5 2.4 %collective-permute-done.1.refs_2_ = bf16[2,2,128,128]{3,2,1,0:T(8,128)(2,1)S(1)} collective-permute-done((bf16[2,2,128,128]{3,2,1,0:T(8,128)(2,1)S(1)}, bf16[2,2,128,128]{3,2,1,0:T(8,128)(2,1)S(1)}, u32[]{:S(2)}, u32[]{:S(2)}) %collective-permute-start.1) | collective-permute-done | bytes 131104 | tf_op jit(solution)/shard_map/ppermute | solution.py:317
  12.1 2.8 %collective-permute-start.3 = (bf16[4,2,128,128]{3,2,1,0:T(8,128)(2,1)S(1)}, bf16[4,2,128,128]{3,2,1,0:T(8,128)(2,1)S(1)}, u32[]{:S(2)}, u32[]{:S(2)}) collective-permute-start(bf16[4,2,128,128]{3,2,1,0:T(8,128)(2,1)S(1)} %get-tuple-element.61.refs_6_), channel_id=1, source_target_pairs={{0,16},{2,18},{4,20},{6,22},{8,24},{10,26},{12,28},{14,30},{16,0},... | collective-permute-start | bytes 786440 | tf_op jit(solution)/shard_map/ppermute | solution.py:317
  14.9 1.5 %collective-permute-start.4 = (bf16[4,2,128,128]{3,2,1,0:T(8,128)(2,1)S(1)}, bf16[4,2,128,128]{3,2,1,0:T(8,128)(2,1)S(1)}, u32[]{:S(2)}, u32[]{:S(2)}) collective-permute-start(bf16[4,2,128,128]{3,2,1,0:T(8,128)(2,1)S(1)} %get-tuple-element.61.refs_6_), channel_id=1, source_target_pairs={{0,4},{2,6},{4,0},{6,2},{8,12},{10,14},{12,8},{14,10},{16,20},{18,... | collective-permute-start | bytes 786440 | tf_op jit(solution)/shard_map/ppermute | solution.py:317
  16.5 1.5 %collective-permute-start.5 = (bf16[64,1024]{1,0:T(8,128)(2,1)S(1)}, bf16[64,1024]{1,0:T(8,128)(2,1)S(1)}, u32[]{:S(2)}, u32[]{:S(2)}) collective-permute-start(bf16[64,1024]{1,0:T(8,128)(2,1)S(1)} %copy-done.2), channel_id=1, source_target_pairs={{0,2},{2,0},{4,6},{6,4},{8,10},{10,8},{12,14},{14,12},{16,18},{18,... | collective-permute-start | bytes 393224 | tf_op jit(solution)/shard_map/ppermute | solution.py:317
  17.9 1.6 %collective-permute-start.6 = (bf16[64,1024]{1,0:T(8,128)(2,1)S(1)}, bf16[64,1024]{1,0:T(8,128)(2,1)S(1)}, u32[]{:S(2)}, u32[]{:S(2)}) collective-permute-start(bf16[64,1024]{1,0:T(8,128)(2,1)S(1)} %copy-done.2), channel_id=1, source_target_pairs={{0,8},{2,10},{4,12},{6,14},{8,0},{10,2},{12,4},{14,6},{16,24},{18,... | collective-permute-start | bytes 393224 | tf_op jit(solution)/shard_map/ppermute | solution.py:317
  20.0 2.0 %collective-permute-done.5.refs_1_ = bf16[64,1024]{1,0:T(8,128)(2,1)S(1)} collective-permute-done((bf16[64,1024]{1,0:T(8,128)(2,1)S(1)}, bf16[64,1024]{1,0:T(8,128)(2,1)S(1)}, u32[]{:S(2)}, u32[]{:S(2)}) %collective-permute-start.5) | collective-permute-done | bytes 131104 | tf_op jit(solution)/shard_map/ppermute | solution.py:317
  21.9 5.4 %collective-permute-done.6.refs_2_ = bf16[64,1024]{1,0:T(8,128)(2,1)S(1)} collective-permute-done((bf16[64,1024]{1,0:T(8,128)(2,1)S(1)}, bf16[64,1024]{1,0:T(8,128)(2,1)S(1)}, u32[]{:S(2)}, u32[]{:S(2)}) %collective-permute-start.6) | collective-permute-done | bytes 131104 | tf_op jit(solution)/shard_map/ppermute | solution.py:317
  27.3 1.4 %collective-permute-done.7.refs_3_ = bf16[64,1024]{1,0:T(8,128)(2,1)S(1)} collective-permute-done((bf16[64,1024]{1,0:T(8,128)(2,1)S(1)}, bf16[64,1024]{1,0:T(8,128)(2,1)S(1)}, u32[]{:S(2)}, u32[]{:S(2)}) %collective-permute-start.7) | collective-permute-done | bytes 131104 | tf_op jit(solution)/shard_map/ppermute | solution.py:317
  29.7 1.3 %collective-permute-start.12 = (bf16[4,2,128,128]{3,2,1,0:T(8,128)(2,1)S(1)}, bf16[4,2,128,128]{3,2,1,0:T(8,128)(2,1)S(1)}, u32[]{:S(2)}, u32[]{:S(2)}) collective-permute-start(bf16[4,2,128,128]{3,2,1,0:T(8,128)(2,1)S(1)} %get-tuple-element.76.refs_6_), channel_id=1, source_target_pairs={{0,4},{2,6},{4,0},{6,2},{8,12},{10,14},{12,8},{14,10},{16,20},{18,... | collective-permute-start | bytes 786440 | tf_op jit(solution)/shard_map/ppermute | solution.py:317
  32.0 1.7 %attend.2 = (bf16[512,256]{1,0:T(8,128)(2,1)S(1)}, f32[512,128]{1,0:T(8,128)S(1)}) custom-call(s32[16]{0:T(128)S(1)} %copy-done.3, s32[16]{0:T(128)S(1)} %copy-done.4, s32[4]{0:T(128)S(1)} %copy-done.5, s32[4]{0:T(128)S(1)} %copy-done.6, bf16[512,128]{1,0:T(8,128)(2,1)S(1)} %get-tuple-element.68.refs_4_, f32[512,128]{1,0:T(8,128)S(1)} %get-tuple-element.69.refs_5_, ...), custom_call_target="tpu_custom_call" | custom-call | tf_op jit(solution)/shard_map/attend/pallas_call | solution.py:358
  33.7 4.3 %collective-permute-done.9.refs_6_ = bf16[4,2,128,128]{3,2,1,0:T(8,128)(2,1)S(1)} collective-permute-done((bf16[4,2,128,128]{3,2,1,0:T(8,128)(2,1)S(1)}, bf16[4,2,128,128]{3,2,1,0:T(8,128)(2,1)S(1)}, u32[]{:S(2)}, u32[]{:S(2)}) %collective-permute-start.9) | collective-permute-done | bytes 262176 | tf_op jit(solution)/shard_map/ppermute | solution.py:317
  38.0 1.3 %finish.2.refs_0_ = bf16[512,128]{1,0:T(8,128)(2,1)S(1)} custom-call(s32[16]{0:T(128)S(1)} %copy-done.3, s32[16]{0:T(128)S(1)} %copy-done.4, s32[4]{0:T(128)S(1)} %copy-done.5, bf16[512,256]{1,0:T(8,128)(2,1)S(1)} %get-tuple-element.72.refs_3_, f32[512,128]{1,0:T(8,128)S(1)} %get-tuple-element.73.refs_4_, bf16[512,128]{1,0:T(8,128)(2,1)S(1)} %get-tuple-element.74.refs_5_, ...), custom_call_target="tpu_custom_call" | custom-call | tf_op jit(solution)/shard_map/finish/pallas_call | solution.py:358
  39.3 1.5 %collective-permute-start.13 = (bf16[512,128]{1,0:T(8,128)(2,1)S(1)}, bf16[512,128]{1,0:T(8,128)(2,1)S(1)}, u32[]{:S(2)}, u32[]{:S(2)}) collective-permute-start(bf16[512,128]{1,0:T(8,128)(2,1)S(1)} %finish.2.refs_0_), channel_id=1, source_target_pairs={{0,2},{2,0},{4,6},{6,4},{8,10},{10,8},{12,14},{14,12},{16,18},{18,... | collective-permute-start | bytes 393224 | tf_op jit(solution)/shard_map/ppermute | solution.py:317
  40.8 2.0 %collective-permute-start.10 = (bf16[512,128]{1,0:T(8,128)(2,1)S(1)}, bf16[512,128]{1,0:T(8,128)(2,1)S(1)}, u32[]{:S(2)}, u32[]{:S(2)}) collective-permute-start(bf16[512,128]{1,0:T(8,128)(2,1)S(1)} %finish.2.refs_0_), channel_id=1, source_target_pairs={{0,10},{2,8},{4,14},{6,12},{8,2},{10,0},{12,6},{14,4},{16,26},{18,... | collective-permute-start | bytes 393224 | tf_op jit(solution)/shard_map/ppermute | solution.py:317
  42.9 1.3 %collective-permute-done.11.i_ref = bf16[4,2,128,128]{3,2,1,0:T(8,128)(2,1)S(1)} collective-permute-done((bf16[4,2,128,128]{3,2,1,0:T(8,128)(2,1)S(1)}, bf16[4,2,128,128]{3,2,1,0:T(8,128)(2,1)S(1)}, u32[]{:S(2)}, u32[]{:S(2)}) %collective-permute-start.11) | collective-permute-done | bytes 262176 | tf_op jit(solution)/shard_map/ppermute | solution.py:317
  45.3 2.3 %pick_head.3.refs_3_ = bf16[1024,512]{1,0:T(8,128)(2,1)S(1)} custom-call(bf16[2,1024,4,512]{3,2,1,0:T(4,128)(2,1)} %w_ref.3), custom_call_target="tpu_custom_call" | custom-call | tf_op jit(solution)/shard_map/pick_head/pallas_call | solution.py:358
  48.3 2.0 %collective-permute-done.10.refs_0_ = bf16[512,128]{1,0:T(8,128)(2,1)S(1)} collective-permute-done((bf16[512,128]{1,0:T(8,128)(2,1)S(1)}, bf16[512,128]{1,0:T(8,128)(2,1)S(1)}, u32[]{:S(2)}, u32[]{:S(2)}) %collective-permute-start.10) | collective-permute-done | bytes 131104 | tf_op jit(solution)/shard_map/ppermute | solution.py:317
  51.8 1.6 %collective-permute-done.16.refs_1_ = bf16[512,1024]{1,0:T(8,128)(2,1)S(1)} collective-permute-done((bf16[512,1024]{1,0:T(8,128)(2,1)S(1)}, bf16[512,1024]{1,0:T(8,128)(2,1)S(1)}, u32[]{:S(2)}, u32[]{:S(2)}) %collective-permute-start.16) | collective-permute-done | bytes 1048608 | tf_op jit(solution)/shard_map/ppermute | solution.py:339
  54.4 1.8 %attend.3 = (bf16[512,256]{1,0:T(8,128)(2,1)S(1)}, f32[512,128]{1,0:T(8,128)S(1)}) custom-call(s32[16]{0:T(128)S(1)} %copy-done.3, s32[16]{0:T(128)S(1)} %copy-done.4, s32[4]{0:T(128)S(1)} %copy-done.5, s32[4]{0:T(128)S(1)} %copy-done.6, bf16[512,128]{1,0:T(8,128)(2,1)S(1)} %get-tuple-element.87.refs_4_, f32[512,128]{1,0:T(8,128)S(1)} %get-tuple-element.88.refs_5_, ...), custom_call_target="tpu_custom_call" | custom-call | tf_op jit(solution)/shard_map/attend/pallas_call | solution.py:358
  58.9 2.6 %collective-permute-start.20 = (bf16[128,128]{1,0:T(8,128)(2,1)S(1)}, bf16[128,128]{1,0:T(8,128)(2,1)S(1)}, u32[]{:S(2)}, u32[]{:S(2)}) collective-permute-start(bf16[128,128]{1,0:T(8,128)(2,1)S(1)} %get-tuple-element.98), channel_id=1, source_target_pairs={{0,10},{2,8},{4,14},{6,12},{8,2},{10,0},{12,6},{14,4},{16,26},{18,... | collective-permute-start | bytes 98312 | tf_op jit(solution)/shard_map/ppermute | solution.py:317
  64.2 1.3 %collective-permute-done.21.refs_2_ = bf16[64,1024]{1,0:T(8,128)(2,1)S(1)} collective-permute-done((bf16[64,1024]{1,0:T(8,128)(2,1)S(1)}, bf16[64,1024]{1,0:T(8,128)(2,1)S(1)}, u32[]{:S(2)}, u32[]{:S(2)}) %collective-permute-start.21) | collective-permute-done | bytes 131104 | tf_op jit(solution)/shard_map/ppermute | solution.py:339
  (50 shorter events, 15.3 us)
Async XLA Ops:
  1.5 7.0 %collective-permute-start = (bf16[2,2,128,128]{3,2,1,0:T(8,128)(2,1)S(1)}, bf16[2,2,128,128]{3,2,1,0:T(8,128)(2,1)S(1)}, u32[]{:S(2)}, u32[]{:S(2)}) collective-permute-start(bf16[2,2,128,128]{3,2,1,0:T(8,128)(2,1)S(1)} %get-tuple-element.54), channel_id=1, source_target_pairs={{0,2},{2,0},{4,6},{6,4},{8,10},{10,8},{12,14},{14,12},{16,18},{18,... | collective-permute-start | bytes 393224 | tf_op jit(solution)/shard_map/ppermute | solution.py:317
  4.5 6.4 %collective-permute-start.1 = (bf16[2,2,128,128]{3,2,1,0:T(8,128)(2,1)S(1)}, bf16[2,2,128,128]{3,2,1,0:T(8,128)(2,1)S(1)}, u32[]{:S(2)}, u32[]{:S(2)}) collective-permute-start(bf16[2,2,128,128]{3,2,1,0:T(8,128)(2,1)S(1)} %get-tuple-element.55), channel_id=1, source_target_pairs={{0,8},{2,10},{4,12},{6,14},{8,0},{10,2},{12,4},{14,6},{16,24},{18,... | collective-permute-start | bytes 393224 | tf_op jit(solution)/shard_map/ppermute | solution.py:317
  6.1 6.0 %collective-permute-start.2 = (bf16[2,2,128,128]{3,2,1,0:T(8,128)(2,1)S(1)}, bf16[2,2,128,128]{3,2,1,0:T(8,128)(2,1)S(1)}, u32[]{:S(2)}, u32[]{:S(2)}) collective-permute-start(bf16[2,2,128,128]{3,2,1,0:T(8,128)(2,1)S(1)} %get-tuple-element.56), channel_id=1, source_target_pairs={{0,10},{2,8},{4,14},{6,12},{8,2},{10,0},{12,6},{14,4},{16,26},{18,... | collective-permute-start | bytes 393224 | tf_op jit(solution)/shard_map/ppermute | solution.py:317
  8.4 23.5 %copy-start.3 = (s32[16]{0:T(128)S(1)}, s32[16]{0:T(128)}, u32[]{:S(2)}) copy-start(s32[16]{0:T(128)} %refs_0_.9) | copy-start | bytes 196
  8.4 23.5 %copy-start.4 = (s32[16]{0:T(128)S(1)}, s32[16]{0:T(128)}, u32[]{:S(2)}) copy-start(s32[16]{0:T(128)} %refs_1_.9) | copy-start | bytes 196
  12.1 16.6 %collective-permute-start.3 = (bf16[4,2,128,128]{3,2,1,0:T(8,128)(2,1)S(1)}, bf16[4,2,128,128]{3,2,1,0:T(8,128)(2,1)S(1)}, u32[]{:S(2)}, u32[]{:S(2)}) collective-permute-start(bf16[4,2,128,128]{3,2,1,0:T(8,128)(2,1)S(1)} %get-tuple-element.61.refs_6_), channel_id=1, source_target_pairs={{0,16},{2,18},{4,20},{6,22},{8,24},{10,26},{12,28},{14,30},{16,0},... | collective-permute-start | bytes 786440 | tf_op jit(solution)/shard_map/ppermute | solution.py:317
  14.9 13.8 %collective-permute-start.4 = (bf16[4,2,128,128]{3,2,1,0:T(8,128)(2,1)S(1)}, bf16[4,2,128,128]{3,2,1,0:T(8,128)(2,1)S(1)}, u32[]{:S(2)}, u32[]{:S(2)}) collective-permute-start(bf16[4,2,128,128]{3,2,1,0:T(8,128)(2,1)S(1)} %get-tuple-element.61.refs_6_), channel_id=1, source_target_pairs={{0,4},{2,6},{4,0},{6,2},{8,12},{10,14},{12,8},{14,10},{16,20},{18,... | collective-permute-start | bytes 786440 | tf_op jit(solution)/shard_map/ppermute | solution.py:317
  16.5 5.5 %collective-permute-start.5 = (bf16[64,1024]{1,0:T(8,128)(2,1)S(1)}, bf16[64,1024]{1,0:T(8,128)(2,1)S(1)}, u32[]{:S(2)}, u32[]{:S(2)}) collective-permute-start(bf16[64,1024]{1,0:T(8,128)(2,1)S(1)} %copy-done.2), channel_id=1, source_target_pairs={{0,2},{2,0},{4,6},{6,4},{8,10},{10,8},{12,14},{14,12},{16,18},{18,... | collective-permute-start | bytes 393224 | tf_op jit(solution)/shard_map/ppermute | solution.py:317
  17.9 9.4 %collective-permute-start.6 = (bf16[64,1024]{1,0:T(8,128)(2,1)S(1)}, bf16[64,1024]{1,0:T(8,128)(2,1)S(1)}, u32[]{:S(2)}, u32[]{:S(2)}) collective-permute-start(bf16[64,1024]{1,0:T(8,128)(2,1)S(1)} %copy-done.2), channel_id=1, source_target_pairs={{0,8},{2,10},{4,12},{6,14},{8,0},{10,2},{12,4},{14,6},{16,24},{18,... | collective-permute-start | bytes 393224 | tf_op jit(solution)/shard_map/ppermute | solution.py:317
  19.5 9.2 %collective-permute-start.7 = (bf16[64,1024]{1,0:T(8,128)(2,1)S(1)}, bf16[64,1024]{1,0:T(8,128)(2,1)S(1)}, u32[]{:S(2)}, u32[]{:S(2)}) collective-permute-start(bf16[64,1024]{1,0:T(8,128)(2,1)S(1)} %copy-done.2), channel_id=1, source_target_pairs={{0,10},{2,8},{4,14},{6,12},{8,2},{10,0},{12,6},{14,4},{16,26},{18,... | collective-permute-start | bytes 393224 | tf_op jit(solution)/shard_map/ppermute | solution.py:317
  28.8 2.2 %collective-permute-start.8 = (bf16[4,64,1024]{2,1,0:T(8,128)(2,1)S(1)}, bf16[4,64,1024]{2,1,0:T(8,128)(2,1)S(1)}, u32[]{:S(2)}, u32[]{:S(2)}) collective-permute-start(bf16[4,64,1024]{2,1,0:T(8,128)(2,1)S(1)} %join.1), channel_id=1, source_target_pairs={{0,1},{1,0},{2,3},{3,2},{4,5},{5,4},{6,7},{7,6},{8,9},{9,8},{10,11... | collective-permute-start | bytes 1572872 | tf_op jit(solution)/shard_map/ppermute | solution.py:339
  28.9 9.2 %collective-permute-start.9 = (bf16[4,2,128,128]{3,2,1,0:T(8,128)(2,1)S(1)}, bf16[4,2,128,128]{3,2,1,0:T(8,128)(2,1)S(1)}, u32[]{:S(2)}, u32[]{:S(2)}) collective-permute-start(bf16[4,2,128,128]{3,2,1,0:T(8,128)(2,1)S(1)} %collective-permute-done.3.refs_8_), channel_id=1, source_target_pairs={{0,4},{2,6},{4,0},{6,2},{8,12},{10,14},{12,8},{14,10},{16,20},{18,... | collective-permute-start | bytes 786440 | tf_op jit(solution)/shard_map/ppermute | solution.py:317
  29.7 14.6 %collective-permute-start.11 = (bf16[4,2,128,128]{3,2,1,0:T(8,128)(2,1)S(1)}, bf16[4,2,128,128]{3,2,1,0:T(8,128)(2,1)S(1)}, u32[]{:S(2)}, u32[]{:S(2)}) collective-permute-start(bf16[4,2,128,128]{3,2,1,0:T(8,128)(2,1)S(1)} %get-tuple-element.76.refs_6_), channel_id=1, source_target_pairs={{0,16},{2,18},{4,20},{6,22},{8,24},{10,26},{12,28},{14,30},{16,0},... | collective-permute-start | bytes 786440 | tf_op jit(solution)/shard_map/ppermute | solution.py:317
  29.7 14.5 %collective-permute-start.12 = (bf16[4,2,128,128]{3,2,1,0:T(8,128)(2,1)S(1)}, bf16[4,2,128,128]{3,2,1,0:T(8,128)(2,1)S(1)}, u32[]{:S(2)}, u32[]{:S(2)}) collective-permute-start(bf16[4,2,128,128]{3,2,1,0:T(8,128)(2,1)S(1)} %get-tuple-element.76.refs_6_), channel_id=1, source_target_pairs={{0,4},{2,6},{4,0},{6,2},{8,12},{10,14},{12,8},{14,10},{16,20},{18,... | collective-permute-start | bytes 786440 | tf_op jit(solution)/shard_map/ppermute | solution.py:317
  39.3 5.0 %collective-permute-start.13 = (bf16[512,128]{1,0:T(8,128)(2,1)S(1)}, bf16[512,128]{1,0:T(8,128)(2,1)S(1)}, u32[]{:S(2)}, u32[]{:S(2)}) collective-permute-start(bf16[512,128]{1,0:T(8,128)(2,1)S(1)} %finish.2.refs_0_), channel_id=1, source_target_pairs={{0,2},{2,0},{4,6},{6,4},{8,10},{10,8},{12,14},{14,12},{16,18},{18,... | collective-permute-start | bytes 393224 | tf_op jit(solution)/shard_map/ppermute | solution.py:317
  40.8 6.8 %collective-permute-start.15 = (bf16[512,128]{1,0:T(8,128)(2,1)S(1)}, bf16[512,128]{1,0:T(8,128)(2,1)S(1)}, u32[]{:S(2)}, u32[]{:S(2)}) collective-permute-start(bf16[512,128]{1,0:T(8,128)(2,1)S(1)} %finish.2.refs_0_), channel_id=1, source_target_pairs={{0,8},{2,10},{4,12},{6,14},{8,0},{10,2},{12,4},{14,6},{16,24},{18,... | collective-permute-start | bytes 393224 | tf_op jit(solution)/shard_map/ppermute | solution.py:317
  40.8 9.5 %collective-permute-start.10 = (bf16[512,128]{1,0:T(8,128)(2,1)S(1)}, bf16[512,128]{1,0:T(8,128)(2,1)S(1)}, u32[]{:S(2)}, u32[]{:S(2)}) collective-permute-start(bf16[512,128]{1,0:T(8,128)(2,1)S(1)} %finish.2.refs_0_), channel_id=1, source_target_pairs={{0,10},{2,8},{4,14},{6,12},{8,2},{10,0},{12,6},{14,4},{16,26},{18,... | collective-permute-start | bytes 393224 | tf_op jit(solution)/shard_map/ppermute | solution.py:317
  44.4 5.9 %collective-permute-start.14 = (bf16[2,2,128,128]{3,2,1,0:T(8,128)(2,1)S(1)}, bf16[2,2,128,128]{3,2,1,0:T(8,128)(2,1)S(1)}, u32[]{:S(2)}, u32[]{:S(2)}) collective-permute-start(bf16[2,2,128,128]{3,2,1,0:T(8,128)(2,1)S(1)} %get-tuple-element.89.refs_8_), channel_id=1, source_target_pairs={{0,4},{2,6},{4,0},{6,2},{8,12},{10,14},{12,8},{14,10},{16,20},{18,... | collective-permute-start | bytes 393224 | tf_op jit(solution)/shard_map/ppermute | solution.py:317
  50.7 2.7 %collective-permute-start.16 = (bf16[512,1024]{1,0:T(8,128)(2,1)S(1)}, bf16[512,1024]{1,0:T(8,128)(2,1)S(1)}, u32[]{:S(2)}, u32[]{:S(2)}) collective-permute-start(bf16[512,1024]{1,0:T(8,128)(2,1)S(1)} %term.3.refs_0_), channel_id=1, source_target_pairs={{0,1},{1,0},{2,3},{3,2},{4,5},{5,4},{6,7},{7,6},{8,9},{9,8},{10,11... | collective-permute-start | bytes 3145736 | tf_op jit(solution)/shard_map/ppermute | solution.py:339
  50.8 5.9 %collective-permute-start.17 = (bf16[2,2,128,128]{3,2,1,0:T(8,128)(2,1)S(1)}, bf16[2,2,128,128]{3,2,1,0:T(8,128)(2,1)S(1)}, u32[]{:S(2)}, u32[]{:S(2)}) collective-permute-start(bf16[2,2,128,128]{3,2,1,0:T(8,128)(2,1)S(1)} %get-tuple-element.90.refs_9_), channel_id=1, source_target_pairs={{0,4},{2,6},{4,0},{6,2},{8,12},{10,14},{12,8},{14,10},{16,20},{18,... | collective-permute-start | bytes 393224 | tf_op jit(solution)/shard_map/ppermute | solution.py:317
  57.9 4.3 %collective-permute-start.18 = (bf16[128,128]{1,0:T(8,128)(2,1)S(1)}, bf16[128,128]{1,0:T(8,128)(2,1)S(1)}, u32[]{:S(2)}, u32[]{:S(2)}) collective-permute-start(bf16[128,128]{1,0:T(8,128)(2,1)S(1)} %get-tuple-element.96), channel_id=1, source_target_pairs={{0,2},{2,0},{4,6},{6,4},{8,10},{10,8},{12,14},{14,12},{16,18},{18,... | collective-permute-start | bytes 98312 | tf_op jit(solution)/shard_map/ppermute | solution.py:317
  58.9 3.9 %collective-permute-start.19 = (bf16[128,128]{1,0:T(8,128)(2,1)S(1)}, bf16[128,128]{1,0:T(8,128)(2,1)S(1)}, u32[]{:S(2)}, u32[]{:S(2)}) collective-permute-start(bf16[128,128]{1,0:T(8,128)(2,1)S(1)} %get-tuple-element.97), channel_id=1, source_target_pairs={{0,8},{2,10},{4,12},{6,14},{8,0},{10,2},{12,4},{14,6},{16,24},{18,... | collective-permute-start | bytes 98312 | tf_op jit(solution)/shard_map/ppermute | solution.py:317
  58.9 4.8 %collective-permute-start.20 = (bf16[128,128]{1,0:T(8,128)(2,1)S(1)}, bf16[128,128]{1,0:T(8,128)(2,1)S(1)}, u32[]{:S(2)}, u32[]{:S(2)}) collective-permute-start(bf16[128,128]{1,0:T(8,128)(2,1)S(1)} %get-tuple-element.98), channel_id=1, source_target_pairs={{0,10},{2,8},{4,14},{6,12},{8,2},{10,0},{12,6},{14,4},{16,26},{18,... | collective-permute-start | bytes 98312 | tf_op jit(solution)/shard_map/ppermute | solution.py:317
  64.1 1.4 %collective-permute-start.21 = (bf16[64,1024]{1,0:T(8,128)(2,1)S(1)}, bf16[64,1024]{1,0:T(8,128)(2,1)S(1)}, u32[]{:S(2)}, u32[]{:S(2)}) collective-permute-start(bf16[64,1024]{1,0:T(8,128)(2,1)S(1)} %get-tuple-element.100), channel_id=1, source_target_pairs={{0,1},{1,0},{2,3},{3,2},{4,5},{5,4},{6,7},{7,6},{8,9},{9,8},{10,11... | collective-permute-start | bytes 393224 | tf_op jit(solution)/shard_map/ppermute | solution.py:339
  (5 other events, 61.7 us)

commit v5 on v4

--- a/solution.py
+++ b/solution.py
@@ -424,8 +424,10 @@
         near_mask, far_mask = member_masks[1:3]
         far = swap(first, far_mask)
         near = swap(first, near_mask)
-        far, near, x_pieces = together(far, near, x_pieces)
-        history = [[first, near, far, swap(far, near_mask)]]
+        far, near = together(far, near)
+        onward = swap(far, near_mask)
+        x_pieces[1:] = [after(piece, far) for piece in x_pieces[1:]]
+        history = [[first, near, far, onward]]
     else:
         history = [gather_members(first)]
     x_group = x_pieces + [shift_core(join(x_pieces), s) for s in range(1, cores)]

time: 66.4 us -> 66 us (level)
  no operation moved by 1% of the time
where the time goes in v5:
time: 66 us; the launch traced here: 65.9 us
  waiting for transfers between devices  26 us (39%)
  starting transfers between devices  23.3 us (35%)
  Pallas kernels  15.3 us (23%)
  local copies, waits for them, and re-layouts  1.08 us (2%)
    ppermute x19, starting transfers between devices, swap(): return lax.ppermute(value, 'users', [(u, u ^ mask) for u in range(chips)])  23.1 us
    ppermute x19, waiting for transfers between devices, swap(): return lax.ppermute(value, 'users', [(u, u ^ mask) for u in range(chips)])  22.8 us
    pallas_call x16, Pallas kernels, kernel_call(): pl.pallas_call(kernel, out_shape=[jax.ShapeDtypeStruct(*out) for out in o...  15.3 us
    ppermute x3, waiting for transfers between devices, shift_core(): return lax.ppermute(value, 'cand', pairs)  3.18 us
  transfers between devices with their start and end apart: 22, of which 15 were waited for; matrix products, arithmetic and copies ran while one was open for 0% of the time, Pallas kernels for 18%

profile of v5, /device:TPU:0, one launch (start us, length us, event | category | flops | bytes accessed | tf_op | source)
XLA Modules:
  0.0 65.9 jit_solution(11130764333574473359)
XLA Ops:
  1.5 3.0 %collective-permute-start = (bf16[2,2,128,128]{3,2,1,0:T(8,128)(2,1)S(1)}, bf16[2,2,128,128]{3,2,1,0:T(8,128)(2,1)S(1)}, u32[]{:S(2)}, u32[]{:S(2)}) collective-permute-start(bf16[2,2,128,128]{3,2,1,0:T(8,128)(2,1)S(1)} %get-tuple-element.53), channel_id=1, source_target_pairs={{0,2},{2,0},{4,6},{6,4},{8,10},{10,8},{12,14},{14,12},{16,18},{18,... | collective-permute-start | bytes 393224 | tf_op jit(solution)/shard_map/ppermute | solution.py:317
  4.5 1.6 %collective-permute-start.1 = (bf16[2,2,128,128]{3,2,1,0:T(8,128)(2,1)S(1)}, bf16[2,2,128,128]{3,2,1,0:T(8,128)(2,1)S(1)}, u32[]{:S(2)}, u32[]{:S(2)}) collective-permute-start(bf16[2,2,128,128]{3,2,1,0:T(8,128)(2,1)S(1)} %get-tuple-element.54), channel_id=1, source_target_pairs={{0,8},{2,10},{4,12},{6,14},{8,0},{10,2},{12,4},{14,6},{16,24},{18,... | collective-permute-start | bytes 393224 | tf_op jit(solution)/shard_map/ppermute | solution.py:317
  6.1 2.3 %pick_head.2.refs_5_ = bf16[1024,512]{1,0:T(8,128)(2,1)S(1)} custom-call(bf16[2,1024,4,512]{3,2,1,0:T(4,128)(2,1)} %w_ref.3), custom_call_target="tpu_custom_call" | custom-call | tf_op jit(solution)/shard_map/pick_head/pallas_call | solution.py:358
  8.5 2.4 %collective-permute-done.1.refs_2_ = bf16[2,2,128,128]{3,2,1,0:T(8,128)(2,1)S(1)} collective-permute-done((bf16[2,2,128,128]{3,2,1,0:T(8,128)(2,1)S(1)}, bf16[2,2,128,128]{3,2,1,0:T(8,128)(2,1)S(1)}, u32[]{:S(2)}, u32[]{:S(2)}) %collective-permute-start.1) | collective-permute-done | bytes 131104 | tf_op jit(solution)/shard_map/ppermute | solution.py:317
  10.9 1.2 %collective-permute-done.2.refs_3_ = bf16[2,2,128,128]{3,2,1,0:T(8,128)(2,1)S(1)} collective-permute-done((bf16[2,2,128,128]{3,2,1,0:T(8,128)(2,1)S(1)}, bf16[2,2,128,128]{3,2,1,0:T(8,128)(2,1)S(1)}, u32[]{:S(2)}, u32[]{:S(2)}) %collective-permute-start.2) | collective-permute-done | bytes 131104 | tf_op jit(solution)/shard_map/ppermute | solution.py:317
  12.1 2.8 %collective-permute-start.4 = (bf16[4,2,128,128]{3,2,1,0:T(8,128)(2,1)S(1)}, bf16[4,2,128,128]{3,2,1,0:T(8,128)(2,1)S(1)}, u32[]{:S(2)}, u32[]{:S(2)}) collective-permute-start(bf16[4,2,128,128]{3,2,1,0:T(8,128)(2,1)S(1)} %get-tuple-element.60.refs_6_), channel_id=1, source_target_pairs={{0,16},{2,18},{4,20},{6,22},{8,24},{10,26},{12,28},{14,30},{16,0},... | collective-permute-start | bytes 786440 | tf_op jit(solution)/shard_map/ppermute | solution.py:317
  14.9 1.5 %collective-permute-start.5 = (bf16[4,2,128,128]{3,2,1,0:T(8,128)(2,1)S(1)}, bf16[4,2,128,128]{3,2,1,0:T(8,128)(2,1)S(1)}, u32[]{:S(2)}, u32[]{:S(2)}) collective-permute-start(bf16[4,2,128,128]{3,2,1,0:T(8,128)(2,1)S(1)} %get-tuple-element.60.refs_6_), channel_id=1, source_target_pairs={{0,4},{2,6},{4,0},{6,2},{8,12},{10,14},{12,8},{14,10},{16,20},{18,... | collective-permute-start | bytes 786440 | tf_op jit(solution)/shard_map/ppermute | solution.py:317
  16.5 2.5 %collective-permute-start.7 = (bf16[64,1024]{1,0:T(8,128)(2,1)S(1)}, bf16[64,1024]{1,0:T(8,128)(2,1)S(1)}, u32[]{:S(2)}, u32[]{:S(2)}) collective-permute-start(bf16[64,1024]{1,0:T(8,128)(2,1)S(1)} %copy-done.2), channel_id=1, source_target_pairs={{0,10},{2,8},{4,14},{6,12},{8,2},{10,0},{12,6},{14,4},{16,26},{18,... | collective-permute-start | bytes 393224 | tf_op jit(solution)/shard_map/ppermute | solution.py:317
  20.0 6.1 %collective-permute-done.4.refs_8_ = bf16[4,2,128,128]{3,2,1,0:T(8,128)(2,1)S(1)} collective-permute-done((bf16[4,2,128,128]{3,2,1,0:T(8,128)(2,1)S(1)}, bf16[4,2,128,128]{3,2,1,0:T(8,128)(2,1)S(1)}, u32[]{:S(2)}, u32[]{:S(2)}) %collective-permute-start.4) | collective-permute-done | bytes 262176 | tf_op jit(solution)/shard_map/ppermute | solution.py:317
  27.1 1.4 %collective-permute-done.6.refs_2_ = bf16[64,1024]{1,0:T(8,128)(2,1)S(1)} collective-permute-done((bf16[64,1024]{1,0:T(8,128)(2,1)S(1)}, bf16[64,1024]{1,0:T(8,128)(2,1)S(1)}, u32[]{:S(2)}, u32[]{:S(2)}) %collective-permute-start.6) | collective-permute-done | bytes 131104 | tf_op jit(solution)/shard_map/ppermute | solution.py:317
  29.2 1.5 %collective-permute-start.12 = (bf16[4,2,128,128]{3,2,1,0:T(8,128)(2,1)S(1)}, bf16[4,2,128,128]{3,2,1,0:T(8,128)(2,1)S(1)}, u32[]{:S(2)}, u32[]{:S(2)}) collective-permute-start(bf16[4,2,128,128]{3,2,1,0:T(8,128)(2,1)S(1)} %get-tuple-element.74.refs_6_), channel_id=1, source_target_pairs={{0,4},{2,6},{4,0},{6,2},{8,12},{10,14},{12,8},{14,10},{16,20},{18,... | collective-permute-start | bytes 786440 | tf_op jit(solution)/shard_map/ppermute | solution.py:317
  31.7 1.7 %attend.2 = (bf16[512,256]{1,0:T(8,128)(2,1)S(1)}, f32[512,128]{1,0:T(8,128)S(1)}) custom-call(s32[16]{0:T(128)S(1)} %copy-done.3, s32[16]{0:T(128)S(1)} %copy-done.4, s32[4]{0:T(128)S(1)} %copy-done.5, s32[4]{0:T(128)S(1)} %copy-done.6, bf16[512,128]{1,0:T(8,128)(2,1)S(1)} %get-tuple-element.67.refs_4_, f32[512,128]{1,0:T(8,128)S(1)} %get-tuple-element.68.refs_5_, ...), custom_call_target="tpu_custom_call" | custom-call | tf_op jit(solution)/shard_map/attend/pallas_call | solution.py:358
  33.4 4.3 %collective-permute-done.9.refs_6_ = bf16[4,2,128,128]{3,2,1,0:T(8,128)(2,1)S(1)} collective-permute-done((bf16[4,2,128,128]{3,2,1,0:T(8,128)(2,1)S(1)}, bf16[4,2,128,128]{3,2,1,0:T(8,128)(2,1)S(1)}, u32[]{:S(2)}, u32[]{:S(2)}) %collective-permute-start.9) | collective-permute-done | bytes 262176 | tf_op jit(solution)/shard_map/ppermute | solution.py:317
  37.7 1.3 %finish.2.refs_0_ = bf16[512,128]{1,0:T(8,128)(2,1)S(1)} custom-call(s32[16]{0:T(128)S(1)} %copy-done.3, s32[16]{0:T(128)S(1)} %copy-done.4, s32[4]{0:T(128)S(1)} %copy-done.5, bf16[512,256]{1,0:T(8,128)(2,1)S(1)} %get-tuple-element.70.refs_3_, f32[512,128]{1,0:T(8,128)S(1)} %get-tuple-element.71.refs_4_, bf16[512,128]{1,0:T(8,128)(2,1)S(1)} %get-tuple-element.72.refs_5_, ...), custom_call_target="tpu_custom_call" | custom-call | tf_op jit(solution)/shard_map/finish/pallas_call | solution.py:358
  39.7 2.9 %collective-permute-start.10 = (bf16[512,128]{1,0:T(8,128)(2,1)S(1)}, bf16[512,128]{1,0:T(8,128)(2,1)S(1)}, u32[]{:S(2)}, u32[]{:S(2)}) collective-permute-start(bf16[512,128]{1,0:T(8,128)(2,1)S(1)} %finish.2.refs_0_), channel_id=1, source_target_pairs={{0,10},{2,8},{4,14},{6,12},{8,2},{10,0},{12,6},{14,4},{16,26},{18,... | collective-permute-start | bytes 393224 | tf_op jit(solution)/shard_map/ppermute | solution.py:317
  42.6 1.3 %collective-permute-done.11.i_ref = bf16[4,2,128,128]{3,2,1,0:T(8,128)(2,1)S(1)} collective-permute-done((bf16[4,2,128,128]{3,2,1,0:T(8,128)(2,1)S(1)}, bf16[4,2,128,128]{3,2,1,0:T(8,128)(2,1)S(1)}, u32[]{:S(2)}, u32[]{:S(2)}) %collective-permute-start.11) | collective-permute-done | bytes 262176 | tf_op jit(solution)/shard_map/ppermute | solution.py:317
  44.7 2.3 %pick_head.3.refs_3_ = bf16[1024,512]{1,0:T(8,128)(2,1)S(1)} custom-call(bf16[2,1024,4,512]{3,2,1,0:T(4,128)(2,1)} %w_ref.3), custom_call_target="tpu_custom_call" | custom-call | tf_op jit(solution)/shard_map/pick_head/pallas_call | solution.py:358
  47.8 1.9 %collective-permute-done.10.refs_0_ = bf16[512,128]{1,0:T(8,128)(2,1)S(1)} collective-permute-done((bf16[512,128]{1,0:T(8,128)(2,1)S(1)}, bf16[512,128]{1,0:T(8,128)(2,1)S(1)}, u32[]{:S(2)}, u32[]{:S(2)}) %collective-permute-start.10) | collective-permute-done | bytes 131104 | tf_op jit(solution)/shard_map/ppermute | solution.py:317
  51.0 1.8 %collective-permute-done.16.refs_1_ = bf16[512,1024]{1,0:T(8,128)(2,1)S(1)} collective-permute-done((bf16[512,1024]{1,0:T(8,128)(2,1)S(1)}, bf16[512,1024]{1,0:T(8,128)(2,1)S(1)}, u32[]{:S(2)}, u32[]{:S(2)}) %collective-permute-start.16) | collective-permute-done | bytes 1048608 | tf_op jit(solution)/shard_map/ppermute | solution.py:339
  53.8 1.8 %attend.3 = (bf16[512,256]{1,0:T(8,128)(2,1)S(1)}, f32[512,128]{1,0:T(8,128)S(1)}) custom-call(s32[16]{0:T(128)S(1)} %copy-done.3, s32[16]{0:T(128)S(1)} %copy-done.4, s32[4]{0:T(128)S(1)} %copy-done.5, s32[4]{0:T(128)S(1)} %copy-done.6, bf16[512,128]{1,0:T(8,128)(2,1)S(1)} %get-tuple-element.85.refs_4_, f32[512,128]{1,0:T(8,128)S(1)} %get-tuple-element.86.refs_5_, ...), custom_call_target="tpu_custom_call" | custom-call | tf_op jit(solution)/shard_map/attend/pallas_call | solution.py:358
  57.3 1.3 %collective-permute-start.18 = (bf16[128,128]{1,0:T(8,128)(2,1)S(1)}, bf16[128,128]{1,0:T(8,128)(2,1)S(1)}, u32[]{:S(2)}, u32[]{:S(2)}) collective-permute-start(bf16[128,128]{1,0:T(8,128)(2,1)S(1)} %get-tuple-element.94), channel_id=1, source_target_pairs={{0,2},{2,0},{4,6},{6,4},{8,10},{10,8},{12,14},{14,12},{16,18},{18,... | collective-permute-start | bytes 98312 | tf_op jit(solution)/shard_map/ppermute | solution.py:317
  58.6 2.3 %collective-permute-start.20 = (bf16[128,128]{1,0:T(8,128)(2,1)S(1)}, bf16[128,128]{1,0:T(8,128)(2,1)S(1)}, u32[]{:S(2)}, u32[]{:S(2)}) collective-permute-start(bf16[128,128]{1,0:T(8,128)(2,1)S(1)} %get-tuple-element.96), channel_id=1, source_target_pairs={{0,10},{2,8},{4,14},{6,12},{8,2},{10,0},{12,6},{14,4},{16,26},{18,... | collective-permute-start | bytes 98312 | tf_op jit(solution)/shard_map/ppermute | solution.py:317
  61.3 1.2 %collective-permute-done.19.refs_2_ = bf16[128,128]{1,0:T(8,128)(2,1)S(1)} collective-permute-done((bf16[128,128]{1,0:T(8,128)(2,1)S(1)}, bf16[128,128]{1,0:T(8,128)(2,1)S(1)}, u32[]{:S(2)}, u32[]{:S(2)}) %collective-permute-start.19) | collective-permute-done | bytes 32800 | tf_op jit(solution)/shard_map/ppermute | solution.py:317
  63.8 1.3 %collective-permute-done.21.refs_2_ = bf16[64,1024]{1,0:T(8,128)(2,1)S(1)} collective-permute-done((bf16[64,1024]{1,0:T(8,128)(2,1)S(1)}, bf16[64,1024]{1,0:T(8,128)(2,1)S(1)}, u32[]{:S(2)}, u32[]{:S(2)}) %collective-permute-start.21) | collective-permute-done | bytes 131104 | tf_op jit(solution)/shard_map/ppermute | solution.py:339
  (50 shorter events, 13.8 us)
Async XLA Ops:
  1.5 7.0 %collective-permute-start = (bf16[2,2,128,128]{3,2,1,0:T(8,128)(2,1)S(1)}, bf16[2,2,128,128]{3,2,1,0:T(8,128)(2,1)S(1)}, u32[]{:S(2)}, u32[]{:S(2)}) collective-permute-start(bf16[2,2,128,128]{3,2,1,0:T(8,128)(2,1)S(1)} %get-tuple-element.53), channel_id=1, source_target_pairs={{0,2},{2,0},{4,6},{6,4},{8,10},{10,8},{12,14},{14,12},{16,18},{18,... | collective-permute-start | bytes 393224 | tf_op jit(solution)/shard_map/ppermute | solution.py:317
  4.5 6.4 %collective-permute-start.1 = (bf16[2,2,128,128]{3,2,1,0:T(8,128)(2,1)S(1)}, bf16[2,2,128,128]{3,2,1,0:T(8,128)(2,1)S(1)}, u32[]{:S(2)}, u32[]{:S(2)}) collective-permute-start(bf16[2,2,128,128]{3,2,1,0:T(8,128)(2,1)S(1)} %get-tuple-element.54), channel_id=1, source_target_pairs={{0,8},{2,10},{4,12},{6,14},{8,0},{10,2},{12,4},{14,6},{16,24},{18,... | collective-permute-start | bytes 393224 | tf_op jit(solution)/shard_map/ppermute | solution.py:317
  6.1 6.0 %collective-permute-start.2 = (bf16[2,2,128,128]{3,2,1,0:T(8,128)(2,1)S(1)}, bf16[2,2,128,128]{3,2,1,0:T(8,128)(2,1)S(1)}, u32[]{:S(2)}, u32[]{:S(2)}) collective-permute-start(bf16[2,2,128,128]{3,2,1,0:T(8,128)(2,1)S(1)} %get-tuple-element.55), channel_id=1, source_target_pairs={{0,10},{2,8},{4,14},{6,12},{8,2},{10,0},{12,6},{14,4},{16,26},{18,... | collective-permute-start | bytes 393224 | tf_op jit(solution)/shard_map/ppermute | solution.py:317
  8.4 23.2 %copy-start.3 = (s32[16]{0:T(128)S(1)}, s32[16]{0:T(128)}, u32[]{:S(2)}) copy-start(s32[16]{0:T(128)} %refs_0_.9) | copy-start | bytes 196
  8.4 23.2 %copy-start.4 = (s32[16]{0:T(128)S(1)}, s32[16]{0:T(128)}, u32[]{:S(2)}) copy-start(s32[16]{0:T(128)} %refs_1_.9) | copy-start | bytes 196
  12.1 14.0 %collective-permute-start.4 = (bf16[4,2,128,128]{3,2,1,0:T(8,128)(2,1)S(1)}, bf16[4,2,128,128]{3,2,1,0:T(8,128)(2,1)S(1)}, u32[]{:S(2)}, u32[]{:S(2)}) collective-permute-start(bf16[4,2,128,128]{3,2,1,0:T(8,128)(2,1)S(1)} %get-tuple-element.60.refs_6_), channel_id=1, source_target_pairs={{0,16},{2,18},{4,20},{6,22},{8,24},{10,26},{12,28},{14,30},{16,0},... | collective-permute-start | bytes 786440 | tf_op jit(solution)/shard_map/ppermute | solution.py:317
  14.9 11.1 %collective-permute-start.5 = (bf16[4,2,128,128]{3,2,1,0:T(8,128)(2,1)S(1)}, bf16[4,2,128,128]{3,2,1,0:T(8,128)(2,1)S(1)}, u32[]{:S(2)}, u32[]{:S(2)}) collective-permute-start(bf16[4,2,128,128]{3,2,1,0:T(8,128)(2,1)S(1)} %get-tuple-element.60.refs_6_), channel_id=1, source_target_pairs={{0,4},{2,6},{4,0},{6,2},{8,12},{10,14},{12,8},{14,10},{16,20},{18,... | collective-permute-start | bytes 786440 | tf_op jit(solution)/shard_map/ppermute | solution.py:317
  16.5 10.6 %collective-permute-start.7 = (bf16[64,1024]{1,0:T(8,128)(2,1)S(1)}, bf16[64,1024]{1,0:T(8,128)(2,1)S(1)}, u32[]{:S(2)}, u32[]{:S(2)}) collective-permute-start(bf16[64,1024]{1,0:T(8,128)(2,1)S(1)} %copy-done.2), channel_id=1, source_target_pairs={{0,10},{2,8},{4,14},{6,12},{8,2},{10,0},{12,6},{14,4},{16,26},{18,... | collective-permute-start | bytes 393224 | tf_op jit(solution)/shard_map/ppermute | solution.py:317
  19.0 9.5 %collective-permute-start.6 = (bf16[64,1024]{1,0:T(8,128)(2,1)S(1)}, bf16[64,1024]{1,0:T(8,128)(2,1)S(1)}, u32[]{:S(2)}, u32[]{:S(2)}) collective-permute-start(bf16[64,1024]{1,0:T(8,128)(2,1)S(1)} %copy-done.2), channel_id=1, source_target_pairs={{0,8},{2,10},{4,12},{6,14},{8,0},{10,2},{12,4},{14,6},{16,24},{18,... | collective-permute-start | bytes 393224 | tf_op jit(solution)/shard_map/ppermute | solution.py:317
  19.4 9.0 %collective-permute-start.3 = (bf16[64,1024]{1,0:T(8,128)(2,1)S(1)}, bf16[64,1024]{1,0:T(8,128)(2,1)S(1)}, u32[]{:S(2)}, u32[]{:S(2)}) collective-permute-start(bf16[64,1024]{1,0:T(8,128)(2,1)S(1)} %copy-done.2), channel_id=1, source_target_pairs={{0,2},{2,0},{4,6},{6,4},{8,10},{10,8},{12,14},{14,12},{16,18},{18,... | collective-permute-start | bytes 393224 | tf_op jit(solution)/shard_map/ppermute | solution.py:317
  28.5 2.2 %collective-permute-start.8 = (bf16[4,64,1024]{2,1,0:T(8,128)(2,1)S(1)}, bf16[4,64,1024]{2,1,0:T(8,128)(2,1)S(1)}, u32[]{:S(2)}, u32[]{:S(2)}) collective-permute-start(bf16[4,64,1024]{2,1,0:T(8,128)(2,1)S(1)} %join.1), channel_id=1, source_target_pairs={{0,1},{1,0},{2,3},{3,2},{4,5},{5,4},{6,7},{7,6},{8,9},{9,8},{10,11... | collective-permute-start | bytes 1572872 | tf_op jit(solution)/shard_map/ppermute | solution.py:339
  28.6 9.2 %collective-permute-start.9 = (bf16[4,2,128,128]{3,2,1,0:T(8,128)(2,1)S(1)}, bf16[4,2,128,128]{3,2,1,0:T(8,128)(2,1)S(1)}, u32[]{:S(2)}, u32[]{:S(2)}) collective-permute-start(bf16[4,2,128,128]{3,2,1,0:T(8,128)(2,1)S(1)} %collective-permute-done.4.refs_8_), channel_id=1, source_target_pairs={{0,4},{2,6},{4,0},{6,2},{8,12},{10,14},{12,8},{14,10},{16,20},{18,... | collective-permute-start | bytes 786440 | tf_op jit(solution)/shard_map/ppermute | solution.py:317
  29.2 14.7 %collective-permute-start.11 = (bf16[4,2,128,128]{3,2,1,0:T(8,128)(2,1)S(1)}, bf16[4,2,128,128]{3,2,1,0:T(8,128)(2,1)S(1)}, u32[]{:S(2)}, u32[]{:S(2)}) collective-permute-start(bf16[4,2,128,128]{3,2,1,0:T(8,128)(2,1)S(1)} %get-tuple-element.74.refs_6_), channel_id=1, source_target_pairs={{0,16},{2,18},{4,20},{6,22},{8,24},{10,26},{12,28},{14,30},{16,0},... | collective-permute-start | bytes 786440 | tf_op jit(solution)/shard_map/ppermute | solution.py:317
  29.2 14.7 %collective-permute-start.12 = (bf16[4,2,128,128]{3,2,1,0:T(8,128)(2,1)S(1)}, bf16[4,2,128,128]{3,2,1,0:T(8,128)(2,1)S(1)}, u32[]{:S(2)}, u32[]{:S(2)}) collective-permute-start(bf16[4,2,128,128]{3,2,1,0:T(8,128)(2,1)S(1)} %get-tuple-element.74.refs_6_), channel_id=1, source_target_pairs={{0,4},{2,6},{4,0},{6,2},{8,12},{10,14},{12,8},{14,10},{16,20},{18,... | collective-permute-start | bytes 786440 | tf_op jit(solution)/shard_map/ppermute | solution.py:317
  39.0 5.0 %collective-permute-start.13 = (bf16[512,128]{1,0:T(8,128)(2,1)S(1)}, bf16[512,128]{1,0:T(8,128)(2,1)S(1)}, u32[]{:S(2)}, u32[]{:S(2)}) collective-permute-start(bf16[512,128]{1,0:T(8,128)(2,1)S(1)} %finish.2.refs_0_), channel_id=1, source_target_pairs={{0,2},{2,0},{4,6},{6,4},{8,10},{10,8},{12,14},{14,12},{16,18},{18,... | collective-permute-start | bytes 393224 | tf_op jit(solution)/shard_map/ppermute | solution.py:317
  39.7 7.4 %collective-permute-start.15 = (bf16[512,128]{1,0:T(8,128)(2,1)S(1)}, bf16[512,128]{1,0:T(8,128)(2,1)S(1)}, u32[]{:S(2)}, u32[]{:S(2)}) collective-permute-start(bf16[512,128]{1,0:T(8,128)(2,1)S(1)} %finish.2.refs_0_), channel_id=1, source_target_pairs={{0,8},{2,10},{4,12},{6,14},{8,0},{10,2},{12,4},{14,6},{16,24},{18,... | collective-permute-start | bytes 393224 | tf_op jit(solution)/shard_map/ppermute | solution.py:317
  39.7 10.0 %collective-permute-start.10 = (bf16[512,128]{1,0:T(8,128)(2,1)S(1)}, bf16[512,128]{1,0:T(8,128)(2,1)S(1)}, u32[]{:S(2)}, u32[]{:S(2)}) collective-permute-start(bf16[512,128]{1,0:T(8,128)(2,1)S(1)} %finish.2.refs_0_), channel_id=1, source_target_pairs={{0,10},{2,8},{4,14},{6,12},{8,2},{10,0},{12,6},{14,4},{16,26},{18,... | collective-permute-start | bytes 393224 | tf_op jit(solution)/shard_map/ppermute | solution.py:317
  44.1 5.6 %collective-permute-start.14 = (bf16[2,2,128,128]{3,2,1,0:T(8,128)(2,1)S(1)}, bf16[2,2,128,128]{3,2,1,0:T(8,128)(2,1)S(1)}, u32[]{:S(2)}, u32[]{:S(2)}) collective-permute-start(bf16[2,2,128,128]{3,2,1,0:T(8,128)(2,1)S(1)} %get-tuple-element.87.refs_8_), channel_id=1, source_target_pairs={{0,4},{2,6},{4,0},{6,2},{8,12},{10,14},{12,8},{14,10},{16,20},{18,... | collective-permute-start | bytes 393224 | tf_op jit(solution)/shard_map/ppermute | solution.py:317
  50.1 2.7 %collective-permute-start.16 = (bf16[512,1024]{1,0:T(8,128)(2,1)S(1)}, bf16[512,1024]{1,0:T(8,128)(2,1)S(1)}, u32[]{:S(2)}, u32[]{:S(2)}) collective-permute-start(bf16[512,1024]{1,0:T(8,128)(2,1)S(1)} %term.3.refs_0_), channel_id=1, source_target_pairs={{0,1},{1,0},{2,3},{3,2},{4,5},{5,4},{6,7},{7,6},{8,9},{9,8},{10,11... | collective-permute-start | bytes 3145736 | tf_op jit(solution)/shard_map/ppermute | solution.py:339
  50.2 5.9 %collective-permute-start.17 = (bf16[2,2,128,128]{3,2,1,0:T(8,128)(2,1)S(1)}, bf16[2,2,128,128]{3,2,1,0:T(8,128)(2,1)S(1)}, u32[]{:S(2)}, u32[]{:S(2)}) collective-permute-start(bf16[2,2,128,128]{3,2,1,0:T(8,128)(2,1)S(1)} %get-tuple-element.88.refs_9_), channel_id=1, source_target_pairs={{0,4},{2,6},{4,0},{6,2},{8,12},{10,14},{12,8},{14,10},{16,20},{18,... | collective-permute-start | bytes 393224 | tf_op jit(solution)/shard_map/ppermute | solution.py:317
  57.3 4.0 %collective-permute-start.18 = (bf16[128,128]{1,0:T(8,128)(2,1)S(1)}, bf16[128,128]{1,0:T(8,128)(2,1)S(1)}, u32[]{:S(2)}, u32[]{:S(2)}) collective-permute-start(bf16[128,128]{1,0:T(8,128)(2,1)S(1)} %get-tuple-element.94), channel_id=1, source_target_pairs={{0,2},{2,0},{4,6},{6,4},{8,10},{10,8},{12,14},{14,12},{16,18},{18,... | collective-permute-start | bytes 98312 | tf_op jit(solution)/shard_map/ppermute | solution.py:317
  58.6 3.9 %collective-permute-start.19 = (bf16[128,128]{1,0:T(8,128)(2,1)S(1)}, bf16[128,128]{1,0:T(8,128)(2,1)S(1)}, u32[]{:S(2)}, u32[]{:S(2)}) collective-permute-start(bf16[128,128]{1,0:T(8,128)(2,1)S(1)} %get-tuple-element.95), channel_id=1, source_target_pairs={{0,8},{2,10},{4,12},{6,14},{8,0},{10,2},{12,4},{14,6},{16,24},{18,... | collective-permute-start | bytes 98312 | tf_op jit(solution)/shard_map/ppermute | solution.py:317
  58.6 4.8 %collective-permute-start.20 = (bf16[128,128]{1,0:T(8,128)(2,1)S(1)}, bf16[128,128]{1,0:T(8,128)(2,1)S(1)}, u32[]{:S(2)}, u32[]{:S(2)}) collective-permute-start(bf16[128,128]{1,0:T(8,128)(2,1)S(1)} %get-tuple-element.96), channel_id=1, source_target_pairs={{0,10},{2,8},{4,14},{6,12},{8,2},{10,0},{12,6},{14,4},{16,26},{18,... | collective-permute-start | bytes 98312 | tf_op jit(solution)/shard_map/ppermute | solution.py:317
  63.8 1.4 %collective-permute-start.21 = (bf16[64,1024]{1,0:T(8,128)(2,1)S(1)}, bf16[64,1024]{1,0:T(8,128)(2,1)S(1)}, u32[]{:S(2)}, u32[]{:S(2)}) collective-permute-start(bf16[64,1024]{1,0:T(8,128)(2,1)S(1)} %get-tuple-element.98), channel_id=1, source_target_pairs={{0,1},{1,0},{2,3},{3,2},{4,5},{5,4},{6,7},{7,6},{8,9},{9,8},{10,11... | collective-permute-start | bytes 393224 | tf_op jit(solution)/shard_map/ppermute | solution.py:339
  (5 other events, 60.8 us)

commit v6 on v5

--- a/solution.py
+++ b/solution.py
@@ -105,10 +105,7 @@
     for shift in range(cores):
         core = lax.rem(core_here + (cores - shift), cores)
         for step in range(spots):
-            if shift == 0:
-                piece = x_refs[step][...]
-            else:
-                piece = x_refs[spots + shift - 1][step]
+            piece = x_refs[shift * spots + step][...]
             at = ((spot ^ step) * cores + core) * own_rows
             x_out[pl.ds(pl.multiple_of(at, own_rows), own_rows)] = piece
     project(x_out, w_ref, q_ref, gate_ref, own_ref, score_scale)
@@ -430,7 +427,7 @@
         history = [[first, near, far, onward]]
     else:
         history = [gather_members(first)]
-    x_group = x_pieces + [shift_core(join(x_pieces), s) for s in range(1, cores)]
+    x_group = x_pieces + [shift_core(piece, s) for s in range(1, cores) for piece in x_pieces]
 
     scalars = [block_user, block_offset, history_length, candidate_count]
     one_head = (all_rows, head_dim)

time: 66 us -> 66 us (level)
    ppermute x19, waiting for transfers between devices: 22.8 us -> 21.7 us  [swap(): return lax.ppermute(value, 'users', [(u, u ^ mask) for u in range(chips)])]
    ppermute x3 -> x6, starting transfers between devices: 0.23 us -> 0.89 us  [shift_core(): return lax.ppermute(value, 'cand', pairs)]
    ppermute x3 -> x6, waiting for transfers between devices: 3.18 us -> 3.84 us  [shift_core(): return lax.ppermute(value, 'cand', pairs)]
    pallas_call x16 -> x15, Pallas kernels: 15.3 us -> 15.3 us  [kernel_call(): pl.pallas_call(kernel, out_shape=[jax.ShapeDtypeStruct(*out) for out in o...]
  transfers between devices with their start and end apart: 22 -> 25, of which waited for: 15 -> 15; matrix products, arithmetic and copies ran while one was open for 0% -> 0% of each run, Pallas kernels for 18% -> 18%
where the time goes in v6:
time: 66 us; the launch traced here: 65.8 us
  waiting for transfers between devices  25.5 us (39%)
  starting transfers between devices  23.7 us (36%)
  Pallas kernels  15.3 us (23%)
  local copies, waits for them, and re-layouts  1.08 us (2%)
    ppermute x19, starting transfers between devices, swap(): return lax.ppermute(value, 'users', [(u, u ^ mask) for u in range(chips)])  22.9 us
    ppermute x19, waiting for transfers between devices, swap(): return lax.ppermute(value, 'users', [(u, u ^ mask) for u in range(chips)])  21.7 us
    pallas_call x15, Pallas kernels, kernel_call(): pl.pallas_call(kernel, out_shape=[jax.ShapeDtypeStruct(*out) for out in o...  15.3 us
    ppermute x6, waiting for transfers between devices, shift_core(): return lax.ppermute(value, 'cand', pairs)  3.84 us
  transfers between devices with their start and end apart: 25, of which 15 were waited for; matrix products, arithmetic and copies ran while one was open for 0% of the time, Pallas kernels for 18%

profile of v6, /device:TPU:0, one launch (start us, length us, event | category | flops | bytes accessed | tf_op | source)
XLA Modules:
  0.0 65.8 jit_solution(15142455334150372223)
XLA Ops:
  1.5 3.0 %collective-permute-start = (bf16[2,2,128,128]{3,2,1,0:T(8,128)(2,1)S(1)}, bf16[2,2,128,128]{3,2,1,0:T(8,128)(2,1)S(1)}, u32[]{:S(2)}, u32[]{:S(2)}) collective-permute-start(bf16[2,2,128,128]{3,2,1,0:T(8,128)(2,1)S(1)} %get-tuple-element.53), channel_id=1, source_target_pairs={{0,2},{2,0},{4,6},{6,4},{8,10},{10,8},{12,14},{14,12},{16,18},{18,... | collective-permute-start | bytes 393224 | tf_op jit(solution)/shard_map/ppermute | solution.py:314
  4.5 1.6 %collective-permute-start.1 = (bf16[2,2,128,128]{3,2,1,0:T(8,128)(2,1)S(1)}, bf16[2,2,128,128]{3,2,1,0:T(8,128)(2,1)S(1)}, u32[]{:S(2)}, u32[]{:S(2)}) collective-permute-start(bf16[2,2,128,128]{3,2,1,0:T(8,128)(2,1)S(1)} %get-tuple-element.54), channel_id=1, source_target_pairs={{0,8},{2,10},{4,12},{6,14},{8,0},{10,2},{12,4},{14,6},{16,24},{18,... | collective-permute-start | bytes 393224 | tf_op jit(solution)/shard_map/ppermute | solution.py:314
  6.1 2.3 %pick_head.2.refs_8_ = bf16[1024,512]{1,0:T(8,128)(2,1)S(1)} custom-call(bf16[2,1024,4,512]{3,2,1,0:T(4,128)(2,1)} %w_ref.3), custom_call_target="tpu_custom_call" | custom-call | tf_op jit(solution)/shard_map/pick_head/pallas_call | solution.py:355
  8.5 2.4 %collective-permute-done.1.refs_2_ = bf16[2,2,128,128]{3,2,1,0:T(8,128)(2,1)S(1)} collective-permute-done((bf16[2,2,128,128]{3,2,1,0:T(8,128)(2,1)S(1)}, bf16[2,2,128,128]{3,2,1,0:T(8,128)(2,1)S(1)}, u32[]{:S(2)}, u32[]{:S(2)}) %collective-permute-start.1) | collective-permute-done | bytes 131104 | tf_op jit(solution)/shard_map/ppermute | solution.py:314
  10.9 1.2 %collective-permute-done.2.refs_3_ = bf16[2,2,128,128]{3,2,1,0:T(8,128)(2,1)S(1)} collective-permute-done((bf16[2,2,128,128]{3,2,1,0:T(8,128)(2,1)S(1)}, bf16[2,2,128,128]{3,2,1,0:T(8,128)(2,1)S(1)}, u32[]{:S(2)}, u32[]{:S(2)}) %collective-permute-start.2) | collective-permute-done | bytes 131104 | tf_op jit(solution)/shard_map/ppermute | solution.py:314
  12.1 2.8 %collective-permute-start.4 = (bf16[4,2,128,128]{3,2,1,0:T(8,128)(2,1)S(1)}, bf16[4,2,128,128]{3,2,1,0:T(8,128)(2,1)S(1)}, u32[]{:S(2)}, u32[]{:S(2)}) collective-permute-start(bf16[4,2,128,128]{3,2,1,0:T(8,128)(2,1)S(1)} %get-tuple-element.60.refs_6_), channel_id=1, source_target_pairs={{0,16},{2,18},{4,20},{6,22},{8,24},{10,26},{12,28},{14,30},{16,0},... | collective-permute-start | bytes 786440 | tf_op jit(solution)/shard_map/ppermute | solution.py:314
  14.9 1.5 %collective-permute-start.5 = (bf16[4,2,128,128]{3,2,1,0:T(8,128)(2,1)S(1)}, bf16[4,2,128,128]{3,2,1,0:T(8,128)(2,1)S(1)}, u32[]{:S(2)}, u32[]{:S(2)}) collective-permute-start(bf16[4,2,128,128]{3,2,1,0:T(8,128)(2,1)S(1)} %get-tuple-element.60.refs_6_), channel_id=1, source_target_pairs={{0,4},{2,6},{4,0},{6,2},{8,12},{10,14},{12,8},{14,10},{16,20},{18,... | collective-permute-start | bytes 786440 | tf_op jit(solution)/shard_map/ppermute | solution.py:314
  16.5 2.5 %collective-permute-start.7 = (bf16[64,1024]{1,0:T(8,128)(2,1)S(1)}, bf16[64,1024]{1,0:T(8,128)(2,1)S(1)}, u32[]{:S(2)}, u32[]{:S(2)}) collective-permute-start(bf16[64,1024]{1,0:T(8,128)(2,1)S(1)} %copy-done.2), channel_id=1, source_target_pairs={{0,10},{2,8},{4,14},{6,12},{8,2},{10,0},{12,6},{14,4},{16,26},{18,... | collective-permute-start | bytes 393224 | tf_op jit(solution)/shard_map/ppermute | solution.py:314
  20.0 6.1 %collective-permute-done.4.refs_8_ = bf16[4,2,128,128]{3,2,1,0:T(8,128)(2,1)S(1)} collective-permute-done((bf16[4,2,128,128]{3,2,1,0:T(8,128)(2,1)S(1)}, bf16[4,2,128,128]{3,2,1,0:T(8,128)(2,1)S(1)}, u32[]{:S(2)}, u32[]{:S(2)}) %collective-permute-start.4) | collective-permute-done | bytes 262176 | tf_op jit(solution)/shard_map/ppermute | solution.py:314
  26.1 1.6 %collective-permute-start.12 = (bf16[4,2,128,128]{3,2,1,0:T(8,128)(2,1)S(1)}, bf16[4,2,128,128]{3,2,1,0:T(8,128)(2,1)S(1)}, u32[]{:S(2)}, u32[]{:S(2)}) collective-permute-start(bf16[4,2,128,128]{3,2,1,0:T(8,128)(2,1)S(1)} %collective-permute-done.4.refs_8_), channel_id=1, source_target_pairs={{0,4},{2,6},{4,0},{6,2},{8,12},{10,14},{12,8},{14,10},{16,20},{18,... | collective-permute-start | bytes 786440 | tf_op jit(solution)/shard_map/ppermute | solution.py:314
  31.0 1.7 %attend.2 = (bf16[512,256]{1,0:T(8,128)(2,1)S(1)}, f32[512,128]{1,0:T(8,128)S(1)}) custom-call(s32[16]{0:T(128)S(1)} %copy-done.3, s32[16]{0:T(128)S(1)} %copy-done.4, s32[4]{0:T(128)S(1)} %copy-done.5, s32[4]{0:T(128)S(1)} %copy-done.6, bf16[512,128]{1,0:T(8,128)(2,1)S(1)} %get-tuple-element.67.refs_4_, f32[512,128]{1,0:T(8,128)S(1)} %get-tuple-element.68.refs_5_, ...), custom_call_target="tpu_custom_call" | custom-call | tf_op jit(solution)/shard_map/attend/pallas_call | solution.py:355
  32.7 2.5 %collective-permute-done.12.refs_6_ = bf16[4,2,128,128]{3,2,1,0:T(8,128)(2,1)S(1)} collective-permute-done((bf16[4,2,128,128]{3,2,1,0:T(8,128)(2,1)S(1)}, bf16[4,2,128,128]{3,2,1,0:T(8,128)(2,1)S(1)}, u32[]{:S(2)}, u32[]{:S(2)}) %collective-permute-start.12) | collective-permute-done | bytes 262176 | tf_op jit(solution)/shard_map/ppermute | solution.py:314
  35.2 1.3 %finish.2.refs_0_ = bf16[512,128]{1,0:T(8,128)(2,1)S(1)} custom-call(s32[16]{0:T(128)S(1)} %copy-done.3, s32[16]{0:T(128)S(1)} %copy-done.4, s32[4]{0:T(128)S(1)} %copy-done.5, bf16[512,256]{1,0:T(8,128)(2,1)S(1)} %get-tuple-element.70.refs_3_, f32[512,128]{1,0:T(8,128)S(1)} %get-tuple-element.71.refs_4_, bf16[512,128]{1,0:T(8,128)(2,1)S(1)} %get-tuple-element.72.refs_5_, ...), custom_call_target="tpu_custom_call" | custom-call | tf_op jit(solution)/shard_map/finish/pallas_call | solution.py:355
  38.1 1.9 %collective-permute-start.13 = (bf16[512,128]{1,0:T(8,128)(2,1)S(1)}, bf16[512,128]{1,0:T(8,128)(2,1)S(1)}, u32[]{:S(2)}, u32[]{:S(2)}) collective-permute-start(bf16[512,128]{1,0:T(8,128)(2,1)S(1)} %finish.2.refs_0_), channel_id=1, source_target_pairs={{0,10},{2,8},{4,14},{6,12},{8,2},{10,0},{12,6},{14,4},{16,26},{18,... | collective-permute-start | bytes 393224 | tf_op jit(solution)/shard_map/ppermute | solution.py:314
  40.0 3.8 %collective-permute-done.14.i_ref = bf16[4,2,128,128]{3,2,1,0:T(8,128)(2,1)S(1)} collective-permute-done((bf16[4,2,128,128]{3,2,1,0:T(8,128)(2,1)S(1)}, bf16[4,2,128,128]{3,2,1,0:T(8,128)(2,1)S(1)}, u32[]{:S(2)}, u32[]{:S(2)}) %collective-permute-start.14) | collective-permute-done | bytes 262176 | tf_op jit(solution)/shard_map/ppermute | solution.py:314
  44.5 2.3 %pick_head.3.refs_3_ = bf16[1024,512]{1,0:T(8,128)(2,1)S(1)} custom-call(bf16[2,1024,4,512]{3,2,1,0:T(4,128)(2,1)} %w_ref.3), custom_call_target="tpu_custom_call" | custom-call | tf_op jit(solution)/shard_map/pick_head/pallas_call | solution.py:355
  47.6 1.8 %collective-permute-done.13.refs_0_ = bf16[512,128]{1,0:T(8,128)(2,1)S(1)} collective-permute-done((bf16[512,128]{1,0:T(8,128)(2,1)S(1)}, bf16[512,128]{1,0:T(8,128)(2,1)S(1)}, u32[]{:S(2)}, u32[]{:S(2)}) %collective-permute-start.13) | collective-permute-done | bytes 131104 | tf_op jit(solution)/shard_map/ppermute | solution.py:314
  50.5 2.1 %collective-permute-done.19.refs_1_ = bf16[512,1024]{1,0:T(8,128)(2,1)S(1)} collective-permute-done((bf16[512,1024]{1,0:T(8,128)(2,1)S(1)}, bf16[512,1024]{1,0:T(8,128)(2,1)S(1)}, u32[]{:S(2)}, u32[]{:S(2)}) %collective-permute-start.19) | collective-permute-done | bytes 1048608 | tf_op jit(solution)/shard_map/ppermute | solution.py:336
  53.5 1.8 %attend.3 = (bf16[512,256]{1,0:T(8,128)(2,1)S(1)}, f32[512,128]{1,0:T(8,128)S(1)}) custom-call(s32[16]{0:T(128)S(1)} %copy-done.3, s32[16]{0:T(128)S(1)} %copy-done.4, s32[4]{0:T(128)S(1)} %copy-done.5, s32[4]{0:T(128)S(1)} %copy-done.6, bf16[512,128]{1,0:T(8,128)(2,1)S(1)} %get-tuple-element.85.refs_4_, f32[512,128]{1,0:T(8,128)S(1)} %get-tuple-element.86.refs_5_, ...), custom_call_target="tpu_custom_call" | custom-call | tf_op jit(solution)/shard_map/attend/pallas_call | solution.py:355
  55.8 1.2 %finish.3 = (bf16[128,128]{1,0:T(8,128)(2,1)S(1)}, bf16[128,128]{1,0:T(8,128)(2,1)S(1)}, bf16[128,128]{1,0:T(8,128)(2,1)S(1)}, bf16[128,128]{1,0:T(8,128)(2,1)S(1)}) custom-call(s32[16]{0:T(128)S(1)} %copy-done.3, s32[16]{0:T(128)S(1)} %copy-done.4, s32[4]{0:T(128)S(1)} %copy-done.5, bf16[512,256]{1,0:T(8,128)(2,1)S(1)} %get-tuple-element.90.refs_3_, ...), custom_call_target="tpu_custom_call" | custom-call | tf_op jit(solution)/shard_map/finish/pallas_call | solution.py:355
  57.0 1.5 %collective-permute-start.21 = (bf16[128,128]{1,0:T(8,128)(2,1)S(1)}, bf16[128,128]{1,0:T(8,128)(2,1)S(1)}, u32[]{:S(2)}, u32[]{:S(2)}) collective-permute-start(bf16[128,128]{1,0:T(8,128)(2,1)S(1)} %get-tuple-element.94), channel_id=1, source_target_pairs={{0,2},{2,0},{4,6},{6,4},{8,10},{10,8},{12,14},{14,12},{16,18},{18,... | collective-permute-start | bytes 98312 | tf_op jit(solution)/shard_map/ppermute | solution.py:314
  58.5 2.0 %collective-permute-start.23 = (bf16[128,128]{1,0:T(8,128)(2,1)S(1)}, bf16[128,128]{1,0:T(8,128)(2,1)S(1)}, u32[]{:S(2)}, u32[]{:S(2)}) collective-permute-start(bf16[128,128]{1,0:T(8,128)(2,1)S(1)} %get-tuple-element.96), channel_id=1, source_target_pairs={{0,10},{2,8},{4,14},{6,12},{8,2},{10,0},{12,6},{14,4},{16,26},{18,... | collective-permute-start | bytes 98312 | tf_op jit(solution)/shard_map/ppermute | solution.py:314
  61.0 1.4 %collective-permute-done.22.refs_2_ = bf16[128,128]{1,0:T(8,128)(2,1)S(1)} collective-permute-done((bf16[128,128]{1,0:T(8,128)(2,1)S(1)}, bf16[128,128]{1,0:T(8,128)(2,1)S(1)}, u32[]{:S(2)}, u32[]{:S(2)}) %collective-permute-start.22) | collective-permute-done | bytes 32800 | tf_op jit(solution)/shard_map/ppermute | solution.py:314
  63.8 1.3 %collective-permute-done.24.refs_2_ = bf16[64,1024]{1,0:T(8,128)(2,1)S(1)} collective-permute-done((bf16[64,1024]{1,0:T(8,128)(2,1)S(1)}, bf16[64,1024]{1,0:T(8,128)(2,1)S(1)}, u32[]{:S(2)}, u32[]{:S(2)}) %collective-permute-start.24) | collective-permute-done | bytes 131104 | tf_op jit(solution)/shard_map/ppermute | solution.py:336
  (55 shorter events, 13.8 us)
Async XLA Ops:
  1.5 7.0 %collective-permute-start = (bf16[2,2,128,128]{3,2,1,0:T(8,128)(2,1)S(1)}, bf16[2,2,128,128]{3,2,1,0:T(8,128)(2,1)S(1)}, u32[]{:S(2)}, u32[]{:S(2)}) collective-permute-start(bf16[2,2,128,128]{3,2,1,0:T(8,128)(2,1)S(1)} %get-tuple-element.53), channel_id=1, source_target_pairs={{0,2},{2,0},{4,6},{6,4},{8,10},{10,8},{12,14},{14,12},{16,18},{18,... | collective-permute-start | bytes 393224 | tf_op jit(solution)/shard_map/ppermute | solution.py:314
  4.5 6.4 %collective-permute-start.1 = (bf16[2,2,128,128]{3,2,1,0:T(8,128)(2,1)S(1)}, bf16[2,2,128,128]{3,2,1,0:T(8,128)(2,1)S(1)}, u32[]{:S(2)}, u32[]{:S(2)}) collective-permute-start(bf16[2,2,128,128]{3,2,1,0:T(8,128)(2,1)S(1)} %get-tuple-element.54), channel_id=1, source_target_pairs={{0,8},{2,10},{4,12},{6,14},{8,0},{10,2},{12,4},{14,6},{16,24},{18,... | collective-permute-start | bytes 393224 | tf_op jit(solution)/shard_map/ppermute | solution.py:314
  6.1 6.0 %collective-permute-start.2 = (bf16[2,2,128,128]{3,2,1,0:T(8,128)(2,1)S(1)}, bf16[2,2,128,128]{3,2,1,0:T(8,128)(2,1)S(1)}, u32[]{:S(2)}, u32[]{:S(2)}) collective-permute-start(bf16[2,2,128,128]{3,2,1,0:T(8,128)(2,1)S(1)} %get-tuple-element.55), channel_id=1, source_target_pairs={{0,10},{2,8},{4,14},{6,12},{8,2},{10,0},{12,6},{14,4},{16,26},{18,... | collective-permute-start | bytes 393224 | tf_op jit(solution)/shard_map/ppermute | solution.py:314
  12.1 14.0 %collective-permute-start.4 = (bf16[4,2,128,128]{3,2,1,0:T(8,128)(2,1)S(1)}, bf16[4,2,128,128]{3,2,1,0:T(8,128)(2,1)S(1)}, u32[]{:S(2)}, u32[]{:S(2)}) collective-permute-start(bf16[4,2,128,128]{3,2,1,0:T(8,128)(2,1)S(1)} %get-tuple-element.60.refs_6_), channel_id=1, source_target_pairs={{0,16},{2,18},{4,20},{6,22},{8,24},{10,26},{12,28},{14,30},{16,0},... | collective-permute-start | bytes 786440 | tf_op jit(solution)/shard_map/ppermute | solution.py:314
  14.9 11.1 %collective-permute-start.5 = (bf16[4,2,128,128]{3,2,1,0:T(8,128)(2,1)S(1)}, bf16[4,2,128,128]{3,2,1,0:T(8,128)(2,1)S(1)}, u32[]{:S(2)}, u32[]{:S(2)}) collective-permute-start(bf16[4,2,128,128]{3,2,1,0:T(8,128)(2,1)S(1)} %get-tuple-element.60.refs_6_), channel_id=1, source_target_pairs={{0,4},{2,6},{4,0},{6,2},{8,12},{10,14},{12,8},{14,10},{16,20},{18,... | collective-permute-start | bytes 786440 | tf_op jit(solution)/shard_map/ppermute | solution.py:314
  16.5 11.2 %collective-permute-start.7 = (bf16[64,1024]{1,0:T(8,128)(2,1)S(1)}, bf16[64,1024]{1,0:T(8,128)(2,1)S(1)}, u32[]{:S(2)}, u32[]{:S(2)}) collective-permute-start(bf16[64,1024]{1,0:T(8,128)(2,1)S(1)} %copy-done.2), channel_id=1, source_target_pairs={{0,10},{2,8},{4,14},{6,12},{8,2},{10,0},{12,6},{14,4},{16,26},{18,... | collective-permute-start | bytes 393224 | tf_op jit(solution)/shard_map/ppermute | solution.py:314
  19.0 9.5 %collective-permute-start.6 = (bf16[64,1024]{1,0:T(8,128)(2,1)S(1)}, bf16[64,1024]{1,0:T(8,128)(2,1)S(1)}, u32[]{:S(2)}, u32[]{:S(2)}) collective-permute-start(bf16[64,1024]{1,0:T(8,128)(2,1)S(1)} %copy-done.2), channel_id=1, source_target_pairs={{0,8},{2,10},{4,12},{6,14},{8,0},{10,2},{12,4},{14,6},{16,24},{18,... | collective-permute-start | bytes 393224 | tf_op jit(solution)/shard_map/ppermute | solution.py:314
  19.4 9.0 %collective-permute-start.3 = (bf16[64,1024]{1,0:T(8,128)(2,1)S(1)}, bf16[64,1024]{1,0:T(8,128)(2,1)S(1)}, u32[]{:S(2)}, u32[]{:S(2)}) collective-permute-start(bf16[64,1024]{1,0:T(8,128)(2,1)S(1)} %copy-done.2), channel_id=1, source_target_pairs={{0,2},{2,0},{4,6},{6,4},{8,10},{10,8},{12,14},{14,12},{16,18},{18,... | collective-permute-start | bytes 393224 | tf_op jit(solution)/shard_map/ppermute | solution.py:314
  26.1 2.9 %collective-permute-start.8 = (bf16[64,1024]{1,0:T(8,128)(2,1)S(1)}, bf16[64,1024]{1,0:T(8,128)(2,1)S(1)}, u32[]{:S(2)}, u32[]{:S(2)}) collective-permute-start(bf16[64,1024]{1,0:T(8,128)(2,1)S(1)} %copy-done.2), channel_id=1, source_target_pairs={{0,1},{1,0},{2,3},{3,2},{4,5},{5,4},{6,7},{7,6},{8,9},{9,8},{10,11... | collective-permute-start | bytes 393224 | tf_op jit(solution)/shard_map/ppermute | solution.py:336
  26.1 9.1 %collective-permute-start.12 = (bf16[4,2,128,128]{3,2,1,0:T(8,128)(2,1)S(1)}, bf16[4,2,128,128]{3,2,1,0:T(8,128)(2,1)S(1)}, u32[]{:S(2)}, u32[]{:S(2)}) collective-permute-start(bf16[4,2,128,128]{3,2,1,0:T(8,128)(2,1)S(1)} %collective-permute-done.4.refs_8_), channel_id=1, source_target_pairs={{0,4},{2,6},{4,0},{6,2},{8,12},{10,14},{12,8},{14,10},{16,20},{18,... | collective-permute-start | bytes 786440 | tf_op jit(solution)/shard_map/ppermute | solution.py:314
  27.7 1.3 %collective-permute-start.11 = (bf16[64,1024]{1,0:T(8,128)(2,1)S(1)}, bf16[64,1024]{1,0:T(8,128)(2,1)S(1)}, u32[]{:S(2)}, u32[]{:S(2)}) collective-permute-start(bf16[64,1024]{1,0:T(8,128)(2,1)S(1)} %collective-permute-done.7.refs_3_), channel_id=1, source_target_pairs={{0,1},{1,0},{2,3},{3,2},{4,5},{5,4},{6,7},{7,6},{8,9},{9,8},{10,11... | collective-permute-start | bytes 393224 | tf_op jit(solution)/shard_map/ppermute | solution.py:336
  28.5 1.5 %collective-permute-start.9 = (bf16[64,1024]{1,0:T(8,128)(2,1)S(1)}, bf16[64,1024]{1,0:T(8,128)(2,1)S(1)}, u32[]{:S(2)}, u32[]{:S(2)}) collective-permute-start(bf16[64,1024]{1,0:T(8,128)(2,1)S(1)} %collective-permute-done.3.refs_1_), channel_id=1, source_target_pairs={{0,1},{1,0},{2,3},{3,2},{4,5},{5,4},{6,7},{7,6},{8,9},{9,8},{10,11... | collective-permute-start | bytes 393224 | tf_op jit(solution)/shard_map/ppermute | solution.py:336
  29.0 14.9 %collective-permute-start.14 = (bf16[4,2,128,128]{3,2,1,0:T(8,128)(2,1)S(1)}, bf16[4,2,128,128]{3,2,1,0:T(8,128)(2,1)S(1)}, u32[]{:S(2)}, u32[]{:S(2)}) collective-permute-start(bf16[4,2,128,128]{3,2,1,0:T(8,128)(2,1)S(1)} %get-tuple-element.74.refs_6_), channel_id=1, source_target_pairs={{0,16},{2,18},{4,20},{6,22},{8,24},{10,26},{12,28},{14,30},{16,0},... | collective-permute-start | bytes 786440 | tf_op jit(solution)/shard_map/ppermute | solution.py:314
  29.0 14.9 %collective-permute-start.15 = (bf16[4,2,128,128]{3,2,1,0:T(8,128)(2,1)S(1)}, bf16[4,2,128,128]{3,2,1,0:T(8,128)(2,1)S(1)}, u32[]{:S(2)}, u32[]{:S(2)}) collective-permute-start(bf16[4,2,128,128]{3,2,1,0:T(8,128)(2,1)S(1)} %get-tuple-element.74.refs_6_), channel_id=1, source_target_pairs={{0,4},{2,6},{4,0},{6,2},{8,12},{10,14},{12,8},{14,10},{16,20},{18,... | collective-permute-start | bytes 786440 | tf_op jit(solution)/shard_map/ppermute | solution.py:314
  36.5 7.4 %collective-permute-start.16 = (bf16[512,128]{1,0:T(8,128)(2,1)S(1)}, bf16[512,128]{1,0:T(8,128)(2,1)S(1)}, u32[]{:S(2)}, u32[]{:S(2)}) collective-permute-start(bf16[512,128]{1,0:T(8,128)(2,1)S(1)} %finish.2.refs_0_), channel_id=1, source_target_pairs={{0,2},{2,0},{4,6},{6,4},{8,10},{10,8},{12,14},{14,12},{16,18},{18,... | collective-permute-start | bytes 393224 | tf_op jit(solution)/shard_map/ppermute | solution.py:314
  37.5 9.4 %collective-permute-start.18 = (bf16[512,128]{1,0:T(8,128)(2,1)S(1)}, bf16[512,128]{1,0:T(8,128)(2,1)S(1)}, u32[]{:S(2)}, u32[]{:S(2)}) collective-permute-start(bf16[512,128]{1,0:T(8,128)(2,1)S(1)} %finish.2.refs_0_), channel_id=1, source_target_pairs={{0,8},{2,10},{4,12},{6,14},{8,0},{10,2},{12,4},{14,6},{16,24},{18,... | collective-permute-start | bytes 393224 | tf_op jit(solution)/shard_map/ppermute | solution.py:314
  38.1 11.3 %collective-permute-start.13 = (bf16[512,128]{1,0:T(8,128)(2,1)S(1)}, bf16[512,128]{1,0:T(8,128)(2,1)S(1)}, u32[]{:S(2)}, u32[]{:S(2)}) collective-permute-start(bf16[512,128]{1,0:T(8,128)(2,1)S(1)} %finish.2.refs_0_), channel_id=1, source_target_pairs={{0,10},{2,8},{4,14},{6,12},{8,2},{10,0},{12,6},{14,4},{16,26},{18,... | collective-permute-start | bytes 393224 | tf_op jit(solution)/shard_map/ppermute | solution.py:314
  43.9 5.5 %collective-permute-start.17 = (bf16[2,2,128,128]{3,2,1,0:T(8,128)(2,1)S(1)}, bf16[2,2,128,128]{3,2,1,0:T(8,128)(2,1)S(1)}, u32[]{:S(2)}, u32[]{:S(2)}) collective-permute-start(bf16[2,2,128,128]{3,2,1,0:T(8,128)(2,1)S(1)} %get-tuple-element.87.refs_8_), channel_id=1, source_target_pairs={{0,4},{2,6},{4,0},{6,2},{8,12},{10,14},{12,8},{14,10},{16,20},{18,... | collective-permute-start | bytes 393224 | tf_op jit(solution)/shard_map/ppermute | solution.py:314
  49.8 2.7 %collective-permute-start.19 = (bf16[512,1024]{1,0:T(8,128)(2,1)S(1)}, bf16[512,1024]{1,0:T(8,128)(2,1)S(1)}, u32[]{:S(2)}, u32[]{:S(2)}) collective-permute-start(bf16[512,1024]{1,0:T(8,128)(2,1)S(1)} %term.3.refs_0_), channel_id=1, source_target_pairs={{0,1},{1,0},{2,3},{3,2},{4,5},{5,4},{6,7},{7,6},{8,9},{9,8},{10,11... | collective-permute-start | bytes 3145736 | tf_op jit(solution)/shard_map/ppermute | solution.py:336
  49.9 5.9 %collective-permute-start.20 = (bf16[2,2,128,128]{3,2,1,0:T(8,128)(2,1)S(1)}, bf16[2,2,128,128]{3,2,1,0:T(8,128)(2,1)S(1)}, u32[]{:S(2)}, u32[]{:S(2)}) collective-permute-start(bf16[2,2,128,128]{3,2,1,0:T(8,128)(2,1)S(1)} %get-tuple-element.88.refs_9_), channel_id=1, source_target_pairs={{0,4},{2,6},{4,0},{6,2},{8,12},{10,14},{12,8},{14,10},{16,20},{18,... | collective-permute-start | bytes 393224 | tf_op jit(solution)/shard_map/ppermute | solution.py:314
  57.0 4.0 %collective-permute-start.21 = (bf16[128,128]{1,0:T(8,128)(2,1)S(1)}, bf16[128,128]{1,0:T(8,128)(2,1)S(1)}, u32[]{:S(2)}, u32[]{:S(2)}) collective-permute-start(bf16[128,128]{1,0:T(8,128)(2,1)S(1)} %get-tuple-element.94), channel_id=1, source_target_pairs={{0,2},{2,0},{4,6},{6,4},{8,10},{10,8},{12,14},{14,12},{16,18},{18,... | collective-permute-start | bytes 98312 | tf_op jit(solution)/shard_map/ppermute | solution.py:314
  58.5 3.9 %collective-permute-start.22 = (bf16[128,128]{1,0:T(8,128)(2,1)S(1)}, bf16[128,128]{1,0:T(8,128)(2,1)S(1)}, u32[]{:S(2)}, u32[]{:S(2)}) collective-permute-start(bf16[128,128]{1,0:T(8,128)(2,1)S(1)} %get-tuple-element.95), channel_id=1, source_target_pairs={{0,8},{2,10},{4,12},{6,14},{8,0},{10,2},{12,4},{14,6},{16,24},{18,... | collective-permute-start | bytes 98312 | tf_op jit(solution)/shard_map/ppermute | solution.py:314
  58.5 4.8 %collective-permute-start.23 = (bf16[128,128]{1,0:T(8,128)(2,1)S(1)}, bf16[128,128]{1,0:T(8,128)(2,1)S(1)}, u32[]{:S(2)}, u32[]{:S(2)}) collective-permute-start(bf16[128,128]{1,0:T(8,128)(2,1)S(1)} %get-tuple-element.96), channel_id=1, source_target_pairs={{0,10},{2,8},{4,14},{6,12},{8,2},{10,0},{12,6},{14,4},{16,26},{18,... | collective-permute-start | bytes 98312 | tf_op jit(solution)/shard_map/ppermute | solution.py:314
  63.7 1.4 %collective-permute-start.24 = (bf16[64,1024]{1,0:T(8,128)(2,1)S(1)}, bf16[64,1024]{1,0:T(8,128)(2,1)S(1)}, u32[]{:S(2)}, u32[]{:S(2)}) collective-permute-start(bf16[64,1024]{1,0:T(8,128)(2,1)S(1)} %get-tuple-element.98), channel_id=1, source_target_pairs={{0,1},{1,0},{2,3},{3,2},{4,5},{5,4},{6,7},{7,6},{8,9},{9,8},{10,11... | collective-permute-start | bytes 393224 | tf_op jit(solution)/shard_map/ppermute | solution.py:336
  (8 other events, 105.9 us)

commit v7 on v6

--- a/solution.py
+++ b/solution.py
@@ -413,7 +413,10 @@
     def together(*values):
         return lax.optimization_barrier(values)
 
-    pieces, first_weight = together(trade_spots(order_history()), pick_head(0))
+    sibling_rows = [shift_core(candidate_rows, s) for s in range(1, cores)]
+    pieces, first_weight, sibling_rows = together(
+        trade_spots(order_history()), pick_head(0), sibling_rows
+    )
     first, later = join_layers(pieces)
     x_pieces = trade_spots([after(candidate_rows, first)] * spots)
     crossed = groups == 4
@@ -427,7 +430,9 @@
         history = [[first, near, far, onward]]
     else:
         history = [gather_members(first)]
-    x_group = x_pieces + [shift_core(piece, s) for s in range(1, cores) for piece in x_pieces]
+    x_group = list(x_pieces)
+    for s in range(1, cores):
+        x_group += [sibling_rows[s - 1]] + [shift_core(piece, s) for piece in x_pieces[1:]]
 
     scalars = [block_user, block_offset, history_length, candidate_count]
     one_head = (all_rows, head_dim)

time: 66 us -> 65.9 us (level)
  transfers between devices with their start and end apart: 25 -> 25, of which waited for: 15 -> 16; matrix products, arithmetic and copies ran while one was open for 0% -> 0% of each run, Pallas kernels for 18% -> 18%
where the time goes in v7:
time: 65.9 us; the launch traced here: 65.8 us
  waiting for transfers between devices  25.6 us (39%)
  starting transfers between devices  23.6 us (36%)
  Pallas kernels  15.3 us (23%)
  local copies, waits for them, and re-layouts  1.08 us (2%)
    ppermute x19, starting transfers between devices, swap(): return lax.ppermute(value, 'users', [(u, u ^ mask) for u in range(chips)])  23 us
    ppermute x19, waiting for transfers between devices, swap(): return lax.ppermute(value, 'users', [(u, u ^ mask) for u in range(chips)])  21.8 us
    pallas_call x15, Pallas kernels, kernel_call(): pl.pallas_call(kernel, out_shape=[jax.ShapeDtypeStruct(*out) for out in o...  15.3 us
    ppermute x6, waiting for transfers between devices, shift_core(): return lax.ppermute(value, 'cand', pairs)  3.76 us
  transfers between devices with their start and end apart: 25, of which 16 were waited for; matrix products, arithmetic and copies ran while one was open for 0% of the time, Pallas kernels for 18%

profile of v7, /device:TPU:0, one launch (start us, length us, event | category | flops | bytes accessed | tf_op | source)
XLA Modules:
  0.0 65.8 jit_solution(9914676917432706909)
XLA Ops:
  1.5 3.0 %collective-permute-start = (bf16[2,2,128,128]{3,2,1,0:T(8,128)(2,1)S(1)}, bf16[2,2,128,128]{3,2,1,0:T(8,128)(2,1)S(1)}, u32[]{:S(2)}, u32[]{:S(2)}) collective-permute-start(bf16[2,2,128,128]{3,2,1,0:T(8,128)(2,1)S(1)} %get-tuple-element.54), channel_id=1, source_target_pairs={{0,2},{2,0},{4,6},{6,4},{8,10},{10,8},{12,14},{14,12},{16,18},{18,... | collective-permute-start | bytes 393224 | tf_op jit(solution)/shard_map/ppermute | solution.py:314
  4.5 1.6 %collective-permute-start.1 = (bf16[2,2,128,128]{3,2,1,0:T(8,128)(2,1)S(1)}, bf16[2,2,128,128]{3,2,1,0:T(8,128)(2,1)S(1)}, u32[]{:S(2)}, u32[]{:S(2)}) collective-permute-start(bf16[2,2,128,128]{3,2,1,0:T(8,128)(2,1)S(1)} %get-tuple-element.55), channel_id=1, source_target_pairs={{0,8},{2,10},{4,12},{6,14},{8,0},{10,2},{12,4},{14,6},{16,24},{18,... | collective-permute-start | bytes 393224 | tf_op jit(solution)/shard_map/ppermute | solution.py:314
  6.1 2.3 %pick_head.2.refs_8_ = bf16[1024,512]{1,0:T(8,128)(2,1)S(1)} custom-call(bf16[2,1024,4,512]{3,2,1,0:T(4,128)(2,1)} %w_ref.3), custom_call_target="tpu_custom_call" | custom-call | tf_op jit(solution)/shard_map/pick_head/pallas_call | solution.py:355
  8.5 2.4 %collective-permute-done.1.refs_2_ = bf16[2,2,128,128]{3,2,1,0:T(8,128)(2,1)S(1)} collective-permute-done((bf16[2,2,128,128]{3,2,1,0:T(8,128)(2,1)S(1)}, bf16[2,2,128,128]{3,2,1,0:T(8,128)(2,1)S(1)}, u32[]{:S(2)}, u32[]{:S(2)}) %collective-permute-start.1) | collective-permute-done | bytes 131104 | tf_op jit(solution)/shard_map/ppermute | solution.py:314
  10.9 1.2 %collective-permute-done.2.refs_3_ = bf16[2,2,128,128]{3,2,1,0:T(8,128)(2,1)S(1)} collective-permute-done((bf16[2,2,128,128]{3,2,1,0:T(8,128)(2,1)S(1)}, bf16[2,2,128,128]{3,2,1,0:T(8,128)(2,1)S(1)}, u32[]{:S(2)}, u32[]{:S(2)}) %collective-permute-start.2) | collective-permute-done | bytes 131104 | tf_op jit(solution)/shard_map/ppermute | solution.py:314
  12.1 2.8 %collective-permute-start.5 = (bf16[4,2,128,128]{3,2,1,0:T(8,128)(2,1)S(1)}, bf16[4,2,128,128]{3,2,1,0:T(8,128)(2,1)S(1)}, u32[]{:S(2)}, u32[]{:S(2)}) collective-permute-start(bf16[4,2,128,128]{3,2,1,0:T(8,128)(2,1)S(1)} %get-tuple-element.61.refs_6_), channel_id=1, source_target_pairs={{0,16},{2,18},{4,20},{6,22},{8,24},{10,26},{12,28},{14,30},{16,0},... | collective-permute-start | bytes 786440 | tf_op jit(solution)/shard_map/ppermute | solution.py:314
  14.9 1.5 %collective-permute-start.6 = (bf16[4,2,128,128]{3,2,1,0:T(8,128)(2,1)S(1)}, bf16[4,2,128,128]{3,2,1,0:T(8,128)(2,1)S(1)}, u32[]{:S(2)}, u32[]{:S(2)}) collective-permute-start(bf16[4,2,128,128]{3,2,1,0:T(8,128)(2,1)S(1)} %get-tuple-element.61.refs_6_), channel_id=1, source_target_pairs={{0,4},{2,6},{4,0},{6,2},{8,12},{10,14},{12,8},{14,10},{16,20},{18,... | collective-permute-start | bytes 786440 | tf_op jit(solution)/shard_map/ppermute | solution.py:314
  16.5 2.5 %collective-permute-start.8 = (bf16[64,1024]{1,0:T(8,128)(2,1)S(1)}, bf16[64,1024]{1,0:T(8,128)(2,1)S(1)}, u32[]{:S(2)}, u32[]{:S(2)}) collective-permute-start(bf16[64,1024]{1,0:T(8,128)(2,1)S(1)} %copy-done.2), channel_id=1, source_target_pairs={{0,10},{2,8},{4,14},{6,12},{8,2},{10,0},{12,6},{14,4},{16,26},{18,... | collective-permute-start | bytes 393224 | tf_op jit(solution)/shard_map/ppermute | solution.py:314
  20.0 6.1 %collective-permute-done.5.refs_8_ = bf16[4,2,128,128]{3,2,1,0:T(8,128)(2,1)S(1)} collective-permute-done((bf16[4,2,128,128]{3,2,1,0:T(8,128)(2,1)S(1)}, bf16[4,2,128,128]{3,2,1,0:T(8,128)(2,1)S(1)}, u32[]{:S(2)}, u32[]{:S(2)}) %collective-permute-start.5) | collective-permute-done | bytes 262176 | tf_op jit(solution)/shard_map/ppermute | solution.py:314
  26.1 1.6 %collective-permute-start.12 = (bf16[4,2,128,128]{3,2,1,0:T(8,128)(2,1)S(1)}, bf16[4,2,128,128]{3,2,1,0:T(8,128)(2,1)S(1)}, u32[]{:S(2)}, u32[]{:S(2)}) collective-permute-start(bf16[4,2,128,128]{3,2,1,0:T(8,128)(2,1)S(1)} %collective-permute-done.5.refs_8_), channel_id=1, source_target_pairs={{0,4},{2,6},{4,0},{6,2},{8,12},{10,14},{12,8},{14,10},{16,20},{18,... | collective-permute-start | bytes 786440 | tf_op jit(solution)/shard_map/ppermute | solution.py:314
  31.0 1.7 %attend.2 = (bf16[512,256]{1,0:T(8,128)(2,1)S(1)}, f32[512,128]{1,0:T(8,128)S(1)}) custom-call(s32[16]{0:T(128)S(1)} %copy-done.3, s32[16]{0:T(128)S(1)} %copy-done.4, s32[4]{0:T(128)S(1)} %copy-done.5, s32[4]{0:T(128)S(1)} %copy-done.6, bf16[512,128]{1,0:T(8,128)(2,1)S(1)} %get-tuple-element.69.refs_4_, f32[512,128]{1,0:T(8,128)S(1)} %get-tuple-element.70.refs_5_, ...), custom_call_target="tpu_custom_call" | custom-call | tf_op jit(solution)/shard_map/attend/pallas_call | solution.py:355
  32.7 2.6 %collective-permute-done.12.refs_6_ = bf16[4,2,128,128]{3,2,1,0:T(8,128)(2,1)S(1)} collective-permute-done((bf16[4,2,128,128]{3,2,1,0:T(8,128)(2,1)S(1)}, bf16[4,2,128,128]{3,2,1,0:T(8,128)(2,1)S(1)}, u32[]{:S(2)}, u32[]{:S(2)}) %collective-permute-start.12) | collective-permute-done | bytes 262176 | tf_op jit(solution)/shard_map/ppermute | solution.py:314
  35.3 1.3 %finish.2.refs_0_ = bf16[512,128]{1,0:T(8,128)(2,1)S(1)} custom-call(s32[16]{0:T(128)S(1)} %copy-done.3, s32[16]{0:T(128)S(1)} %copy-done.4, s32[4]{0:T(128)S(1)} %copy-done.5, bf16[512,256]{1,0:T(8,128)(2,1)S(1)} %get-tuple-element.72.refs_3_, f32[512,128]{1,0:T(8,128)S(1)} %get-tuple-element.73.refs_4_, bf16[512,128]{1,0:T(8,128)(2,1)S(1)} %get-tuple-element.74.refs_5_, ...), custom_call_target="tpu_custom_call" | custom-call | tf_op jit(solution)/shard_map/finish/pallas_call | solution.py:355
  37.8 2.4 %collective-permute-start.13 = (bf16[512,128]{1,0:T(8,128)(2,1)S(1)}, bf16[512,128]{1,0:T(8,128)(2,1)S(1)}, u32[]{:S(2)}, u32[]{:S(2)}) collective-permute-start(bf16[512,128]{1,0:T(8,128)(2,1)S(1)} %finish.2.refs_0_), channel_id=1, source_target_pairs={{0,10},{2,8},{4,14},{6,12},{8,2},{10,0},{12,6},{14,4},{16,26},{18,... | collective-permute-start | bytes 393224 | tf_op jit(solution)/shard_map/ppermute | solution.py:314
  40.2 3.6 %collective-permute-done.14.i_ref = bf16[4,2,128,128]{3,2,1,0:T(8,128)(2,1)S(1)} collective-permute-done((bf16[4,2,128,128]{3,2,1,0:T(8,128)(2,1)S(1)}, bf16[4,2,128,128]{3,2,1,0:T(8,128)(2,1)S(1)}, u32[]{:S(2)}, u32[]{:S(2)}) %collective-permute-start.14) | collective-permute-done | bytes 262176 | tf_op jit(solution)/shard_map/ppermute | solution.py:314
  44.5 2.3 %pick_head.3.refs_3_ = bf16[1024,512]{1,0:T(8,128)(2,1)S(1)} custom-call(bf16[2,1024,4,512]{3,2,1,0:T(4,128)(2,1)} %w_ref.3), custom_call_target="tpu_custom_call" | custom-call | tf_op jit(solution)/shard_map/pick_head/pallas_call | solution.py:355
  47.5 1.2 %collective-permute-done.13.refs_0_ = bf16[512,128]{1,0:T(8,128)(2,1)S(1)} collective-permute-done((bf16[512,128]{1,0:T(8,128)(2,1)S(1)}, bf16[512,128]{1,0:T(8,128)(2,1)S(1)}, u32[]{:S(2)}, u32[]{:S(2)}) %collective-permute-start.13) | collective-permute-done | bytes 131104 | tf_op jit(solution)/shard_map/ppermute | solution.py:314
  50.4 1.9 %collective-permute-done.19.refs_1_ = bf16[512,1024]{1,0:T(8,128)(2,1)S(1)} collective-permute-done((bf16[512,1024]{1,0:T(8,128)(2,1)S(1)}, bf16[512,1024]{1,0:T(8,128)(2,1)S(1)}, u32[]{:S(2)}, u32[]{:S(2)}) %collective-permute-start.19) | collective-permute-done | bytes 1048608 | tf_op jit(solution)/shard_map/ppermute | solution.py:336
  53.3 1.8 %attend.3 = (bf16[512,256]{1,0:T(8,128)(2,1)S(1)}, f32[512,128]{1,0:T(8,128)S(1)}) custom-call(s32[16]{0:T(128)S(1)} %copy-done.3, s32[16]{0:T(128)S(1)} %copy-done.4, s32[4]{0:T(128)S(1)} %copy-done.5, s32[4]{0:T(128)S(1)} %copy-done.6, bf16[512,128]{1,0:T(8,128)(2,1)S(1)} %get-tuple-element.87.refs_4_, f32[512,128]{1,0:T(8,128)S(1)} %get-tuple-element.88.refs_5_, ...), custom_call_target="tpu_custom_call" | custom-call | tf_op jit(solution)/shard_map/attend/pallas_call | solution.py:355
  55.6 1.2 %finish.3 = (bf16[128,128]{1,0:T(8,128)(2,1)S(1)}, bf16[128,128]{1,0:T(8,128)(2,1)S(1)}, bf16[128,128]{1,0:T(8,128)(2,1)S(1)}, bf16[128,128]{1,0:T(8,128)(2,1)S(1)}) custom-call(s32[16]{0:T(128)S(1)} %copy-done.3, s32[16]{0:T(128)S(1)} %copy-done.4, s32[4]{0:T(128)S(1)} %copy-done.5, bf16[512,256]{1,0:T(8,128)(2,1)S(1)} %get-tuple-element.92.refs_3_, ...), custom_call_target="tpu_custom_call" | custom-call | tf_op jit(solution)/shard_map/finish/pallas_call | solution.py:355
  56.8 1.6 %collective-permute-start.21 = (bf16[128,128]{1,0:T(8,128)(2,1)S(1)}, bf16[128,128]{1,0:T(8,128)(2,1)S(1)}, u32[]{:S(2)}, u32[]{:S(2)}) collective-permute-start(bf16[128,128]{1,0:T(8,128)(2,1)S(1)} %get-tuple-element.96), channel_id=1, source_target_pairs={{0,2},{2,0},{4,6},{6,4},{8,10},{10,8},{12,14},{14,12},{16,18},{18,... | collective-permute-start | bytes 98312 | tf_op jit(solution)/shard_map/ppermute | solution.py:314
  58.5 1.9 %collective-permute-start.23 = (bf16[128,128]{1,0:T(8,128)(2,1)S(1)}, bf16[128,128]{1,0:T(8,128)(2,1)S(1)}, u32[]{:S(2)}, u32[]{:S(2)}) collective-permute-start(bf16[128,128]{1,0:T(8,128)(2,1)S(1)} %get-tuple-element.98), channel_id=1, source_target_pairs={{0,10},{2,8},{4,14},{6,12},{8,2},{10,0},{12,6},{14,4},{16,26},{18,... | collective-permute-start | bytes 98312 | tf_op jit(solution)/shard_map/ppermute | solution.py:314
  60.8 1.6 %collective-permute-done.22.refs_2_ = bf16[128,128]{1,0:T(8,128)(2,1)S(1)} collective-permute-done((bf16[128,128]{1,0:T(8,128)(2,1)S(1)}, bf16[128,128]{1,0:T(8,128)(2,1)S(1)}, u32[]{:S(2)}, u32[]{:S(2)}) %collective-permute-start.22) | collective-permute-done | bytes 32800 | tf_op jit(solution)/shard_map/ppermute | solution.py:314
  63.7 1.3 %collective-permute-done.24.refs_2_ = bf16[64,1024]{1,0:T(8,128)(2,1)S(1)} collective-permute-done((bf16[64,1024]{1,0:T(8,128)(2,1)S(1)}, bf16[64,1024]{1,0:T(8,128)(2,1)S(1)}, u32[]{:S(2)}, u32[]{:S(2)}) %collective-permute-start.24) | collective-permute-done | bytes 131104 | tf_op jit(solution)/shard_map/ppermute | solution.py:336
  (55 shorter events, 14.0 us)
Async XLA Ops:
  1.5 7.0 %collective-permute-start = (bf16[2,2,128,128]{3,2,1,0:T(8,128)(2,1)S(1)}, bf16[2,2,128,128]{3,2,1,0:T(8,128)(2,1)S(1)}, u32[]{:S(2)}, u32[]{:S(2)}) collective-permute-start(bf16[2,2,128,128]{3,2,1,0:T(8,128)(2,1)S(1)} %get-tuple-element.54), channel_id=1, source_target_pairs={{0,2},{2,0},{4,6},{6,4},{8,10},{10,8},{12,14},{14,12},{16,18},{18,... | collective-permute-start | bytes 393224 | tf_op jit(solution)/shard_map/ppermute | solution.py:314
  4.5 6.4 %collective-permute-start.1 = (bf16[2,2,128,128]{3,2,1,0:T(8,128)(2,1)S(1)}, bf16[2,2,128,128]{3,2,1,0:T(8,128)(2,1)S(1)}, u32[]{:S(2)}, u32[]{:S(2)}) collective-permute-start(bf16[2,2,128,128]{3,2,1,0:T(8,128)(2,1)S(1)} %get-tuple-element.55), channel_id=1, source_target_pairs={{0,8},{2,10},{4,12},{6,14},{8,0},{10,2},{12,4},{14,6},{16,24},{18,... | collective-permute-start | bytes 393224 | tf_op jit(solution)/shard_map/ppermute | solution.py:314
  6.1 6.0 %collective-permute-start.2 = (bf16[2,2,128,128]{3,2,1,0:T(8,128)(2,1)S(1)}, bf16[2,2,128,128]{3,2,1,0:T(8,128)(2,1)S(1)}, u32[]{:S(2)}, u32[]{:S(2)}) collective-permute-start(bf16[2,2,128,128]{3,2,1,0:T(8,128)(2,1)S(1)} %get-tuple-element.56), channel_id=1, source_target_pairs={{0,10},{2,8},{4,14},{6,12},{8,2},{10,0},{12,6},{14,4},{16,26},{18,... | collective-permute-start | bytes 393224 | tf_op jit(solution)/shard_map/ppermute | solution.py:314
  6.1 6.0 %collective-permute-start.3 = (bf16[64,1024]{1,0:T(8,128)(2,1)}, bf16[64,1024]{1,0:T(8,128)(2,1)S(1)}, u32[]{:S(2)}, u32[]{:S(2)}) collective-permute-start(bf16[64,1024]{1,0:T(8,128)(2,1)} %refs_0_.4), channel_id=1, source_target_pairs={{0,1},{1,0},{2,3},{3,2},{4,5},{5,4},{6,7},{7,6},{8,9},{9,8},{10,11... | collective-permute-start | bytes 393224 | tf_op jit(solution)/shard_map/ppermute | solution.py:336
  12.1 14.0 %collective-permute-start.5 = (bf16[4,2,128,128]{3,2,1,0:T(8,128)(2,1)S(1)}, bf16[4,2,128,128]{3,2,1,0:T(8,128)(2,1)S(1)}, u32[]{:S(2)}, u32[]{:S(2)}) collective-permute-start(bf16[4,2,128,128]{3,2,1,0:T(8,128)(2,1)S(1)} %get-tuple-element.61.refs_6_), channel_id=1, source_target_pairs={{0,16},{2,18},{4,20},{6,22},{8,24},{10,26},{12,28},{14,30},{16,0},... | collective-permute-start | bytes 786440 | tf_op jit(solution)/shard_map/ppermute | solution.py:314
  14.9 11.1 %collective-permute-start.6 = (bf16[4,2,128,128]{3,2,1,0:T(8,128)(2,1)S(1)}, bf16[4,2,128,128]{3,2,1,0:T(8,128)(2,1)S(1)}, u32[]{:S(2)}, u32[]{:S(2)}) collective-permute-start(bf16[4,2,128,128]{3,2,1,0:T(8,128)(2,1)S(1)} %get-tuple-element.61.refs_6_), channel_id=1, source_target_pairs={{0,4},{2,6},{4,0},{6,2},{8,12},{10,14},{12,8},{14,10},{16,20},{18,... | collective-permute-start | bytes 786440 | tf_op jit(solution)/shard_map/ppermute | solution.py:314
  16.5 11.2 %collective-permute-start.8 = (bf16[64,1024]{1,0:T(8,128)(2,1)S(1)}, bf16[64,1024]{1,0:T(8,128)(2,1)S(1)}, u32[]{:S(2)}, u32[]{:S(2)}) collective-permute-start(bf16[64,1024]{1,0:T(8,128)(2,1)S(1)} %copy-done.2), channel_id=1, source_target_pairs={{0,10},{2,8},{4,14},{6,12},{8,2},{10,0},{12,6},{14,4},{16,26},{18,... | collective-permute-start | bytes 393224 | tf_op jit(solution)/shard_map/ppermute | solution.py:314
  19.0 9.5 %collective-permute-start.7 = (bf16[64,1024]{1,0:T(8,128)(2,1)S(1)}, bf16[64,1024]{1,0:T(8,128)(2,1)S(1)}, u32[]{:S(2)}, u32[]{:S(2)}) collective-permute-start(bf16[64,1024]{1,0:T(8,128)(2,1)S(1)} %copy-done.2), channel_id=1, source_target_pairs={{0,8},{2,10},{4,12},{6,14},{8,0},{10,2},{12,4},{14,6},{16,24},{18,... | collective-permute-start | bytes 393224 | tf_op jit(solution)/shard_map/ppermute | solution.py:314
  19.4 9.0 %collective-permute-start.4 = (bf16[64,1024]{1,0:T(8,128)(2,1)S(1)}, bf16[64,1024]{1,0:T(8,128)(2,1)S(1)}, u32[]{:S(2)}, u32[]{:S(2)}) collective-permute-start(bf16[64,1024]{1,0:T(8,128)(2,1)S(1)} %copy-done.2), channel_id=1, source_target_pairs={{0,2},{2,0},{4,6},{6,4},{8,10},{10,8},{12,14},{14,12},{16,18},{18,... | collective-permute-start | bytes 393224 | tf_op jit(solution)/shard_map/ppermute | solution.py:314
  26.1 9.2 %collective-permute-start.12 = (bf16[4,2,128,128]{3,2,1,0:T(8,128)(2,1)S(1)}, bf16[4,2,128,128]{3,2,1,0:T(8,128)(2,1)S(1)}, u32[]{:S(2)}, u32[]{:S(2)}) collective-permute-start(bf16[4,2,128,128]{3,2,1,0:T(8,128)(2,1)S(1)} %collective-permute-done.5.refs_8_), channel_id=1, source_target_pairs={{0,4},{2,6},{4,0},{6,2},{8,12},{10,14},{12,8},{14,10},{16,20},{18,... | collective-permute-start | bytes 786440 | tf_op jit(solution)/shard_map/ppermute | solution.py:314
  27.7 1.3 %collective-permute-start.11 = (bf16[64,1024]{1,0:T(8,128)(2,1)S(1)}, bf16[64,1024]{1,0:T(8,128)(2,1)S(1)}, u32[]{:S(2)}, u32[]{:S(2)}) collective-permute-start(bf16[64,1024]{1,0:T(8,128)(2,1)S(1)} %collective-permute-done.8.refs_3_), channel_id=1, source_target_pairs={{0,1},{1,0},{2,3},{3,2},{4,5},{5,4},{6,7},{7,6},{8,9},{9,8},{10,11... | collective-permute-start | bytes 393224 | tf_op jit(solution)/shard_map/ppermute | solution.py:336
  28.5 1.5 %collective-permute-start.9 = (bf16[64,1024]{1,0:T(8,128)(2,1)S(1)}, bf16[64,1024]{1,0:T(8,128)(2,1)S(1)}, u32[]{:S(2)}, u32[]{:S(2)}) collective-permute-start(bf16[64,1024]{1,0:T(8,128)(2,1)S(1)} %collective-permute-done.4.refs_1_), channel_id=1, source_target_pairs={{0,1},{1,0},{2,3},{3,2},{4,5},{5,4},{6,7},{7,6},{8,9},{9,8},{10,11... | collective-permute-start | bytes 393224 | tf_op jit(solution)/shard_map/ppermute | solution.py:336
  29.0 14.8 %collective-permute-start.14 = (bf16[4,2,128,128]{3,2,1,0:T(8,128)(2,1)S(1)}, bf16[4,2,128,128]{3,2,1,0:T(8,128)(2,1)S(1)}, u32[]{:S(2)}, u32[]{:S(2)}) collective-permute-start(bf16[4,2,128,128]{3,2,1,0:T(8,128)(2,1)S(1)} %get-tuple-element.76.refs_6_), channel_id=1, source_target_pairs={{0,16},{2,18},{4,20},{6,22},{8,24},{10,26},{12,28},{14,30},{16,0},... | collective-permute-start | bytes 786440 | tf_op jit(solution)/shard_map/ppermute | solution.py:314
  29.0 14.8 %collective-permute-start.15 = (bf16[4,2,128,128]{3,2,1,0:T(8,128)(2,1)S(1)}, bf16[4,2,128,128]{3,2,1,0:T(8,128)(2,1)S(1)}, u32[]{:S(2)}, u32[]{:S(2)}) collective-permute-start(bf16[4,2,128,128]{3,2,1,0:T(8,128)(2,1)S(1)} %get-tuple-element.76.refs_6_), channel_id=1, source_target_pairs={{0,4},{2,6},{4,0},{6,2},{8,12},{10,14},{12,8},{14,10},{16,20},{18,... | collective-permute-start | bytes 786440 | tf_op jit(solution)/shard_map/ppermute | solution.py:314
  36.6 7.2 %collective-permute-start.16 = (bf16[512,128]{1,0:T(8,128)(2,1)S(1)}, bf16[512,128]{1,0:T(8,128)(2,1)S(1)}, u32[]{:S(2)}, u32[]{:S(2)}) collective-permute-start(bf16[512,128]{1,0:T(8,128)(2,1)S(1)} %finish.2.refs_0_), channel_id=1, source_target_pairs={{0,2},{2,0},{4,6},{6,4},{8,10},{10,8},{12,14},{14,12},{16,18},{18,... | collective-permute-start | bytes 393224 | tf_op jit(solution)/shard_map/ppermute | solution.py:314
  36.8 10.0 %collective-permute-start.18 = (bf16[512,128]{1,0:T(8,128)(2,1)S(1)}, bf16[512,128]{1,0:T(8,128)(2,1)S(1)}, u32[]{:S(2)}, u32[]{:S(2)}) collective-permute-start(bf16[512,128]{1,0:T(8,128)(2,1)S(1)} %finish.2.refs_0_), channel_id=1, source_target_pairs={{0,8},{2,10},{4,12},{6,14},{8,0},{10,2},{12,4},{14,6},{16,24},{18,... | collective-permute-start | bytes 393224 | tf_op jit(solution)/shard_map/ppermute | solution.py:314
  37.8 10.9 %collective-permute-start.13 = (bf16[512,128]{1,0:T(8,128)(2,1)S(1)}, bf16[512,128]{1,0:T(8,128)(2,1)S(1)}, u32[]{:S(2)}, u32[]{:S(2)}) collective-permute-start(bf16[512,128]{1,0:T(8,128)(2,1)S(1)} %finish.2.refs_0_), channel_id=1, source_target_pairs={{0,10},{2,8},{4,14},{6,12},{8,2},{10,0},{12,6},{14,4},{16,26},{18,... | collective-permute-start | bytes 393224 | tf_op jit(solution)/shard_map/ppermute | solution.py:314
  43.8 5.4 %collective-permute-start.17 = (bf16[2,2,128,128]{3,2,1,0:T(8,128)(2,1)S(1)}, bf16[2,2,128,128]{3,2,1,0:T(8,128)(2,1)S(1)}, u32[]{:S(2)}, u32[]{:S(2)}) collective-permute-start(bf16[2,2,128,128]{3,2,1,0:T(8,128)(2,1)S(1)} %get-tuple-element.89.refs_8_), channel_id=1, source_target_pairs={{0,4},{2,6},{4,0},{6,2},{8,12},{10,14},{12,8},{14,10},{16,20},{18,... | collective-permute-start | bytes 393224 | tf_op jit(solution)/shard_map/ppermute | solution.py:314
  49.6 2.7 %collective-permute-start.19 = (bf16[512,1024]{1,0:T(8,128)(2,1)S(1)}, bf16[512,1024]{1,0:T(8,128)(2,1)S(1)}, u32[]{:S(2)}, u32[]{:S(2)}) collective-permute-start(bf16[512,1024]{1,0:T(8,128)(2,1)S(1)} %term.3.refs_0_), channel_id=1, source_target_pairs={{0,1},{1,0},{2,3},{3,2},{4,5},{5,4},{6,7},{7,6},{8,9},{9,8},{10,11... | collective-permute-start | bytes 3145736 | tf_op jit(solution)/shard_map/ppermute | solution.py:336
  49.7 5.9 %collective-permute-start.20 = (bf16[2,2,128,128]{3,2,1,0:T(8,128)(2,1)S(1)}, bf16[2,2,128,128]{3,2,1,0:T(8,128)(2,1)S(1)}, u32[]{:S(2)}, u32[]{:S(2)}) collective-permute-start(bf16[2,2,128,128]{3,2,1,0:T(8,128)(2,1)S(1)} %get-tuple-element.90.refs_9_), channel_id=1, source_target_pairs={{0,4},{2,6},{4,0},{6,2},{8,12},{10,14},{12,8},{14,10},{16,20},{18,... | collective-permute-start | bytes 393224 | tf_op jit(solution)/shard_map/ppermute | solution.py:314
  56.8 4.0 %collective-permute-start.21 = (bf16[128,128]{1,0:T(8,128)(2,1)S(1)}, bf16[128,128]{1,0:T(8,128)(2,1)S(1)}, u32[]{:S(2)}, u32[]{:S(2)}) collective-permute-start(bf16[128,128]{1,0:T(8,128)(2,1)S(1)} %get-tuple-element.96), channel_id=1, source_target_pairs={{0,2},{2,0},{4,6},{6,4},{8,10},{10,8},{12,14},{14,12},{16,18},{18,... | collective-permute-start | bytes 98312 | tf_op jit(solution)/shard_map/ppermute | solution.py:314
  58.5 3.9 %collective-permute-start.22 = (bf16[128,128]{1,0:T(8,128)(2,1)S(1)}, bf16[128,128]{1,0:T(8,128)(2,1)S(1)}, u32[]{:S(2)}, u32[]{:S(2)}) collective-permute-start(bf16[128,128]{1,0:T(8,128)(2,1)S(1)} %get-tuple-element.97), channel_id=1, source_target_pairs={{0,8},{2,10},{4,12},{6,14},{8,0},{10,2},{12,4},{14,6},{16,24},{18,... | collective-permute-start | bytes 98312 | tf_op jit(solution)/shard_map/ppermute | solution.py:314
  58.5 4.8 %collective-permute-start.23 = (bf16[128,128]{1,0:T(8,128)(2,1)S(1)}, bf16[128,128]{1,0:T(8,128)(2,1)S(1)}, u32[]{:S(2)}, u32[]{:S(2)}) collective-permute-start(bf16[128,128]{1,0:T(8,128)(2,1)S(1)} %get-tuple-element.98), channel_id=1, source_target_pairs={{0,10},{2,8},{4,14},{6,12},{8,2},{10,0},{12,6},{14,4},{16,26},{18,... | collective-permute-start | bytes 98312 | tf_op jit(solution)/shard_map/ppermute | solution.py:314
  63.6 1.4 %collective-permute-start.24 = (bf16[64,1024]{1,0:T(8,128)(2,1)S(1)}, bf16[64,1024]{1,0:T(8,128)(2,1)S(1)}, u32[]{:S(2)}, u32[]{:S(2)}) collective-permute-start(bf16[64,1024]{1,0:T(8,128)(2,1)S(1)} %get-tuple-element.100), channel_id=1, source_target_pairs={{0,1},{1,0},{2,3},{3,2},{4,5},{5,4},{6,7},{7,6},{8,9},{9,8},{10,11... | collective-permute-start | bytes 393224 | tf_op jit(solution)/shard_map/ppermute | solution.py:336
  (8 other events, 105.9 us)

commit v8 on v7

--- a/solution.py
+++ b/solution.py
@@ -485,9 +485,7 @@
                 far = halves(after(far, near, gated[1]))
                 ahead = swap(far[0], near_mask)
                 early, far, next_weight = together(gated[:-1], far, next_weight)
-                late, ahead = together(gated[-1:], ahead)
-                parts = [(0, early), (spots - 1, late)]
-                arrays = [whole, near] + far + [ahead, swap(far[1], near_mask)]
+                parts = [(0, early), (spots - 1, gated[-1:])]
             else:
                 arrays = gather_members(later[layer_index])
                 parts = [(0, gated)]
@@ -504,6 +502,9 @@
                     "term",
                     heads + [weight_out] + terms,
                 )
+            if crossed:
+                terms, ahead = together(terms, ahead)
+                arrays = [whole, near] + far + [ahead, swap(far[1], near_mask)]
             terms = terms + [shift_core(terms[0], s) for s in range(1, cores)]
             history.append(arrays)
             x, *projected = kernel_call(

time: 65.9 us -> 65.9 us (level)
  transfers between devices with their start and end apart: 25 -> 25, of which waited for: 16 -> 15; matrix products, arithmetic and copies ran while one was open for 0% -> 0% of each run, Pallas kernels for 18% -> 19%
where the time goes in v8:
time: 65.9 us; the launch traced here: 65.8 us
  waiting for transfers between devices  25 us (38%)
  starting transfers between devices  24.2 us (37%)
  Pallas kernels  15.3 us (23%)
  local copies, waits for them, and re-layouts  1.08 us (2%)
    ppermute x19, starting transfers between devices, swap(): return lax.ppermute(value, 'users', [(u, u ^ mask) for u in range(chips)])  23.5 us
    ppermute x19, waiting for transfers between devices, swap(): return lax.ppermute(value, 'users', [(u, u ^ mask) for u in range(chips)])  21.7 us
    pallas_call x15, Pallas kernels, kernel_call(): pl.pallas_call(kernel, out_shape=[jax.ShapeDtypeStruct(*out) for out in o...  15.3 us
    ppermute x6, waiting for transfers between devices, shift_core(): return lax.ppermute(value, 'cand', pairs)  3.29 us
  transfers between devices with their start and end apart: 25, of which 15 were waited for; matrix products, arithmetic and copies ran while one was open for 0% of the time, Pallas kernels for 19%

profile of v8, /device:TPU:0, one launch (start us, length us, event | category | flops | bytes accessed | tf_op | source)
XLA Modules:
  0.0 65.8 jit_solution(3092567754084524747)
XLA Ops:
  1.5 3.0 %collective-permute-start = (bf16[2,2,128,128]{3,2,1,0:T(8,128)(2,1)S(1)}, bf16[2,2,128,128]{3,2,1,0:T(8,128)(2,1)S(1)}, u32[]{:S(2)}, u32[]{:S(2)}) collective-permute-start(bf16[2,2,128,128]{3,2,1,0:T(8,128)(2,1)S(1)} %get-tuple-element.54), channel_id=1, source_target_pairs={{0,2},{2,0},{4,6},{6,4},{8,10},{10,8},{12,14},{14,12},{16,18},{18,... | collective-permute-start | bytes 393224 | tf_op jit(solution)/shard_map/ppermute | solution.py:314
  4.5 1.6 %collective-permute-start.1 = (bf16[2,2,128,128]{3,2,1,0:T(8,128)(2,1)S(1)}, bf16[2,2,128,128]{3,2,1,0:T(8,128)(2,1)S(1)}, u32[]{:S(2)}, u32[]{:S(2)}) collective-permute-start(bf16[2,2,128,128]{3,2,1,0:T(8,128)(2,1)S(1)} %get-tuple-element.55), channel_id=1, source_target_pairs={{0,8},{2,10},{4,12},{6,14},{8,0},{10,2},{12,4},{14,6},{16,24},{18,... | collective-permute-start | bytes 393224 | tf_op jit(solution)/shard_map/ppermute | solution.py:314
  6.1 2.3 %pick_head.2.refs_8_ = bf16[1024,512]{1,0:T(8,128)(2,1)S(1)} custom-call(bf16[2,1024,4,512]{3,2,1,0:T(4,128)(2,1)} %w_ref.3), custom_call_target="tpu_custom_call" | custom-call | tf_op jit(solution)/shard_map/pick_head/pallas_call | solution.py:355
  8.5 2.4 %collective-permute-done.1.refs_2_ = bf16[2,2,128,128]{3,2,1,0:T(8,128)(2,1)S(1)} collective-permute-done((bf16[2,2,128,128]{3,2,1,0:T(8,128)(2,1)S(1)}, bf16[2,2,128,128]{3,2,1,0:T(8,128)(2,1)S(1)}, u32[]{:S(2)}, u32[]{:S(2)}) %collective-permute-start.1) | collective-permute-done | bytes 131104 | tf_op jit(solution)/shard_map/ppermute | solution.py:314
  10.9 1.2 %collective-permute-done.2.refs_3_ = bf16[2,2,128,128]{3,2,1,0:T(8,128)(2,1)S(1)} collective-permute-done((bf16[2,2,128,128]{3,2,1,0:T(8,128)(2,1)S(1)}, bf16[2,2,128,128]{3,2,1,0:T(8,128)(2,1)S(1)}, u32[]{:S(2)}, u32[]{:S(2)}) %collective-permute-start.2) | collective-permute-done | bytes 131104 | tf_op jit(solution)/shard_map/ppermute | solution.py:314
  12.1 2.8 %collective-permute-start.5 = (bf16[4,2,128,128]{3,2,1,0:T(8,128)(2,1)S(1)}, bf16[4,2,128,128]{3,2,1,0:T(8,128)(2,1)S(1)}, u32[]{:S(2)}, u32[]{:S(2)}) collective-permute-start(bf16[4,2,128,128]{3,2,1,0:T(8,128)(2,1)S(1)} %get-tuple-element.61.refs_6_), channel_id=1, source_target_pairs={{0,16},{2,18},{4,20},{6,22},{8,24},{10,26},{12,28},{14,30},{16,0},... | collective-permute-start | bytes 786440 | tf_op jit(solution)/shard_map/ppermute | solution.py:314
  14.9 1.5 %collective-permute-start.6 = (bf16[4,2,128,128]{3,2,1,0:T(8,128)(2,1)S(1)}, bf16[4,2,128,128]{3,2,1,0:T(8,128)(2,1)S(1)}, u32[]{:S(2)}, u32[]{:S(2)}) collective-permute-start(bf16[4,2,128,128]{3,2,1,0:T(8,128)(2,1)S(1)} %get-tuple-element.61.refs_6_), channel_id=1, source_target_pairs={{0,4},{2,6},{4,0},{6,2},{8,12},{10,14},{12,8},{14,10},{16,20},{18,... | collective-permute-start | bytes 786440 | tf_op jit(solution)/shard_map/ppermute | solution.py:314
  16.5 2.5 %collective-permute-start.8 = (bf16[64,1024]{1,0:T(8,128)(2,1)S(1)}, bf16[64,1024]{1,0:T(8,128)(2,1)S(1)}, u32[]{:S(2)}, u32[]{:S(2)}) collective-permute-start(bf16[64,1024]{1,0:T(8,128)(2,1)S(1)} %copy-done.2), channel_id=1, source_target_pairs={{0,10},{2,8},{4,14},{6,12},{8,2},{10,0},{12,6},{14,4},{16,26},{18,... | collective-permute-start | bytes 393224 | tf_op jit(solution)/shard_map/ppermute | solution.py:314
  20.0 6.1 %collective-permute-done.5.refs_8_ = bf16[4,2,128,128]{3,2,1,0:T(8,128)(2,1)S(1)} collective-permute-done((bf16[4,2,128,128]{3,2,1,0:T(8,128)(2,1)S(1)}, bf16[4,2,128,128]{3,2,1,0:T(8,128)(2,1)S(1)}, u32[]{:S(2)}, u32[]{:S(2)}) %collective-permute-start.5) | collective-permute-done | bytes 262176 | tf_op jit(solution)/shard_map/ppermute | solution.py:314
  26.1 1.6 %collective-permute-start.12 = (bf16[4,2,128,128]{3,2,1,0:T(8,128)(2,1)S(1)}, bf16[4,2,128,128]{3,2,1,0:T(8,128)(2,1)S(1)}, u32[]{:S(2)}, u32[]{:S(2)}) collective-permute-start(bf16[4,2,128,128]{3,2,1,0:T(8,128)(2,1)S(1)} %collective-permute-done.5.refs_8_), channel_id=1, source_target_pairs={{0,4},{2,6},{4,0},{6,2},{8,12},{10,14},{12,8},{14,10},{16,20},{18,... | collective-permute-start | bytes 786440 | tf_op jit(solution)/shard_map/ppermute | solution.py:314
  31.0 1.7 %attend.2 = (bf16[512,256]{1,0:T(8,128)(2,1)S(1)}, f32[512,128]{1,0:T(8,128)S(1)}) custom-call(s32[16]{0:T(128)S(1)} %copy-done.3, s32[16]{0:T(128)S(1)} %copy-done.4, s32[4]{0:T(128)S(1)} %copy-done.5, s32[4]{0:T(128)S(1)} %copy-done.6, bf16[512,128]{1,0:T(8,128)(2,1)S(1)} %get-tuple-element.69.refs_4_, f32[512,128]{1,0:T(8,128)S(1)} %get-tuple-element.70.refs_5_, ...), custom_call_target="tpu_custom_call" | custom-call | tf_op jit(solution)/shard_map/attend/pallas_call | solution.py:355
  32.7 2.6 %collective-permute-done.12.refs_6_ = bf16[4,2,128,128]{3,2,1,0:T(8,128)(2,1)S(1)} collective-permute-done((bf16[4,2,128,128]{3,2,1,0:T(8,128)(2,1)S(1)}, bf16[4,2,128,128]{3,2,1,0:T(8,128)(2,1)S(1)}, u32[]{:S(2)}, u32[]{:S(2)}) %collective-permute-start.12) | collective-permute-done | bytes 262176 | tf_op jit(solution)/shard_map/ppermute | solution.py:314
  35.3 1.3 %finish.2.refs_0_ = bf16[512,128]{1,0:T(8,128)(2,1)S(1)} custom-call(s32[16]{0:T(128)S(1)} %copy-done.3, s32[16]{0:T(128)S(1)} %copy-done.4, s32[4]{0:T(128)S(1)} %copy-done.5, bf16[512,256]{1,0:T(8,128)(2,1)S(1)} %get-tuple-element.72.refs_3_, f32[512,128]{1,0:T(8,128)S(1)} %get-tuple-element.73.refs_4_, bf16[512,128]{1,0:T(8,128)(2,1)S(1)} %get-tuple-element.74.refs_5_, ...), custom_call_target="tpu_custom_call" | custom-call | tf_op jit(solution)/shard_map/finish/pallas_call | solution.py:355
  37.8 2.4 %collective-permute-start.13 = (bf16[512,128]{1,0:T(8,128)(2,1)S(1)}, bf16[512,128]{1,0:T(8,128)(2,1)S(1)}, u32[]{:S(2)}, u32[]{:S(2)}) collective-permute-start(bf16[512,128]{1,0:T(8,128)(2,1)S(1)} %finish.2.refs_0_), channel_id=1, source_target_pairs={{0,10},{2,8},{4,14},{6,12},{8,2},{10,0},{12,6},{14,4},{16,26},{18,... | collective-permute-start | bytes 393224 | tf_op jit(solution)/shard_map/ppermute | solution.py:314
  40.2 3.6 %collective-permute-done.16.i_ref = bf16[4,2,128,128]{3,2,1,0:T(8,128)(2,1)S(1)} collective-permute-done((bf16[4,2,128,128]{3,2,1,0:T(8,128)(2,1)S(1)}, bf16[4,2,128,128]{3,2,1,0:T(8,128)(2,1)S(1)}, u32[]{:S(2)}, u32[]{:S(2)}) %collective-permute-start.16) | collective-permute-done | bytes 262176 | tf_op jit(solution)/shard_map/ppermute | solution.py:314
  44.5 2.3 %pick_head.3.refs_3_ = bf16[1024,512]{1,0:T(8,128)(2,1)S(1)} custom-call(bf16[2,1024,4,512]{3,2,1,0:T(4,128)(2,1)} %w_ref.3), custom_call_target="tpu_custom_call" | custom-call | tf_op jit(solution)/shard_map/pick_head/pallas_call | solution.py:355
  47.5 1.2 %collective-permute-done.13.refs_0_ = bf16[512,128]{1,0:T(8,128)(2,1)S(1)} collective-permute-done((bf16[512,128]{1,0:T(8,128)(2,1)S(1)}, bf16[512,128]{1,0:T(8,128)(2,1)S(1)}, u32[]{:S(2)}, u32[]{:S(2)}) %collective-permute-start.13) | collective-permute-done | bytes 131104 | tf_op jit(solution)/shard_map/ppermute | solution.py:314
  49.2 1.2 %collective-permute-start.20 = (bf16[2,2,128,128]{3,2,1,0:T(8,128)(2,1)S(1)}, bf16[2,2,128,128]{3,2,1,0:T(8,128)(2,1)S(1)}, u32[]{:S(2)}, u32[]{:S(2)}) collective-permute-start(bf16[2,2,128,128]{3,2,1,0:T(8,128)(2,1)S(1)} %get-tuple-element.90.refs_9_), channel_id=1, source_target_pairs={{0,4},{2,6},{4,0},{6,2},{8,12},{10,14},{12,8},{14,10},{16,20},{18,... | collective-permute-start | bytes 393224 | tf_op jit(solution)/shard_map/ppermute | solution.py:314
  50.4 1.4 %collective-permute-done.19.refs_1_ = bf16[512,1024]{1,0:T(8,128)(2,1)S(1)} collective-permute-done((bf16[512,1024]{1,0:T(8,128)(2,1)S(1)}, bf16[512,1024]{1,0:T(8,128)(2,1)S(1)}, u32[]{:S(2)}, u32[]{:S(2)}) %collective-permute-start.19) | collective-permute-done | bytes 1048608 | tf_op jit(solution)/shard_map/ppermute | solution.py:336
  52.8 1.8 %attend.3 = (bf16[512,256]{1,0:T(8,128)(2,1)S(1)}, f32[512,128]{1,0:T(8,128)S(1)}) custom-call(s32[16]{0:T(128)S(1)} %copy-done.3, s32[16]{0:T(128)S(1)} %copy-done.4, s32[4]{0:T(128)S(1)} %copy-done.5, s32[4]{0:T(128)S(1)} %copy-done.6, bf16[512,128]{1,0:T(8,128)(2,1)S(1)} %get-tuple-element.87.refs_4_, f32[512,128]{1,0:T(8,128)S(1)} %get-tuple-element.88.refs_5_, ...), custom_call_target="tpu_custom_call" | custom-call | tf_op jit(solution)/shard_map/attend/pallas_call | solution.py:355
  56.3 2.1 %collective-permute-start.21 = (bf16[128,128]{1,0:T(8,128)(2,1)S(1)}, bf16[128,128]{1,0:T(8,128)(2,1)S(1)}, u32[]{:S(2)}, u32[]{:S(2)}) collective-permute-start(bf16[128,128]{1,0:T(8,128)(2,1)S(1)} %get-tuple-element.96), channel_id=1, source_target_pairs={{0,2},{2,0},{4,6},{6,4},{8,10},{10,8},{12,14},{14,12},{16,18},{18,... | collective-permute-start | bytes 98312 | tf_op jit(solution)/shard_map/ppermute | solution.py:314
  58.5 1.5 %collective-permute-start.23 = (bf16[128,128]{1,0:T(8,128)(2,1)S(1)}, bf16[128,128]{1,0:T(8,128)(2,1)S(1)}, u32[]{:S(2)}, u32[]{:S(2)}) collective-permute-start(bf16[128,128]{1,0:T(8,128)(2,1)S(1)} %get-tuple-element.98), channel_id=1, source_target_pairs={{0,10},{2,8},{4,14},{6,12},{8,2},{10,0},{12,6},{14,4},{16,26},{18,... | collective-permute-start | bytes 98312 | tf_op jit(solution)/shard_map/ppermute | solution.py:314
  60.4 2.0 %collective-permute-done.22.refs_2_ = bf16[128,128]{1,0:T(8,128)(2,1)S(1)} collective-permute-done((bf16[128,128]{1,0:T(8,128)(2,1)S(1)}, bf16[128,128]{1,0:T(8,128)(2,1)S(1)}, u32[]{:S(2)}, u32[]{:S(2)}) %collective-permute-start.22) | collective-permute-done | bytes 32800 | tf_op jit(solution)/shard_map/ppermute | solution.py:314
  63.7 1.3 %collective-permute-done.24.refs_2_ = bf16[64,1024]{1,0:T(8,128)(2,1)S(1)} collective-permute-done((bf16[64,1024]{1,0:T(8,128)(2,1)S(1)}, bf16[64,1024]{1,0:T(8,128)(2,1)S(1)}, u32[]{:S(2)}, u32[]{:S(2)}) %collective-permute-start.24) | collective-permute-done | bytes 131104 | tf_op jit(solution)/shard_map/ppermute | solution.py:336
  (55 shorter events, 13.9 us)
Async XLA Ops:
  1.5 7.0 %collective-permute-start = (bf16[2,2,128,128]{3,2,1,0:T(8,128)(2,1)S(1)}, bf16[2,2,128,128]{3,2,1,0:T(8,128)(2,1)S(1)}, u32[]{:S(2)}, u32[]{:S(2)}) collective-permute-start(bf16[2,2,128,128]{3,2,1,0:T(8,128)(2,1)S(1)} %get-tuple-element.54), channel_id=1, source_target_pairs={{0,2},{2,0},{4,6},{6,4},{8,10},{10,8},{12,14},{14,12},{16,18},{18,... | collective-permute-start | bytes 393224 | tf_op jit(solution)/shard_map/ppermute | solution.py:314
  4.5 6.4 %collective-permute-start.1 = (bf16[2,2,128,128]{3,2,1,0:T(8,128)(2,1)S(1)}, bf16[2,2,128,128]{3,2,1,0:T(8,128)(2,1)S(1)}, u32[]{:S(2)}, u32[]{:S(2)}) collective-permute-start(bf16[2,2,128,128]{3,2,1,0:T(8,128)(2,1)S(1)} %get-tuple-element.55), channel_id=1, source_target_pairs={{0,8},{2,10},{4,12},{6,14},{8,0},{10,2},{12,4},{14,6},{16,24},{18,... | collective-permute-start | bytes 393224 | tf_op jit(solution)/shard_map/ppermute | solution.py:314
  6.1 6.0 %collective-permute-start.2 = (bf16[2,2,128,128]{3,2,1,0:T(8,128)(2,1)S(1)}, bf16[2,2,128,128]{3,2,1,0:T(8,128)(2,1)S(1)}, u32[]{:S(2)}, u32[]{:S(2)}) collective-permute-start(bf16[2,2,128,128]{3,2,1,0:T(8,128)(2,1)S(1)} %get-tuple-element.56), channel_id=1, source_target_pairs={{0,10},{2,8},{4,14},{6,12},{8,2},{10,0},{12,6},{14,4},{16,26},{18,... | collective-permute-start | bytes 393224 | tf_op jit(solution)/shard_map/ppermute | solution.py:314
  6.1 6.0 %collective-permute-start.3 = (bf16[64,1024]{1,0:T(8,128)(2,1)}, bf16[64,1024]{1,0:T(8,128)(2,1)S(1)}, u32[]{:S(2)}, u32[]{:S(2)}) collective-permute-start(bf16[64,1024]{1,0:T(8,128)(2,1)} %refs_0_.4), channel_id=1, source_target_pairs={{0,1},{1,0},{2,3},{3,2},{4,5},{5,4},{6,7},{7,6},{8,9},{9,8},{10,11... | collective-permute-start | bytes 393224 | tf_op jit(solution)/shard_map/ppermute | solution.py:336
  12.1 14.0 %collective-permute-start.5 = (bf16[4,2,128,128]{3,2,1,0:T(8,128)(2,1)S(1)}, bf16[4,2,128,128]{3,2,1,0:T(8,128)(2,1)S(1)}, u32[]{:S(2)}, u32[]{:S(2)}) collective-permute-start(bf16[4,2,128,128]{3,2,1,0:T(8,128)(2,1)S(1)} %get-tuple-element.61.refs_6_), channel_id=1, source_target_pairs={{0,16},{2,18},{4,20},{6,22},{8,24},{10,26},{12,28},{14,30},{16,0},... | collective-permute-start | bytes 786440 | tf_op jit(solution)/shard_map/ppermute | solution.py:314
  14.9 11.1 %collective-permute-start.6 = (bf16[4,2,128,128]{3,2,1,0:T(8,128)(2,1)S(1)}, bf16[4,2,128,128]{3,2,1,0:T(8,128)(2,1)S(1)}, u32[]{:S(2)}, u32[]{:S(2)}) collective-permute-start(bf16[4,2,128,128]{3,2,1,0:T(8,128)(2,1)S(1)} %get-tuple-element.61.refs_6_), channel_id=1, source_target_pairs={{0,4},{2,6},{4,0},{6,2},{8,12},{10,14},{12,8},{14,10},{16,20},{18,... | collective-permute-start | bytes 786440 | tf_op jit(solution)/shard_map/ppermute | solution.py:314
  16.5 11.2 %collective-permute-start.8 = (bf16[64,1024]{1,0:T(8,128)(2,1)S(1)}, bf16[64,1024]{1,0:T(8,128)(2,1)S(1)}, u32[]{:S(2)}, u32[]{:S(2)}) collective-permute-start(bf16[64,1024]{1,0:T(8,128)(2,1)S(1)} %copy-done.2), channel_id=1, source_target_pairs={{0,10},{2,8},{4,14},{6,12},{8,2},{10,0},{12,6},{14,4},{16,26},{18,... | collective-permute-start | bytes 393224 | tf_op jit(solution)/shard_map/ppermute | solution.py:314
  19.0 9.5 %collective-permute-start.7 = (bf16[64,1024]{1,0:T(8,128)(2,1)S(1)}, bf16[64,1024]{1,0:T(8,128)(2,1)S(1)}, u32[]{:S(2)}, u32[]{:S(2)}) collective-permute-start(bf16[64,1024]{1,0:T(8,128)(2,1)S(1)} %copy-done.2), channel_id=1, source_target_pairs={{0,8},{2,10},{4,12},{6,14},{8,0},{10,2},{12,4},{14,6},{16,24},{18,... | collective-permute-start | bytes 393224 | tf_op jit(solution)/shard_map/ppermute | solution.py:314
  19.4 9.0 %collective-permute-start.4 = (bf16[64,1024]{1,0:T(8,128)(2,1)S(1)}, bf16[64,1024]{1,0:T(8,128)(2,1)S(1)}, u32[]{:S(2)}, u32[]{:S(2)}) collective-permute-start(bf16[64,1024]{1,0:T(8,128)(2,1)S(1)} %copy-done.2), channel_id=1, source_target_pairs={{0,2},{2,0},{4,6},{6,4},{8,10},{10,8},{12,14},{14,12},{16,18},{18,... | collective-permute-start | bytes 393224 | tf_op jit(solution)/shard_map/ppermute | solution.py:314
  26.1 9.2 %collective-permute-start.12 = (bf16[4,2,128,128]{3,2,1,0:T(8,128)(2,1)S(1)}, bf16[4,2,128,128]{3,2,1,0:T(8,128)(2,1)S(1)}, u32[]{:S(2)}, u32[]{:S(2)}) collective-permute-start(bf16[4,2,128,128]{3,2,1,0:T(8,128)(2,1)S(1)} %collective-permute-done.5.refs_8_), channel_id=1, source_target_pairs={{0,4},{2,6},{4,0},{6,2},{8,12},{10,14},{12,8},{14,10},{16,20},{18,... | collective-permute-start | bytes 786440 | tf_op jit(solution)/shard_map/ppermute | solution.py:314
  27.7 1.3 %collective-permute-start.11 = (bf16[64,1024]{1,0:T(8,128)(2,1)S(1)}, bf16[64,1024]{1,0:T(8,128)(2,1)S(1)}, u32[]{:S(2)}, u32[]{:S(2)}) collective-permute-start(bf16[64,1024]{1,0:T(8,128)(2,1)S(1)} %collective-permute-done.8.refs_3_), channel_id=1, source_target_pairs={{0,1},{1,0},{2,3},{3,2},{4,5},{5,4},{6,7},{7,6},{8,9},{9,8},{10,11... | collective-permute-start | bytes 393224 | tf_op jit(solution)/shard_map/ppermute | solution.py:336
  28.5 1.5 %collective-permute-start.9 = (bf16[64,1024]{1,0:T(8,128)(2,1)S(1)}, bf16[64,1024]{1,0:T(8,128)(2,1)S(1)}, u32[]{:S(2)}, u32[]{:S(2)}) collective-permute-start(bf16[64,1024]{1,0:T(8,128)(2,1)S(1)} %collective-permute-done.4.refs_1_), channel_id=1, source_target_pairs={{0,1},{1,0},{2,3},{3,2},{4,5},{5,4},{6,7},{7,6},{8,9},{9,8},{10,11... | collective-permute-start | bytes 393224 | tf_op jit(solution)/shard_map/ppermute | solution.py:336
  29.0 14.8 %collective-permute-start.16 = (bf16[4,2,128,128]{3,2,1,0:T(8,128)(2,1)S(1)}, bf16[4,2,128,128]{3,2,1,0:T(8,128)(2,1)S(1)}, u32[]{:S(2)}, u32[]{:S(2)}) collective-permute-start(bf16[4,2,128,128]{3,2,1,0:T(8,128)(2,1)S(1)} %get-tuple-element.76.refs_6_), channel_id=1, source_target_pairs={{0,16},{2,18},{4,20},{6,22},{8,24},{10,26},{12,28},{14,30},{16,0},... | collective-permute-start | bytes 786440 | tf_op jit(solution)/shard_map/ppermute | solution.py:314
  29.0 14.8 %collective-permute-start.17 = (bf16[4,2,128,128]{3,2,1,0:T(8,128)(2,1)S(1)}, bf16[4,2,128,128]{3,2,1,0:T(8,128)(2,1)S(1)}, u32[]{:S(2)}, u32[]{:S(2)}) collective-permute-start(bf16[4,2,128,128]{3,2,1,0:T(8,128)(2,1)S(1)} %get-tuple-element.76.refs_6_), channel_id=1, source_target_pairs={{0,4},{2,6},{4,0},{6,2},{8,12},{10,14},{12,8},{14,10},{16,20},{18,... | collective-permute-start | bytes 786440 | tf_op jit(solution)/shard_map/ppermute | solution.py:314
  36.6 7.2 %collective-permute-start.14 = (bf16[512,128]{1,0:T(8,128)(2,1)S(1)}, bf16[512,128]{1,0:T(8,128)(2,1)S(1)}, u32[]{:S(2)}, u32[]{:S(2)}) collective-permute-start(bf16[512,128]{1,0:T(8,128)(2,1)S(1)} %finish.2.refs_0_), channel_id=1, source_target_pairs={{0,2},{2,0},{4,6},{6,4},{8,10},{10,8},{12,14},{14,12},{16,18},{18,... | collective-permute-start | bytes 393224 | tf_op jit(solution)/shard_map/ppermute | solution.py:314
  36.8 10.0 %collective-permute-start.15 = (bf16[512,128]{1,0:T(8,128)(2,1)S(1)}, bf16[512,128]{1,0:T(8,128)(2,1)S(1)}, u32[]{:S(2)}, u32[]{:S(2)}) collective-permute-start(bf16[512,128]{1,0:T(8,128)(2,1)S(1)} %finish.2.refs_0_), channel_id=1, source_target_pairs={{0,8},{2,10},{4,12},{6,14},{8,0},{10,2},{12,4},{14,6},{16,24},{18,... | collective-permute-start | bytes 393224 | tf_op jit(solution)/shard_map/ppermute | solution.py:314
  37.8 10.9 %collective-permute-start.13 = (bf16[512,128]{1,0:T(8,128)(2,1)S(1)}, bf16[512,128]{1,0:T(8,128)(2,1)S(1)}, u32[]{:S(2)}, u32[]{:S(2)}) collective-permute-start(bf16[512,128]{1,0:T(8,128)(2,1)S(1)} %finish.2.refs_0_), channel_id=1, source_target_pairs={{0,10},{2,8},{4,14},{6,12},{8,2},{10,0},{12,6},{14,4},{16,26},{18,... | collective-permute-start | bytes 393224 | tf_op jit(solution)/shard_map/ppermute | solution.py:314
  43.8 5.4 %collective-permute-start.18 = (bf16[2,2,128,128]{3,2,1,0:T(8,128)(2,1)S(1)}, bf16[2,2,128,128]{3,2,1,0:T(8,128)(2,1)S(1)}, u32[]{:S(2)}, u32[]{:S(2)}) collective-permute-start(bf16[2,2,128,128]{3,2,1,0:T(8,128)(2,1)S(1)} %get-tuple-element.89.refs_8_), channel_id=1, source_target_pairs={{0,4},{2,6},{4,0},{6,2},{8,12},{10,14},{12,8},{14,10},{16,20},{18,... | collective-permute-start | bytes 393224 | tf_op jit(solution)/shard_map/ppermute | solution.py:314
  49.2 2.7 %collective-permute-start.19 = (bf16[512,1024]{1,0:T(8,128)(2,1)S(1)}, bf16[512,1024]{1,0:T(8,128)(2,1)S(1)}, u32[]{:S(2)}, u32[]{:S(2)}) collective-permute-start(bf16[512,1024]{1,0:T(8,128)(2,1)S(1)} %term.3.refs_0_), channel_id=1, source_target_pairs={{0,1},{1,0},{2,3},{3,2},{4,5},{5,4},{6,7},{7,6},{8,9},{9,8},{10,11... | collective-permute-start | bytes 3145736 | tf_op jit(solution)/shard_map/ppermute | solution.py:336
  49.2 5.9 %collective-permute-start.20 = (bf16[2,2,128,128]{3,2,1,0:T(8,128)(2,1)S(1)}, bf16[2,2,128,128]{3,2,1,0:T(8,128)(2,1)S(1)}, u32[]{:S(2)}, u32[]{:S(2)}) collective-permute-start(bf16[2,2,128,128]{3,2,1,0:T(8,128)(2,1)S(1)} %get-tuple-element.90.refs_9_), channel_id=1, source_target_pairs={{0,4},{2,6},{4,0},{6,2},{8,12},{10,14},{12,8},{14,10},{16,20},{18,... | collective-permute-start | bytes 393224 | tf_op jit(solution)/shard_map/ppermute | solution.py:314
  56.3 4.0 %collective-permute-start.21 = (bf16[128,128]{1,0:T(8,128)(2,1)S(1)}, bf16[128,128]{1,0:T(8,128)(2,1)S(1)}, u32[]{:S(2)}, u32[]{:S(2)}) collective-permute-start(bf16[128,128]{1,0:T(8,128)(2,1)S(1)} %get-tuple-element.96), channel_id=1, source_target_pairs={{0,2},{2,0},{4,6},{6,4},{8,10},{10,8},{12,14},{14,12},{16,18},{18,... | collective-permute-start | bytes 98312 | tf_op jit(solution)/shard_map/ppermute | solution.py:314
  58.5 3.9 %collective-permute-start.22 = (bf16[128,128]{1,0:T(8,128)(2,1)S(1)}, bf16[128,128]{1,0:T(8,128)(2,1)S(1)}, u32[]{:S(2)}, u32[]{:S(2)}) collective-permute-start(bf16[128,128]{1,0:T(8,128)(2,1)S(1)} %get-tuple-element.97), channel_id=1, source_target_pairs={{0,8},{2,10},{4,12},{6,14},{8,0},{10,2},{12,4},{14,6},{16,24},{18,... | collective-permute-start | bytes 98312 | tf_op jit(solution)/shard_map/ppermute | solution.py:314
  58.5 4.8 %collective-permute-start.23 = (bf16[128,128]{1,0:T(8,128)(2,1)S(1)}, bf16[128,128]{1,0:T(8,128)(2,1)S(1)}, u32[]{:S(2)}, u32[]{:S(2)}) collective-permute-start(bf16[128,128]{1,0:T(8,128)(2,1)S(1)} %get-tuple-element.98), channel_id=1, source_target_pairs={{0,10},{2,8},{4,14},{6,12},{8,2},{10,0},{12,6},{14,4},{16,26},{18,... | collective-permute-start | bytes 98312 | tf_op jit(solution)/shard_map/ppermute | solution.py:314
  63.6 1.4 %collective-permute-start.24 = (bf16[64,1024]{1,0:T(8,128)(2,1)S(1)}, bf16[64,1024]{1,0:T(8,128)(2,1)S(1)}, u32[]{:S(2)}, u32[]{:S(2)}) collective-permute-start(bf16[64,1024]{1,0:T(8,128)(2,1)S(1)} %get-tuple-element.100), channel_id=1, source_target_pairs={{0,1},{1,0},{2,3},{3,2},{4,5},{5,4},{6,7},{7,6},{8,9},{9,8},{10,11... | collective-permute-start | bytes 393224 | tf_op jit(solution)/shard_map/ppermute | solution.py:336
  (8 other events, 105.9 us)

commit v9 on v7

--- a/solution.py
+++ b/solution.py
@@ -477,7 +477,7 @@
             [SMEM_SPEC] * 3 + [VMEM_SPEC] * (len(operands) - 3),
         )
         if not last:
-            gated = trade_spots(list(gated) * spots, False)
+            gated = trade_spots(list(gated) * spots)
             next_weight = pick_head(layer_index + 1)
             if crossed:
                 whole = after(later[layer_index], far, near)

time: 65.9 us -> 65.9 us (level)
  no operation moved by 1% of the time
where the time goes in v9:
time: 65.9 us; the launch traced here: 65.8 us
  waiting for transfers between devices  25.6 us (39%)
  starting transfers between devices  23.6 us (36%)
  Pallas kernels  15.3 us (23%)
  local copies, waits for them, and re-layouts  1.08 us (2%)
    ppermute x19, starting transfers between devices, swap(): return lax.ppermute(value, 'users', [(u, u ^ mask) for u in range(chips)])  23 us
    ppermute x19, waiting for transfers between devices, swap(): return lax.ppermute(value, 'users', [(u, u ^ mask) for u in range(chips)])  21.8 us
    pallas_call x15, Pallas kernels, kernel_call(): pl.pallas_call(kernel, out_shape=[jax.ShapeDtypeStruct(*out) for out in o...  15.3 us
    ppermute x6, waiting for transfers between devices, shift_core(): return lax.ppermute(value, 'cand', pairs)  3.76 us
  transfers between devices with their start and end apart: 25, of which 16 were waited for; matrix products, arithmetic and copies ran while one was open for 0% of the time, Pallas kernels for 18%

profile of v9, /device:TPU:0, one launch (start us, length us, event | category | flops | bytes accessed | tf_op | source)
XLA Modules:
  0.0 65.8 jit_solution(9914676917432706909)
XLA Ops:
  1.5 3.0 %collective-permute-start = (bf16[2,2,128,128]{3,2,1,0:T(8,128)(2,1)S(1)}, bf16[2,2,128,128]{3,2,1,0:T(8,128)(2,1)S(1)}, u32[]{:S(2)}, u32[]{:S(2)}) collective-permute-start(bf16[2,2,128,128]{3,2,1,0:T(8,128)(2,1)S(1)} %get-tuple-element.54), channel_id=1, source_target_pairs={{0,2},{2,0},{4,6},{6,4},{8,10},{10,8},{12,14},{14,12},{16,18},{18,... | collective-permute-start | bytes 393224 | tf_op jit(solution)/shard_map/ppermute | solution.py:314
  4.5 1.6 %collective-permute-start.1 = (bf16[2,2,128,128]{3,2,1,0:T(8,128)(2,1)S(1)}, bf16[2,2,128,128]{3,2,1,0:T(8,128)(2,1)S(1)}, u32[]{:S(2)}, u32[]{:S(2)}) collective-permute-start(bf16[2,2,128,128]{3,2,1,0:T(8,128)(2,1)S(1)} %get-tuple-element.55), channel_id=1, source_target_pairs={{0,8},{2,10},{4,12},{6,14},{8,0},{10,2},{12,4},{14,6},{16,24},{18,... | collective-permute-start | bytes 393224 | tf_op jit(solution)/shard_map/ppermute | solution.py:314
  6.1 2.3 %pick_head.2.refs_8_ = bf16[1024,512]{1,0:T(8,128)(2,1)S(1)} custom-call(bf16[2,1024,4,512]{3,2,1,0:T(4,128)(2,1)} %w_ref.3), custom_call_target="tpu_custom_call" | custom-call | tf_op jit(solution)/shard_map/pick_head/pallas_call | solution.py:355
  8.5 2.4 %collective-permute-done.1.refs_2_ = bf16[2,2,128,128]{3,2,1,0:T(8,128)(2,1)S(1)} collective-permute-done((bf16[2,2,128,128]{3,2,1,0:T(8,128)(2,1)S(1)}, bf16[2,2,128,128]{3,2,1,0:T(8,128)(2,1)S(1)}, u32[]{:S(2)}, u32[]{:S(2)}) %collective-permute-start.1) | collective-permute-done | bytes 131104 | tf_op jit(solution)/shard_map/ppermute | solution.py:314
  10.9 1.2 %collective-permute-done.2.refs_3_ = bf16[2,2,128,128]{3,2,1,0:T(8,128)(2,1)S(1)} collective-permute-done((bf16[2,2,128,128]{3,2,1,0:T(8,128)(2,1)S(1)}, bf16[2,2,128,128]{3,2,1,0:T(8,128)(2,1)S(1)}, u32[]{:S(2)}, u32[]{:S(2)}) %collective-permute-start.2) | collective-permute-done | bytes 131104 | tf_op jit(solution)/shard_map/ppermute | solution.py:314
  12.1 2.8 %collective-permute-start.5 = (bf16[4,2,128,128]{3,2,1,0:T(8,128)(2,1)S(1)}, bf16[4,2,128,128]{3,2,1,0:T(8,128)(2,1)S(1)}, u32[]{:S(2)}, u32[]{:S(2)}) collective-permute-start(bf16[4,2,128,128]{3,2,1,0:T(8,128)(2,1)S(1)} %get-tuple-element.61.refs_6_), channel_id=1, source_target_pairs={{0,16},{2,18},{4,20},{6,22},{8,24},{10,26},{12,28},{14,30},{16,0},... | collective-permute-start | bytes 786440 | tf_op jit(solution)/shard_map/ppermute | solution.py:314
  14.9 1.5 %collective-permute-start.6 = (bf16[4,2,128,128]{3,2,1,0:T(8,128)(2,1)S(1)}, bf16[4,2,128,128]{3,2,1,0:T(8,128)(2,1)S(1)}, u32[]{:S(2)}, u32[]{:S(2)}) collective-permute-start(bf16[4,2,128,128]{3,2,1,0:T(8,128)(2,1)S(1)} %get-tuple-element.61.refs_6_), channel_id=1, source_target_pairs={{0,4},{2,6},{4,0},{6,2},{8,12},{10,14},{12,8},{14,10},{16,20},{18,... | collective-permute-start | bytes 786440 | tf_op jit(solution)/shard_map/ppermute | solution.py:314
  16.5 2.5 %collective-permute-start.8 = (bf16[64,1024]{1,0:T(8,128)(2,1)S(1)}, bf16[64,1024]{1,0:T(8,128)(2,1)S(1)}, u32[]{:S(2)}, u32[]{:S(2)}) collective-permute-start(bf16[64,1024]{1,0:T(8,128)(2,1)S(1)} %copy-done.2), channel_id=1, source_target_pairs={{0,10},{2,8},{4,14},{6,12},{8,2},{10,0},{12,6},{14,4},{16,26},{18,... | collective-permute-start | bytes 393224 | tf_op jit(solution)/shard_map/ppermute | solution.py:314
  20.0 6.1 %collective-permute-done.5.refs_8_ = bf16[4,2,128,128]{3,2,1,0:T(8,128)(2,1)S(1)} collective-permute-done((bf16[4,2,128,128]{3,2,1,0:T(8,128)(2,1)S(1)}, bf16[4,2,128,128]{3,2,1,0:T(8,128)(2,1)S(1)}, u32[]{:S(2)}, u32[]{:S(2)}) %collective-permute-start.5) | collective-permute-done | bytes 262176 | tf_op jit(solution)/shard_map/ppermute | solution.py:314
  26.1 1.6 %collective-permute-start.12 = (bf16[4,2,128,128]{3,2,1,0:T(8,128)(2,1)S(1)}, bf16[4,2,128,128]{3,2,1,0:T(8,128)(2,1)S(1)}, u32[]{:S(2)}, u32[]{:S(2)}) collective-permute-start(bf16[4,2,128,128]{3,2,1,0:T(8,128)(2,1)S(1)} %collective-permute-done.5.refs_8_), channel_id=1, source_target_pairs={{0,4},{2,6},{4,0},{6,2},{8,12},{10,14},{12,8},{14,10},{16,20},{18,... | collective-permute-start | bytes 786440 | tf_op jit(solution)/shard_map/ppermute | solution.py:314
  31.0 1.7 %attend.2 = (bf16[512,256]{1,0:T(8,128)(2,1)S(1)}, f32[512,128]{1,0:T(8,128)S(1)}) custom-call(s32[16]{0:T(128)S(1)} %copy-done.3, s32[16]{0:T(128)S(1)} %copy-done.4, s32[4]{0:T(128)S(1)} %copy-done.5, s32[4]{0:T(128)S(1)} %copy-done.6, bf16[512,128]{1,0:T(8,128)(2,1)S(1)} %get-tuple-element.69.refs_4_, f32[512,128]{1,0:T(8,128)S(1)} %get-tuple-element.70.refs_5_, ...), custom_call_target="tpu_custom_call" | custom-call | tf_op jit(solution)/shard_map/attend/pallas_call | solution.py:355
  32.7 2.6 %collective-permute-done.12.refs_6_ = bf16[4,2,128,128]{3,2,1,0:T(8,128)(2,1)S(1)} collective-permute-done((bf16[4,2,128,128]{3,2,1,0:T(8,128)(2,1)S(1)}, bf16[4,2,128,128]{3,2,1,0:T(8,128)(2,1)S(1)}, u32[]{:S(2)}, u32[]{:S(2)}) %collective-permute-start.12) | collective-permute-done | bytes 262176 | tf_op jit(solution)/shard_map/ppermute | solution.py:314
  35.3 1.3 %finish.2.refs_0_ = bf16[512,128]{1,0:T(8,128)(2,1)S(1)} custom-call(s32[16]{0:T(128)S(1)} %copy-done.3, s32[16]{0:T(128)S(1)} %copy-done.4, s32[4]{0:T(128)S(1)} %copy-done.5, bf16[512,256]{1,0:T(8,128)(2,1)S(1)} %get-tuple-element.72.refs_3_, f32[512,128]{1,0:T(8,128)S(1)} %get-tuple-element.73.refs_4_, bf16[512,128]{1,0:T(8,128)(2,1)S(1)} %get-tuple-element.74.refs_5_, ...), custom_call_target="tpu_custom_call" | custom-call | tf_op jit(solution)/shard_map/finish/pallas_call | solution.py:355
  37.8 2.4 %collective-permute-start.13 = (bf16[512,128]{1,0:T(8,128)(2,1)S(1)}, bf16[512,128]{1,0:T(8,128)(2,1)S(1)}, u32[]{:S(2)}, u32[]{:S(2)}) collective-permute-start(bf16[512,128]{1,0:T(8,128)(2,1)S(1)} %finish.2.refs_0_), channel_id=1, source_target_pairs={{0,10},{2,8},{4,14},{6,12},{8,2},{10,0},{12,6},{14,4},{16,26},{18,... | collective-permute-start | bytes 393224 | tf_op jit(solution)/shard_map/ppermute | solution.py:314
  40.2 3.6 %collective-permute-done.14.i_ref = bf16[4,2,128,128]{3,2,1,0:T(8,128)(2,1)S(1)} collective-permute-done((bf16[4,2,128,128]{3,2,1,0:T(8,128)(2,1)S(1)}, bf16[4,2,128,128]{3,2,1,0:T(8,128)(2,1)S(1)}, u32[]{:S(2)}, u32[]{:S(2)}) %collective-permute-start.14) | collective-permute-done | bytes 262176 | tf_op jit(solution)/shard_map/ppermute | solution.py:314
  44.5 2.3 %pick_head.3.refs_3_ = bf16[1024,512]{1,0:T(8,128)(2,1)S(1)} custom-call(bf16[2,1024,4,512]{3,2,1,0:T(4,128)(2,1)} %w_ref.3), custom_call_target="tpu_custom_call" | custom-call | tf_op jit(solution)/shard_map/pick_head/pallas_call | solution.py:355
  47.5 1.2 %collective-permute-done.13.refs_0_ = bf16[512,128]{1,0:T(8,128)(2,1)S(1)} collective-permute-done((bf16[512,128]{1,0:T(8,128)(2,1)S(1)}, bf16[512,128]{1,0:T(8,128)(2,1)S(1)}, u32[]{:S(2)}, u32[]{:S(2)}) %collective-permute-start.13) | collective-permute-done | bytes 131104 | tf_op jit(solution)/shard_map/ppermute | solution.py:314
  50.4 1.9 %collective-permute-done.19.refs_1_ = bf16[512,1024]{1,0:T(8,128)(2,1)S(1)} collective-permute-done((bf16[512,1024]{1,0:T(8,128)(2,1)S(1)}, bf16[512,1024]{1,0:T(8,128)(2,1)S(1)}, u32[]{:S(2)}, u32[]{:S(2)}) %collective-permute-start.19) | collective-permute-done | bytes 1048608 | tf_op jit(solution)/shard_map/ppermute | solution.py:336
  53.3 1.8 %attend.3 = (bf16[512,256]{1,0:T(8,128)(2,1)S(1)}, f32[512,128]{1,0:T(8,128)S(1)}) custom-call(s32[16]{0:T(128)S(1)} %copy-done.3, s32[16]{0:T(128)S(1)} %copy-done.4, s32[4]{0:T(128)S(1)} %copy-done.5, s32[4]{0:T(128)S(1)} %copy-done.6, bf16[512,128]{1,0:T(8,128)(2,1)S(1)} %get-tuple-element.87.refs_4_, f32[512,128]{1,0:T(8,128)S(1)} %get-tuple-element.88.refs_5_, ...), custom_call_target="tpu_custom_call" | custom-call | tf_op jit(solution)/shard_map/attend/pallas_call | solution.py:355
  55.6 1.2 %finish.3 = (bf16[128,128]{1,0:T(8,128)(2,1)S(1)}, bf16[128,128]{1,0:T(8,128)(2,1)S(1)}, bf16[128,128]{1,0:T(8,128)(2,1)S(1)}, bf16[128,128]{1,0:T(8,128)(2,1)S(1)}) custom-call(s32[16]{0:T(128)S(1)} %copy-done.3, s32[16]{0:T(128)S(1)} %copy-done.4, s32[4]{0:T(128)S(1)} %copy-done.5, bf16[512,256]{1,0:T(8,128)(2,1)S(1)} %get-tuple-element.92.refs_3_, ...), custom_call_target="tpu_custom_call" | custom-call | tf_op jit(solution)/shard_map/finish/pallas_call | solution.py:355
  56.8 1.6 %collective-permute-start.21 = (bf16[128,128]{1,0:T(8,128)(2,1)S(1)}, bf16[128,128]{1,0:T(8,128)(2,1)S(1)}, u32[]{:S(2)}, u32[]{:S(2)}) collective-permute-start(bf16[128,128]{1,0:T(8,128)(2,1)S(1)} %get-tuple-element.96), channel_id=1, source_target_pairs={{0,2},{2,0},{4,6},{6,4},{8,10},{10,8},{12,14},{14,12},{16,18},{18,... | collective-permute-start | bytes 98312 | tf_op jit(solution)/shard_map/ppermute | solution.py:314
  58.5 1.9 %collective-permute-start.23 = (bf16[128,128]{1,0:T(8,128)(2,1)S(1)}, bf16[128,128]{1,0:T(8,128)(2,1)S(1)}, u32[]{:S(2)}, u32[]{:S(2)}) collective-permute-start(bf16[128,128]{1,0:T(8,128)(2,1)S(1)} %get-tuple-element.98), channel_id=1, source_target_pairs={{0,10},{2,8},{4,14},{6,12},{8,2},{10,0},{12,6},{14,4},{16,26},{18,... | collective-permute-start | bytes 98312 | tf_op jit(solution)/shard_map/ppermute | solution.py:314
  60.8 1.6 %collective-permute-done.22.refs_2_ = bf16[128,128]{1,0:T(8,128)(2,1)S(1)} collective-permute-done((bf16[128,128]{1,0:T(8,128)(2,1)S(1)}, bf16[128,128]{1,0:T(8,128)(2,1)S(1)}, u32[]{:S(2)}, u32[]{:S(2)}) %collective-permute-start.22) | collective-permute-done | bytes 32800 | tf_op jit(solution)/shard_map/ppermute | solution.py:314
  63.7 1.3 %collective-permute-done.24.refs_2_ = bf16[64,1024]{1,0:T(8,128)(2,1)S(1)} collective-permute-done((bf16[64,1024]{1,0:T(8,128)(2,1)S(1)}, bf16[64,1024]{1,0:T(8,128)(2,1)S(1)}, u32[]{:S(2)}, u32[]{:S(2)}) %collective-permute-start.24) | collective-permute-done | bytes 131104 | tf_op jit(solution)/shard_map/ppermute | solution.py:336
  (55 shorter events, 14.0 us)
Async XLA Ops:
  1.5 7.0 %collective-permute-start = (bf16[2,2,128,128]{3,2,1,0:T(8,128)(2,1)S(1)}, bf16[2,2,128,128]{3,2,1,0:T(8,128)(2,1)S(1)}, u32[]{:S(2)}, u32[]{:S(2)}) collective-permute-start(bf16[2,2,128,128]{3,2,1,0:T(8,128)(2,1)S(1)} %get-tuple-element.54), channel_id=1, source_target_pairs={{0,2},{2,0},{4,6},{6,4},{8,10},{10,8},{12,14},{14,12},{16,18},{18,... | collective-permute-start | bytes 393224 | tf_op jit(solution)/shard_map/ppermute | solution.py:314
  4.5 6.4 %collective-permute-start.1 = (bf16[2,2,128,128]{3,2,1,0:T(8,128)(2,1)S(1)}, bf16[2,2,128,128]{3,2,1,0:T(8,128)(2,1)S(1)}, u32[]{:S(2)}, u32[]{:S(2)}) collective-permute-start(bf16[2,2,128,128]{3,2,1,0:T(8,128)(2,1)S(1)} %get-tuple-element.55), channel_id=1, source_target_pairs={{0,8},{2,10},{4,12},{6,14},{8,0},{10,2},{12,4},{14,6},{16,24},{18,... | collective-permute-start | bytes 393224 | tf_op jit(solution)/shard_map/ppermute | solution.py:314
  6.1 6.0 %collective-permute-start.2 = (bf16[2,2,128,128]{3,2,1,0:T(8,128)(2,1)S(1)}, bf16[2,2,128,128]{3,2,1,0:T(8,128)(2,1)S(1)}, u32[]{:S(2)}, u32[]{:S(2)}) collective-permute-start(bf16[2,2,128,128]{3,2,1,0:T(8,128)(2,1)S(1)} %get-tuple-element.56), channel_id=1, source_target_pairs={{0,10},{2,8},{4,14},{6,12},{8,2},{10,0},{12,6},{14,4},{16,26},{18,... | collective-permute-start | bytes 393224 | tf_op jit(solution)/shard_map/ppermute | solution.py:314
  6.1 6.0 %collective-permute-start.3 = (bf16[64,1024]{1,0:T(8,128)(2,1)}, bf16[64,1024]{1,0:T(8,128)(2,1)S(1)}, u32[]{:S(2)}, u32[]{:S(2)}) collective-permute-start(bf16[64,1024]{1,0:T(8,128)(2,1)} %refs_0_.4), channel_id=1, source_target_pairs={{0,1},{1,0},{2,3},{3,2},{4,5},{5,4},{6,7},{7,6},{8,9},{9,8},{10,11... | collective-permute-start | bytes 393224 | tf_op jit(solution)/shard_map/ppermute | solution.py:336
  12.1 14.0 %collective-permute-start.5 = (bf16[4,2,128,128]{3,2,1,0:T(8,128)(2,1)S(1)}, bf16[4,2,128,128]{3,2,1,0:T(8,128)(2,1)S(1)}, u32[]{:S(2)}, u32[]{:S(2)}) collective-permute-start(bf16[4,2,128,128]{3,2,1,0:T(8,128)(2,1)S(1)} %get-tuple-element.61.refs_6_), channel_id=1, source_target_pairs={{0,16},{2,18},{4,20},{6,22},{8,24},{10,26},{12,28},{14,30},{16,0},... | collective-permute-start | bytes 786440 | tf_op jit(solution)/shard_map/ppermute | solution.py:314
  14.9 11.1 %collective-permute-start.6 = (bf16[4,2,128,128]{3,2,1,0:T(8,128)(2,1)S(1)}, bf16[4,2,128,128]{3,2,1,0:T(8,128)(2,1)S(1)}, u32[]{:S(2)}, u32[]{:S(2)}) collective-permute-start(bf16[4,2,128,128]{3,2,1,0:T(8,128)(2,1)S(1)} %get-tuple-element.61.refs_6_), channel_id=1, source_target_pairs={{0,4},{2,6},{4,0},{6,2},{8,12},{10,14},{12,8},{14,10},{16,20},{18,... | collective-permute-start | bytes 786440 | tf_op jit(solution)/shard_map/ppermute | solution.py:314
  16.5 11.2 %collective-permute-start.8 = (bf16[64,1024]{1,0:T(8,128)(2,1)S(1)}, bf16[64,1024]{1,0:T(8,128)(2,1)S(1)}, u32[]{:S(2)}, u32[]{:S(2)}) collective-permute-start(bf16[64,1024]{1,0:T(8,128)(2,1)S(1)} %copy-done.2), channel_id=1, source_target_pairs={{0,10},{2,8},{4,14},{6,12},{8,2},{10,0},{12,6},{14,4},{16,26},{18,... | collective-permute-start | bytes 393224 | tf_op jit(solution)/shard_map/ppermute | solution.py:314
  19.0 9.5 %collective-permute-start.7 = (bf16[64,1024]{1,0:T(8,128)(2,1)S(1)}, bf16[64,1024]{1,0:T(8,128)(2,1)S(1)}, u32[]{:S(2)}, u32[]{:S(2)}) collective-permute-start(bf16[64,1024]{1,0:T(8,128)(2,1)S(1)} %copy-done.2), channel_id=1, source_target_pairs={{0,8},{2,10},{4,12},{6,14},{8,0},{10,2},{12,4},{14,6},{16,24},{18,... | collective-permute-start | bytes 393224 | tf_op jit(solution)/shard_map/ppermute | solution.py:314
  19.4 9.0 %collective-permute-start.4 = (bf16[64,1024]{1,0:T(8,128)(2,1)S(1)}, bf16[64,1024]{1,0:T(8,128)(2,1)S(1)}, u32[]{:S(2)}, u32[]{:S(2)}) collective-permute-start(bf16[64,1024]{1,0:T(8,128)(2,1)S(1)} %copy-done.2), channel_id=1, source_target_pairs={{0,2},{2,0},{4,6},{6,4},{8,10},{10,8},{12,14},{14,12},{16,18},{18,... | collective-permute-start | bytes 393224 | tf_op jit(solution)/shard_map/ppermute | solution.py:314
  26.1 9.2 %collective-permute-start.12 = (bf16[4,2,128,128]{3,2,1,0:T(8,128)(2,1)S(1)}, bf16[4,2,128,128]{3,2,1,0:T(8,128)(2,1)S(1)}, u32[]{:S(2)}, u32[]{:S(2)}) collective-permute-start(bf16[4,2,128,128]{3,2,1,0:T(8,128)(2,1)S(1)} %collective-permute-done.5.refs_8_), channel_id=1, source_target_pairs={{0,4},{2,6},{4,0},{6,2},{8,12},{10,14},{12,8},{14,10},{16,20},{18,... | collective-permute-start | bytes 786440 | tf_op jit(solution)/shard_map/ppermute | solution.py:314
  27.7 1.3 %collective-permute-start.11 = (bf16[64,1024]{1,0:T(8,128)(2,1)S(1)}, bf16[64,1024]{1,0:T(8,128)(2,1)S(1)}, u32[]{:S(2)}, u32[]{:S(2)}) collective-permute-start(bf16[64,1024]{1,0:T(8,128)(2,1)S(1)} %collective-permute-done.8.refs_3_), channel_id=1, source_target_pairs={{0,1},{1,0},{2,3},{3,2},{4,5},{5,4},{6,7},{7,6},{8,9},{9,8},{10,11... | collective-permute-start | bytes 393224 | tf_op jit(solution)/shard_map/ppermute | solution.py:336
  28.5 1.5 %collective-permute-start.9 = (bf16[64,1024]{1,0:T(8,128)(2,1)S(1)}, bf16[64,1024]{1,0:T(8,128)(2,1)S(1)}, u32[]{:S(2)}, u32[]{:S(2)}) collective-permute-start(bf16[64,1024]{1,0:T(8,128)(2,1)S(1)} %collective-permute-done.4.refs_1_), channel_id=1, source_target_pairs={{0,1},{1,0},{2,3},{3,2},{4,5},{5,4},{6,7},{7,6},{8,9},{9,8},{10,11... | collective-permute-start | bytes 393224 | tf_op jit(solution)/shard_map/ppermute | solution.py:336
  29.0 14.8 %collective-permute-start.14 = (bf16[4,2,128,128]{3,2,1,0:T(8,128)(2,1)S(1)}, bf16[4,2,128,128]{3,2,1,0:T(8,128)(2,1)S(1)}, u32[]{:S(2)}, u32[]{:S(2)}) collective-permute-start(bf16[4,2,128,128]{3,2,1,0:T(8,128)(2,1)S(1)} %get-tuple-element.76.refs_6_), channel_id=1, source_target_pairs={{0,16},{2,18},{4,20},{6,22},{8,24},{10,26},{12,28},{14,30},{16,0},... | collective-permute-start | bytes 786440 | tf_op jit(solution)/shard_map/ppermute | solution.py:314
  29.0 14.8 %collective-permute-start.15 = (bf16[4,2,128,128]{3,2,1,0:T(8,128)(2,1)S(1)}, bf16[4,2,128,128]{3,2,1,0:T(8,128)(2,1)S(1)}, u32[]{:S(2)}, u32[]{:S(2)}) collective-permute-start(bf16[4,2,128,128]{3,2,1,0:T(8,128)(2,1)S(1)} %get-tuple-element.76.refs_6_), channel_id=1, source_target_pairs={{0,4},{2,6},{4,0},{6,2},{8,12},{10,14},{12,8},{14,10},{16,20},{18,... | collective-permute-start | bytes 786440 | tf_op jit(solution)/shard_map/ppermute | solution.py:314
  36.6 7.2 %collective-permute-start.16 = (bf16[512,128]{1,0:T(8,128)(2,1)S(1)}, bf16[512,128]{1,0:T(8,128)(2,1)S(1)}, u32[]{:S(2)}, u32[]{:S(2)}) collective-permute-start(bf16[512,128]{1,0:T(8,128)(2,1)S(1)} %finish.2.refs_0_), channel_id=1, source_target_pairs={{0,2},{2,0},{4,6},{6,4},{8,10},{10,8},{12,14},{14,12},{16,18},{18,... | collective-permute-start | bytes 393224 | tf_op jit(solution)/shard_map/ppermute | solution.py:314
  36.8 10.0 %collective-permute-start.18 = (bf16[512,128]{1,0:T(8,128)(2,1)S(1)}, bf16[512,128]{1,0:T(8,128)(2,1)S(1)}, u32[]{:S(2)}, u32[]{:S(2)}) collective-permute-start(bf16[512,128]{1,0:T(8,128)(2,1)S(1)} %finish.2.refs_0_), channel_id=1, source_target_pairs={{0,8},{2,10},{4,12},{6,14},{8,0},{10,2},{12,4},{14,6},{16,24},{18,... | collective-permute-start | bytes 393224 | tf_op jit(solution)/shard_map/ppermute | solution.py:314
  37.8 10.9 %collective-permute-start.13 = (bf16[512,128]{1,0:T(8,128)(2,1)S(1)}, bf16[512,128]{1,0:T(8,128)(2,1)S(1)}, u32[]{:S(2)}, u32[]{:S(2)}) collective-permute-start(bf16[512,128]{1,0:T(8,128)(2,1)S(1)} %finish.2.refs_0_), channel_id=1, source_target_pairs={{0,10},{2,8},{4,14},{6,12},{8,2},{10,0},{12,6},{14,4},{16,26},{18,... | collective-permute-start | bytes 393224 | tf_op jit(solution)/shard_map/ppermute | solution.py:314
  43.8 5.4 %collective-permute-start.17 = (bf16[2,2,128,128]{3,2,1,0:T(8,128)(2,1)S(1)}, bf16[2,2,128,128]{3,2,1,0:T(8,128)(2,1)S(1)}, u32[]{:S(2)}, u32[]{:S(2)}) collective-permute-start(bf16[2,2,128,128]{3,2,1,0:T(8,128)(2,1)S(1)} %get-tuple-element.89.refs_8_), channel_id=1, source_target_pairs={{0,4},{2,6},{4,0},{6,2},{8,12},{10,14},{12,8},{14,10},{16,20},{18,... | collective-permute-start | bytes 393224 | tf_op jit(solution)/shard_map/ppermute | solution.py:314
  49.6 2.7 %collective-permute-start.19 = (bf16[512,1024]{1,0:T(8,128)(2,1)S(1)}, bf16[512,1024]{1,0:T(8,128)(2,1)S(1)}, u32[]{:S(2)}, u32[]{:S(2)}) collective-permute-start(bf16[512,1024]{1,0:T(8,128)(2,1)S(1)} %term.3.refs_0_), channel_id=1, source_target_pairs={{0,1},{1,0},{2,3},{3,2},{4,5},{5,4},{6,7},{7,6},{8,9},{9,8},{10,11... | collective-permute-start | bytes 3145736 | tf_op jit(solution)/shard_map/ppermute | solution.py:336
  49.7 5.9 %collective-permute-start.20 = (bf16[2,2,128,128]{3,2,1,0:T(8,128)(2,1)S(1)}, bf16[2,2,128,128]{3,2,1,0:T(8,128)(2,1)S(1)}, u32[]{:S(2)}, u32[]{:S(2)}) collective-permute-start(bf16[2,2,128,128]{3,2,1,0:T(8,128)(2,1)S(1)} %get-tuple-element.90.refs_9_), channel_id=1, source_target_pairs={{0,4},{2,6},{4,0},{6,2},{8,12},{10,14},{12,8},{14,10},{16,20},{18,... | collective-permute-start | bytes 393224 | tf_op jit(solution)/shard_map/ppermute | solution.py:314
  56.8 4.0 %collective-permute-start.21 = (bf16[128,128]{1,0:T(8,128)(2,1)S(1)}, bf16[128,128]{1,0:T(8,128)(2,1)S(1)}, u32[]{:S(2)}, u32[]{:S(2)}) collective-permute-start(bf16[128,128]{1,0:T(8,128)(2,1)S(1)} %get-tuple-element.96), channel_id=1, source_target_pairs={{0,2},{2,0},{4,6},{6,4},{8,10},{10,8},{12,14},{14,12},{16,18},{18,... | collective-permute-start | bytes 98312 | tf_op jit(solution)/shard_map/ppermute | solution.py:314
  58.5 3.9 %collective-permute-start.22 = (bf16[128,128]{1,0:T(8,128)(2,1)S(1)}, bf16[128,128]{1,0:T(8,128)(2,1)S(1)}, u32[]{:S(2)}, u32[]{:S(2)}) collective-permute-start(bf16[128,128]{1,0:T(8,128)(2,1)S(1)} %get-tuple-element.97), channel_id=1, source_target_pairs={{0,8},{2,10},{4,12},{6,14},{8,0},{10,2},{12,4},{14,6},{16,24},{18,... | collective-permute-start | bytes 98312 | tf_op jit(solution)/shard_map/ppermute | solution.py:314
  58.5 4.8 %collective-permute-start.23 = (bf16[128,128]{1,0:T(8,128)(2,1)S(1)}, bf16[128,128]{1,0:T(8,128)(2,1)S(1)}, u32[]{:S(2)}, u32[]{:S(2)}) collective-permute-start(bf16[128,128]{1,0:T(8,128)(2,1)S(1)} %get-tuple-element.98), channel_id=1, source_target_pairs={{0,10},{2,8},{4,14},{6,12},{8,2},{10,0},{12,6},{14,4},{16,26},{18,... | collective-permute-start | bytes 98312 | tf_op jit(solution)/shard_map/ppermute | solution.py:314
  63.6 1.4 %collective-permute-start.24 = (bf16[64,1024]{1,0:T(8,128)(2,1)S(1)}, bf16[64,1024]{1,0:T(8,128)(2,1)S(1)}, u32[]{:S(2)}, u32[]{:S(2)}) collective-permute-start(bf16[64,1024]{1,0:T(8,128)(2,1)S(1)} %get-tuple-element.100), channel_id=1, source_target_pairs={{0,1},{1,0},{2,3},{3,2},{4,5},{5,4},{6,7},{7,6},{8,9},{9,8},{10,11... | collective-permute-start | bytes 393224 | tf_op jit(solution)/shard_map/ppermute | solution.py:336
  (8 other events, 105.9 us)
